TPU v7x, 256 devices: a whole 4x4x8 slice. The times are simulated.
256 devices in a mesh: shot: 8 (over z_lo, core), rcv: 32 (over y, z_hi, x).
Axes of the slice: x: 4, y: 4, z: 8 (z_hi: 2, z_lo: 4; z = z_hi * 4 + z_lo), core: 2. Of those that a mesh axis runs over, the one named last changes fastest.
Arguments:
- reflection: bfloat16 [512, 512, 256], P('shot', 'rcv'), may hold values from -6 to 6
- focus_index: int32 [2], replicated, may hold values from 0 to 511
- shot_window: int32 [2, 512, 2], P(None, 'shot'), may hold values from 0 to 256, as said below
- rcv_window: int32 [2, 512, 2], P(None, 'rcv'), may hold values from 0 to 256, as said below
Outputs:
- focus_down: float32 [512, 2, 256], P('rcv', None, 'shot')
- focus_up: float32 [512, 2, 256], P(('shot', 'rcv'))
Inputs may be any that keep to these rules, and one draw needn't show every extreme that they name: `shot_window`: onset (index 0) is below end (index 1) for every shot and focal point. `rcv_window`: onset (index 0) is below end (index 1) for every receiver and focal point.
All inputs are finite; a program needn't handle non-finite values.
Results may differ from a plain program's by a relative error of at most 0.0022.
Values may be sent and summed in bfloat16 or wider, within the bound.
No kernel may reach another device: no remote copies, remote signals or barrier semaphores. Data moves between devices by JAX's collectives and lax.ppermute only.
A program may use at most 192 MiB of HBM per device.

v0:
```python
import math

import jax
import jax.numpy as jnp
from jax import lax
from jax.sharding import PartitionSpec as P

ITERS = 2


def window_mask(window, lag_total):
    lag_axis = jnp.arange(lag_total, dtype=jnp.int32)
    return (lag_axis >= window[0][:, :, None]) & (lag_axis < window[1][:, :, None])


def lower_toeplitz(field):
    width, foci, lag_total = field.shape
    padded = jnp.concatenate([field, jnp.zeros_like(field)], axis=2)
    tiled = jnp.tile(padded, (1, 1, lag_total))[:, :, : lag_total * (2 * lag_total - 1)]
    skewed = tiled.reshape(width, foci, lag_total, 2 * lag_total - 1)[:, :, :, :lag_total]
    return jnp.transpose(skewed, (0, 2, 1, 3)).reshape(width * lag_total, foci * lag_total)


def upper_toeplitz(upgoing):
    count, foci, lag_total = upgoing.shape
    padded = jnp.concatenate([upgoing, jnp.zeros_like(upgoing)], axis=2)
    tiled = jnp.tile(padded, (1, 1, lag_total + 1))[:, :, : lag_total * (2 * lag_total + 1)]
    skewed = tiled.reshape(count, foci, lag_total, 2 * lag_total + 1)[:, :, :, :lag_total]
    return jnp.transpose(skewed, (0, 2, 1, 3)).reshape(count, lag_total, foci * lag_total)


def convolve(kernel, field):
    count, width, lag_total = kernel.shape
    foci = field.shape[1]
    block = math.gcd(width, 32)

    def convolve_add_block(block_id, total):
        slab = kernel.reshape(count, block * lag_total)
        product = jnp.dot(slab, lower_toeplitz(field), preferred_element_type=jnp.float32)
        return total + product.reshape(count, foci, lag_total)

    return lax.fori_loop(
        0, width // block, convolve_add_block, jnp.zeros((count, foci, lag_total), jnp.float32)
    )


def correlate(kernel, upgoing):
    count, width, lag_total = kernel.shape
    foci = upgoing.shape[1]
    block = math.gcd(count, 32)

    def correlate_add_block(block_id, total):
        start = block_id * block
        piece = lax.dynamic_slice_in_dim(upgoing, start, block, 0)
        slab = lax.dynamic_slice_in_dim(kernel, start, block, 0)
        product = lax.dot_general(
            slab,
            upper_toeplitz(piece),
            (((0, 2), (0, 1)), ((), ())),
            preferred_element_type=jnp.float32,
        )
        return total + product.reshape(width, foci, lag_total)

    return lax.fori_loop(
        0, count // block, correlate_add_block, jnp.zeros((width, foci, lag_total), jnp.float32)
    )


def initial_field(reflection, focus_index):
    shots_here = reflection.shape[0]
    local_rows = focus_index - lax.axis_index("shot") * shots_here
    picked = []
    for which in range(focus_index.shape[0]):
        inside = (local_rows[which] >= 0) & (local_rows[which] < shots_here)
        trace = lax.dynamic_index_in_dim(
            reflection, jnp.clip(local_rows[which], 0, shots_here - 1), 0, keepdims=False
        )
        picked.append(jnp.where(inside, trace.astype(jnp.float32), 0.0))
    stacked = jnp.flip(jnp.stack(picked, axis=1), axis=2)
    return lax.psum(stacked.astype(jnp.bfloat16), "shot")


def on_device(reflection, focus_index, shot_window, rcv_window):
    shots_here, receivers_here, lag_total = reflection.shape
    rcv_count = lax.axis_size("rcv")
    shot_count = lax.axis_size("shot")
    conv_scale = 1.0 / math.sqrt(receivers_here * rcv_count * lag_total)
    corr_scale = 1.0 / math.sqrt(shots_here * shot_count * lag_total)
    share_rows = shots_here // rcv_count
    share_lags = lag_total // shot_count
    rcv_place = lax.axis_index("rcv")
    shot_place = lax.axis_index("shot")
    shot_mask = window_mask(shot_window, lag_total)
    rcv_mask = window_mask(rcv_window, lag_total)
    start_field = initial_field(reflection, focus_index)
    field = start_field
    focus_down = None
    focus_up = None
    for iteration in range(ITERS):
        convolved = lax.psum_scatter(
            convolve(reflection, field) * conv_scale, "rcv", scatter_dimension=0, tiled=True
        )
        mask_share = lax.dynamic_slice_in_dim(shot_mask, rcv_place * share_rows, share_rows, 0)
        up_exact = jnp.where(mask_share, convolved, 0.0)
        upgoing = up_exact.astype(jnp.bfloat16)
        correlated = (
            correlate(reflection, lax.all_gather(upgoing, "rcv", axis=0, tiled=True)) * corr_scale
        )
        focus_up = up_exact
        corr_share = lax.psum_scatter(correlated, "shot", scatter_dimension=2, tiled=True)
        lag_start = shot_place * share_lags
        mask_share = lax.dynamic_slice_in_dim(rcv_mask, lag_start, share_lags, 2)
        start_share = lax.dynamic_slice_in_dim(start_field, lag_start, share_lags, 2)
        down_share = start_share.astype(jnp.float32) + jnp.where(mask_share, corr_share, 0.0)
        focus_down = down_share
        if iteration + 1 < ITERS:
            field = lax.all_gather(down_share.astype(jnp.bfloat16), "shot", axis=2, tiled=True)
    return (focus_down, focus_up)


def solution(mesh):
    return jax.shard_map(
        on_device,
        mesh=mesh,
        in_specs=(P("shot", "rcv", None), P(), P(None, "shot", None), P(None, "rcv", None)),
        out_specs=(P("rcv", None, "shot"), P(("shot", "rcv"), None, None)),
        check_vma=False,
    )
```

profile of v0, /device:TPU:1, one launch (start us, length us, event | category | flops | bytes accessed | tf_op | source)
XLA Modules:
  0.0 1429.6 jit_solution(6219653414078913337)
XLA Ops:
  7.2 0.7 broadcast_subtract_fusion
  7.9 0.6 fusion.19
  12.4 0.7 constant_dynamic-slice_fusion.5
  13.2 0.3 rev.4
  13.5 27.3 %psum.7 = bf16[16,2,256]{2,1,0:T(2,128)(2,1)S(1)} all-reduce(bf16[16,2,256]{2,1,0:T(2,128)(2,1)S(1)} %rev.4), channel_id=1, replica_groups=mesh['shot'=8,'rcv'=32] {'shot'}, use_global_device_ids=true, to_apply=%region_0.1 | all-reduce | flops 8192 | bytes 32768 | tf_op jit(solution)/shard_map/psum | solution.py:80
  40.8 3.9 tile.70
  44.7 8.9 tile.71
  53.6 7.1 slice.84
  60.7 19.5 %reshape.146 = bf16[16,2,256,511]{3,2,0,1:T(8,128)(2,1)} reshape(bf16[16,2,130816]{2,0,1:T(8,128)(2,1)} %slice.84) | data formatting | bytes 16744448 | tf_op jit(solution)/shard_map/while/body/eval_jaxpr/reshape | solution.py:20
  80.3 4.6 slice_bitcast_fusion.13
  84.9 7.9 copy.47
  92.8 4.4 copy.71
  97.2 0.2 copy.72
  97.4 0.8 copy-done.1
  98.2 1.4 fusion.13
  99.7 196.1 %all-reduce.10 = bf16[64,2,256]{2,1,0:T(2,128)(2,1)S(1)} all-reduce(f32[64,2,256]{2,1,0:T(2,128)S(1)} %mul.54), channel_id=2, replica_groups=mesh['shot'=8,'rcv'=32] {'rcv'}, use_global_device_ids=true, to_apply=%region_1.2.clone | all-reduce | flops 32768 | bytes 196608
  296.0 0.6 dynamic-slice
  297.3 93.5 %all_gather.9 = bf16[64,2,256]{2,1,0:T(2,128)(2,1)S(1)} all-gather(bf16[2,2,256]{2,1,0:T(2,128)(2,1)S(1)} %fusion.17), channel_id=1, replica_groups=mesh['shot'=8,'rcv'=32] {'rcv'}, dimensions={0}, use_global_device_ids=true | all-gather | bytes 67584 | tf_op jit(solution)/shard_map/all_gather | solution.py:107
  390.9 171.1 %while.36 = (s32[]{:T(128)}, f32[16,2,256]{2,0,1:T(8,128)S(1)}, bf16[64,16,256]{2,1,0:T(8,128)(2,1)S(1)}, bf16[64,2,256]{2,1,0:T(2,128)(2,1)S(1)}, s32[]{:T(128)...) while((s32[]{:T(128)}, f32[16,2,256]{2,0,1:T(8,128)S(1)}, ...), condition=%wide.region_3.4_spmd.clone, body=%wide.region_2.3_spmd.clone.sunk | while | flops 134234112 | bytes 126779552 | solution.py:64
  391.0 6.1 tile.82
  397.1 17.2 %tile.83 = bf16[32,2,131584]{2,0,1:T(8,128)(2,1)} reshape(bf16[32,2,257,512]{3,2,0,1:T(8,128)(2,1)} %tile.82) | data formatting | bytes 33685504 | tf_op jit(solution)/shard_map/while/body/eval_jaxpr/tile | solution.py:27
  414.2 13.7 slice.113
  428.0 43.9 %reshape.167 = bf16[32,2,256,513]{3,2,0,1:T(8,128)(2,1)} reshape(bf16[32,2,131328]{2,0,1:T(8,128)(2,1)} %slice.113) | data formatting | bytes 33619968 | tf_op jit(solution)/shard_map/while/body/eval_jaxpr/reshape | solution.py:28
  471.9 4.6 fusion.29
  476.5 6.1 tile.82
  482.6 17.2 %tile.83 = bf16[32,2,131584]{2,0,1:T(8,128)(2,1)} reshape(bf16[32,2,257,512]{3,2,0,1:T(8,128)(2,1)} %tile.82) | data formatting | bytes 33685504 | tf_op jit(solution)/shard_map/while/body/eval_jaxpr/tile | solution.py:27
  499.8 13.7 slice.113
  513.5 43.9 %reshape.167 = bf16[32,2,256,513]{3,2,0,1:T(8,128)(2,1)} reshape(bf16[32,2,131328]{2,0,1:T(8,128)(2,1)} %slice.113) | data formatting | bytes 33619968 | tf_op jit(solution)/shard_map/while/body/eval_jaxpr/reshape | solution.py:28
  557.4 4.6 fusion.29
  562.0 1.2 copy.61
  563.2 1.6 reshape.159
  565.1 69.5 %reduce-scatter.7.cloned.1.call-done = f32[32,32]{1,0:T(8,128)} async-done(((f32[256,32]{1,0:T(8,128)}), f32[32,32]{1,0:T(8,128)}) %reduce-scatter.7.cloned.1.call-update) | async-done | bytes 4112
  634.7 0.9 reshape.160
  635.5 0.2 copy.62
  635.9 17.8 %all_gather.10 = bf16[16,2,256]{0,1,2:T(2,128)(2,1)S(1)} all-gather(bf16[16,2,32]{0,1,2:T(2,128)(2,1)S(1)} %copy.50), channel_id=1, replica_groups=mesh['shot'=8,'rcv'=32] {'shot'}, dimensions={2}, use_global_device_ids=true | all-gather | bytes 18432 | tf_op jit(solution)/shard_map/all_gather | solution.py:117
  653.8 3.9 tile.72
  657.7 8.9 tile.73
  666.6 7.1 slice.86
  673.8 19.5 %reshape.149 = bf16[16,2,256,511]{3,2,0,1:T(8,128)(2,1)} reshape(bf16[16,2,130816]{2,0,1:T(8,128)(2,1)} %slice.86) | data formatting | bytes 16744448 | tf_op jit(solution)/shard_map/while/body/eval_jaxpr/reshape | solution.py:20
  693.3 4.6 slice_bitcast_fusion.12
  697.9 7.9 copy.52
  705.8 4.4 copy.73
  710.2 1.4 fusion.12
  711.6 0.8 mul.58
  712.5 380.6 %all-reduce.9.cloned.1.call-done = f32[64,2,256]{2,1,0:T(2,128)} async-done(((f32[64,2,256]{2,1,0:T(2,128)}), f32[64,2,256]{2,1,0:T(2,128)}) %all-reduce.9.cloned.1.call-update) | async-done | bytes 131088
  1093.1 1.3 fusion.18
  1094.4 100.6 %all_gather.11 = bf16[64,2,256]{2,1,0:T(2,128)(2,1)S(1)} all-gather(bf16[2,2,256]{2,1,0:T(2,128)(2,1)S(1)} %get-tuple-element.248), channel_id=1, replica_groups=mesh['shot'=8,'rcv'=32] {'rcv'}, dimensions={0}, use_global_device_ids=true | all-gather | bytes 67584 | tf_op jit(solution)/shard_map/all_gather | solution.py:107
  1195.0 171.1 %while.37 = (s32[]{:T(128)}, f32[16,2,256]{2,0,1:T(8,128)S(1)}, bf16[64,16,256]{2,1,0:T(8,128)(2,1)S(1)}, bf16[64,2,256]{2,1,0:T(2,128)(2,1)S(1)}, s32[]{:T(128)...) while((s32[]{:T(128)}, f32[16,2,256]{2,0,1:T(8,128)S(1)}, ...), condition=%wide.region_7.8_spmd.clone, body=%wide.region_6.7_spmd.clone.sunk | while | flops 134234112 | bytes 126779552 | solution.py:64
  1195.1 6.1 tile.84
  1201.2 17.2 %tile.85 = bf16[32,2,131584]{2,0,1:T(8,128)(2,1)} reshape(bf16[32,2,257,512]{3,2,0,1:T(8,128)(2,1)} %tile.84) | data formatting | bytes 33685504 | tf_op jit(solution)/shard_map/while/body/eval_jaxpr/tile | solution.py:27
  1218.3 13.7 slice.115
  1232.1 43.9 %reshape.168 = bf16[32,2,256,513]{3,2,0,1:T(8,128)(2,1)} reshape(bf16[32,2,131328]{2,0,1:T(8,128)(2,1)} %slice.115) | data formatting | bytes 33619968 | tf_op jit(solution)/shard_map/while/body/eval_jaxpr/reshape | solution.py:28
  1276.0 4.6 fusion.31
  1280.6 6.1 tile.84
  1286.7 17.2 %tile.85 = bf16[32,2,131584]{2,0,1:T(8,128)(2,1)} reshape(bf16[32,2,257,512]{3,2,0,1:T(8,128)(2,1)} %tile.84) | data formatting | bytes 33685504 | tf_op jit(solution)/shard_map/while/body/eval_jaxpr/tile | solution.py:27
  1303.9 13.7 slice.115
  1317.6 43.9 %reshape.168 = bf16[32,2,256,513]{3,2,0,1:T(8,128)(2,1)} reshape(bf16[32,2,131328]{2,0,1:T(8,128)(2,1)} %slice.115) | data formatting | bytes 33619968 | tf_op jit(solution)/shard_map/while/body/eval_jaxpr/reshape | solution.py:28
  1361.5 4.6 fusion.31
  1366.1 1.2 copy.63
  1367.4 1.6 reshape.161
  1369.0 51.8 %reduce-scatter.9.cloned.1.call-done = f32[32,32]{1,0:T(8,128)} async-done(((f32[256,32]{1,0:T(8,128)}), f32[32,32]{1,0:T(8,128)}) %reduce-scatter.9.cloned.1.call-update) | async-done | bytes 4112
  1420.8 0.9 reshape.162
  1421.7 0.2 copy.64
  1421.9 0.7 convert_add_fusion
  (72 shorter events, 1.3 us)
Async XLA Ops:
  7.2 627.5 %reduce-scatter.7.cloned.1.call-start = ((), (), s32[]{:S(2)}) async-start(), calls=%async_computation.2 | async-start | bytes 147456
  40.8 12.8 copy-start.3
  84.9 12.4 copy-start
  92.8 203.0 %copy-start.14 = (s32[2,64,2]{1,2,0:T(2,128)S(1)}, s32[2,64,2]{1,2,0:T(2,128)}, u32[]{:S(2)}) copy-start(s32[2,64,2]{1,2,0:T(2,128)} %param.10) | copy-start | bytes 3076
  92.8 203.2 %copy-start.16 = (u32[256]{0:T(256)S(1)}, u32[256]{0:T(256)}, u32[]{:S(2)}) copy-start(u32[256]{0:T(256)} %constant.137) | copy-start | bytes 3076
  97.4 0.8 copy-start.1
  297.2 93.6 %copy-start.10 = (s32[2,2]{1,0:T(2,128)}, s32[2,2]{1,0:T(2,128)S(1)}, u32[]{:S(2)}) copy-start(s32[2,2]{1,0:T(2,128)S(1)} %get-tuple-element.260) | copy-start | bytes 52
  297.2 93.6 %copy-start.12 = (s32[2,2]{1,0:T(2,128)}, s32[2,2]{1,0:T(2,128)S(1)}, u32[]{:S(2)}) copy-start(s32[2,2]{1,0:T(2,128)S(1)} %get-tuple-element.261) | copy-start | bytes 52
  390.9 174.1 %copy-start.15 = (s32[2,16,2]{1,2,0:T(2,128)S(1)}, s32[2,16,2]{1,2,0:T(2,128)}, u32[]{:S(2)}) copy-start(s32[2,16,2]{1,2,0:T(2,128)} %param.11) | copy-start | bytes 772
  390.9 244.9 %copy-start.4 = (bf16[16,2,256]{2,1,0:T(2,128)(2,1)S(1)}, bf16[16,2,256]{2,1,0:T(2,128)(2,1)}, u32[]{:S(2)}) copy-start(bf16[16,2,256]{2,1,0:T(2,128)(2,1)} %copy-done.3) | copy-start | bytes 49156
  564.9 528.2 %all-reduce.9.cloned.1.call-start = ((), (), s32[]{:S(2)}) async-start(), calls=%async_computation.4 | async-start | bytes 262144
  565.0 101.6 %copy-start.6 = (s32[16,2]{1,0:T(8,128)}, s32[16,2]{1,0:T(8,128)S(1)}, u32[]{:S(2)}) copy-start(s32[16,2]{1,0:T(8,128)S(1)} %copy.42) | copy-start | bytes 388
  565.1 101.5 %copy-start.8 = (s32[16,2]{1,0:T(8,128)}, s32[16,2]{1,0:T(8,128)S(1)}, u32[]{:S(2)}) copy-start(s32[16,2]{1,0:T(8,128)S(1)} %copy.43) | copy-start | bytes 388
  697.9 12.4 copy-start.2
  705.8 387.2 %copy-start.11 = (s32[2,2]{1,0:T(2,128)S(1)}, s32[2,2]{1,0:T(2,128)}, u32[]{:S(2)}) copy-start(s32[2,2]{1,0:T(2,128)} %copy-done.10) | copy-start | bytes 52
  705.8 387.2 %copy-start.13 = (s32[2,2]{1,0:T(2,128)S(1)}, s32[2,2]{1,0:T(2,128)}, u32[]{:S(2)}) copy-start(s32[2,2]{1,0:T(2,128)} %copy-done.12) | copy-start | bytes 52
  712.4 708.4 %reduce-scatter.9.cloned.1.call-start = ((), (), s32[]{:S(2)}) async-start(), calls=%async_computation.3 | async-start | bytes 147456
  1195.0 226.9 %copy-start.5 = (bf16[16,2,256]{2,1,0:T(2,128)(2,1)S(1)}, bf16[16,2,256]{2,1,0:T(2,128)(2,1)}, u32[]{:S(2)}) copy-start(bf16[16,2,256]{2,1,0:T(2,128)(2,1)} %copy-done.3) | copy-start | bytes 49156
  1195.0 226.9 %copy-start.7 = (s32[16,2]{1,0:T(8,128)S(1)}, s32[16,2]{1,0:T(8,128)}, u32[]{:S(2)}) copy-start(s32[16,2]{1,0:T(8,128)} %copy-done.6) | copy-start | bytes 388
  1195.0 226.9 %copy-start.9 = (s32[16,2]{1,0:T(8,128)S(1)}, s32[16,2]{1,0:T(8,128)}, u32[]{:S(2)}) copy-start(s32[16,2]{1,0:T(8,128)} %copy-done.8) | copy-start | bytes 388
Sparse Core Ops, SparseCore 0:
  565.0 69.6 reduce-scatter.6
  712.5 380.4 all-reduce.8
  1369.1 51.6 reduce-scatter.8
where the time goes:
time: 1440 us; the launch traced here: 1430 us
  waiting for transfers between devices  502 us (35%)
  local copies, waits for them, and re-layouts  449 us (31%)
  blocking collectives  435 us (30%)
  matrix products  21.1 us (1%)
  between operations  19 us (1%)
    unnamed x6, waiting for transfers between devices  502 us
    unnamed x1, blocking collectives  196 us
    all_gather x2, blocking collectives, on_device(): lax.all_gather(upgoing, 'rcv', axis=0, tiled=True)  194 us
    reshape x4, local copies, waits for them, and re-layouts, upper_toeplitz(): tiled.reshape(count, foci, lag_total, 2 * lag_total + 1)  176 us
    another operation x8, local copies, waits for them, and re-layouts, upper_toeplitz(): jnp.tile(padded, (1, 1, lag_total + 1))  93.1 us
    slice x4, local copies, waits for them, and re-layouts, upper_toeplitz(): jnp.tile(padded, (1, 1, lag_total + 1))  55 us
    reshape x2, local copies, waits for them, and re-layouts, lower_toeplitz(): tiled.reshape(width, foci, lag_total, 2 * lag_total - 1)  39 us
  transfers between devices with their start and end apart: 3, of which 3 were waited for; matrix products, arithmetic and copies ran while one was open for 0% of the time, Pallas kernels for 0%

commit v1 on v0

v1 whole, which is shorter than its diff:
```python
import functools
import math

import jax
import jax.numpy as jnp
import ml_dtypes
import numpy as np
from jax import lax
from jax.experimental import pallas as pl
from jax.experimental.pallas import tpu as pltpu
from jax.sharding import PartitionSpec as P


ITERS = 2
LAGS = 256
LANES = 128
FOCI = 2
SHOTS_HERE = 64
RCV_HERE = 16
RCV_AXIS = 32
SHOT_AXIS = 8
SHARE = SHOTS_HERE * FOCI * 2 // 16
HALVES = LAGS // LANES
F32 = jnp.float32
BF16 = jnp.bfloat16


def split_bf16(matrix):
    high = matrix.astype(ml_dtypes.bfloat16)
    low = (matrix - high.astype(np.float64)).astype(ml_dtypes.bfloat16)
    return high, low


def tables():
    times = np.arange(LAGS)[:, None]
    angles = (np.arange(LAGS)[None, :] + 0.5) * (np.pi / LAGS) * times
    forward = np.concatenate([np.cos(angles), -np.sin(angles)], axis=1)
    fwd_high, fwd_low = split_bf16(forward)
    inv_high, inv_low = split_bf16(np.ascontiguousarray(forward.T))
    flip = np.ascontiguousarray(np.eye(LAGS)[::-1]).astype(ml_dtypes.bfloat16)
    return fwd_high, fwd_low, inv_high, inv_low, flip


def dot(left, right):
    return jnp.dot(left, right, preferred_element_type=F32)


def to_spectrum(traces, high, low):
    return dot(traces, high[...]) + dot(traces, low[...])


def to_traces(spectrum, high, low, scale):
    top = spectrum.astype(BF16)
    rest = (spectrum - top.astype(F32)).astype(BF16)
    return (dot(top, high[...]) + (dot(top, low[...]) + dot(rest, high[...]))) * scale


def pick_kernel(focus, reflection, flip, out):
    first = lax.axis_index("shot") * SHOTS_HERE
    picked = []
    for which in range(FOCI):
        row = focus[which] - first
        inside = jnp.logical_and(row >= 0, row < SHOTS_HERE)
        trace = reflection[jnp.clip(row, 0, SHOTS_HERE - 1)].astype(F32)
        picked.append(jnp.where(inside, trace, 0.0).astype(BF16))
    flipped = dot(jnp.concatenate(picked, axis=0), flip[...]).astype(BF16)
    for place in range(SHOT_AXIS):
        out[place] = flipped


def shot_slot(shot):
    y, z, x, j = shot // 16, (shot // 8) % 2, (shot // 2) % 4, shot % 2
    return y * 16 + x * 4 + z * 2 + j


def reflection_kernel(reflection, high, low, out):
    step = 16
    for begin in range(0, SHOTS_HERE, step):
        rows = reflection[begin : begin + step].reshape(step * RCV_HERE, LAGS)
        spectrum = to_spectrum(rows, high, low)
        for local in range(step):
            piece = spectrum[local * RCV_HERE : (local + 1) * RCV_HERE]
            slot = shot_slot(begin + local)
            for chunk in range(4):
                out[chunk, pl.ds(slot, RCV_HERE, SHOTS_HERE), :] = piece[
                    :, chunk * LANES : (chunk + 1) * LANES
                ]


def convolve_in(field, refl, fwd_high, fwd_low, inv_high, inv_low, out, spectrum, product, rows):
    spectrum[...] = to_spectrum(field, fwd_high, fwd_low)
    for chunk in range(2):
        re_lanes = slice(chunk * LANES, (chunk + 1) * LANES)
        im_lanes = slice(LAGS + chunk * LANES, LAGS + (chunk + 1) * LANES)
        totals = [jnp.zeros((SHOTS_HERE, LANES), F32) for _ in range(2 * FOCI)]
        for r in range(RCV_HERE):
            re = refl[chunk, r * SHOTS_HERE : (r + 1) * SHOTS_HERE, :]
            im = refl[2 + chunk, r * SHOTS_HERE : (r + 1) * SHOTS_HERE, :]
            for q in range(FOCI):
                line = q * RCV_HERE + r
                f_re = spectrum[line : line + 1, re_lanes]
                f_im = spectrum[line : line + 1, im_lanes]
                totals[2 * q] += re * f_re - im * f_im
                totals[2 * q + 1] += re * f_im + im * f_re
        for q in range(FOCI):
            product[q * SHOTS_HERE : (q + 1) * SHOTS_HERE, re_lanes] = totals[2 * q]
            product[q * SHOTS_HERE : (q + 1) * SHOTS_HERE, im_lanes] = totals[2 * q + 1]
    scale = 1.0 / (LAGS * math.sqrt(RCV_HERE * RCV_AXIS * LAGS))
    result = to_traces(product[...], inv_high, inv_low, scale)
    for q in range(FOCI):
        for h in range(HALVES):
            rows[pl.ds(h * FOCI + q, SHOTS_HERE, 2 * FOCI), :] = result[
                q * SHOTS_HERE : (q + 1) * SHOTS_HERE, h * LANES : (h + 1) * LANES
            ]
    for place in range(RCV_AXIS):
        group = (place // 8) * 4 + place % 4
        out[place] = rows[group * SHARE : (group + 1) * SHARE, :]


def first_kernel(picked, refl, fwd_high, fwd_low, inv_high, inv_low, start_out, out, spectrum, product, rows):
    start = picked[0].astype(F32)
    for place in range(1, SHOT_AXIS):
        start = start + picked[place].astype(F32)
    start = start.astype(BF16)
    start_out[...] = start
    convolve_in(start, refl, fwd_high, fwd_low, inv_high, inv_low, out, spectrum, product, rows)


def upgoing_kernel(window, parts, up_out, out):
    total = parts[0]
    for place in range(1, RCV_AXIS):
        total = total + parts[place]
    me = lax.axis_index("rcv")
    corner = (me // 8) * 16 + (me % 4) * 2
    row = lax.broadcasted_iota(jnp.int32, (SHARE, LANES), 0)
    onset = jnp.zeros((SHARE, LANES), jnp.int32)
    ending = jnp.zeros((SHARE, LANES), jnp.int32)
    for z in range(2):
        for j in range(2):
            for q in range(FOCI):
                shot = corner + z * 8 + j
                mine = jnp.logical_and(row // 4 == z * 2 + j, row % 2 == q)
                onset = jnp.where(mine, window[0, q, shot], onset)
                ending = jnp.where(mine, window[1, q, shot], ending)
    time = lax.broadcasted_iota(jnp.int32, (SHARE, LANES), 1) + ((row // 2) % 2) * LANES
    up = jnp.where(jnp.logical_and(time >= onset, time < ending), total, 0.0)
    own = jnp.where((me // 4) % 2 == 0, up[:8], up[8:])
    for j in range(2):
        for q in range(FOCI):
            for h in range(HALVES):
                line = j * 4 + h * 2 + q
                up_out[j, q : q + 1, h * LANES : (h + 1) * LANES] = own[line : line + 1]
    rounded = up.astype(BF16)
    for place in range(out.shape[0]):
        out[place] = rounded


def correlate_kernel(upgoing, refl, fwd_high, fwd_low, inv_high, inv_low, out, rows, spectrum, product):
    for place in range(16):
        rows[place * SHARE : (place + 1) * SHARE, :] = upgoing[place].astype(F32)
    traces = jnp.concatenate(
        [
            jnp.concatenate(
                [rows[pl.ds(h * FOCI + q, SHOTS_HERE, 2 * FOCI), :] for h in range(HALVES)], axis=1
            )
            for q in range(FOCI)
        ],
        axis=0,
    ).astype(BF16)
    spectrum[...] = to_spectrum(traces, fwd_high, fwd_low)
    for chunk in range(2):
        re_lanes = slice(chunk * LANES, (chunk + 1) * LANES)
        im_lanes = slice(LAGS + chunk * LANES, LAGS + (chunk + 1) * LANES)
        for r in range(RCV_HERE):
            totals = [jnp.zeros((8, LANES), F32) for _ in range(2 * FOCI)]
            for begin in range(0, SHOTS_HERE, 8):
                re = refl[chunk, r * SHOTS_HERE + begin : r * SHOTS_HERE + begin + 8, :]
                im = refl[2 + chunk, r * SHOTS_HERE + begin : r * SHOTS_HERE + begin + 8, :]
                for q in range(FOCI):
                    lines = slice(q * SHOTS_HERE + begin, q * SHOTS_HERE + begin + 8)
                    u_re = spectrum[lines, re_lanes]
                    u_im = spectrum[lines, im_lanes]
                    totals[2 * q] += re * u_re + im * u_im
                    totals[2 * q + 1] += re * u_im - im * u_re
            for q in range(FOCI):
                line = q * RCV_HERE + r
                product[line : line + 1, re_lanes] = jnp.sum(totals[2 * q], axis=0, keepdims=True)
                product[line : line + 1, im_lanes] = jnp.sum(totals[2 * q + 1], axis=0, keepdims=True)
    scale = 1.0 / (LAGS * math.sqrt(SHOTS_HERE * SHOT_AXIS * LAGS))
    result = to_traces(product[...], inv_high, inv_low, scale)
    for place in range(SHOT_AXIS):
        out[place] = result


def add_down(window, parts, start, onset, ending):
    total = parts[0]
    for place in range(1, SHOT_AXIS):
        total = total + parts[place]
    for q in range(FOCI):
        for r in range(RCV_HERE):
            line = q * RCV_HERE + r
            onset[line : line + 1, :] = jnp.full((1, LANES), window[0, q, r], jnp.int32)
            ending[line : line + 1, :] = jnp.full((1, LANES), window[1, q, r], jnp.int32)
    time = lax.broadcasted_iota(jnp.int32, (FOCI * RCV_HERE, LANES), 1)
    kept = []
    for h in range(HALVES):
        inside = jnp.logical_and(time + h * LANES >= onset[...], time + h * LANES < ending[...])
        kept.append(jnp.where(inside, total[:, h * LANES : (h + 1) * LANES], 0.0))
    return start[...].astype(F32) + jnp.concatenate(kept, axis=1)


def next_kernel(
    window, parts, start, refl, fwd_high, fwd_low, inv_high, inv_low, out, onset, ending, spectrum, product, rows
):
    field = add_down(window, parts, start, onset, ending).astype(BF16)
    convolve_in(field, refl, fwd_high, fwd_low, inv_high, inv_low, out, spectrum, product, rows)


def last_kernel(window, parts, start, out, onset, ending):
    down = add_down(window, parts, start, onset, ending)
    share = LAGS // SHOT_AXIS
    begin = lax.axis_index("shot") * share
    mine = pltpu.roll(down, lax.rem(LAGS - begin, LAGS), 1)[:, :share]
    for q in range(FOCI):
        out[:, q, :] = mine[q * RCV_HERE : (q + 1) * RCV_HERE]


VM = pl.BlockSpec(memory_space=pltpu.VMEM)
SM = pl.BlockSpec(memory_space=pltpu.SMEM)
LIMIT = 24 * 1024 * 1024


def call(kernel, name, specs, outs, scratch, *args):
    many = len(outs) > 1
    shapes = [jax.ShapeDtypeStruct(shape, dtype) for shape, dtype in outs]
    return pl.pallas_call(
        kernel,
        name=name,
        in_specs=specs,
        out_specs=[VM] * len(outs) if many else VM,
        out_shape=shapes if many else shapes[0],
        scratch_shapes=[pltpu.VMEM(shape, dtype) for shape, dtype in scratch],
        compiler_params=pltpu.CompilerParams(vmem_limit_bytes=LIMIT),
    )(*args)


def over_plane():
    places = np.arange(RCV_AXIS).reshape(4, 2, 4)
    return places.transpose(1, 0, 2).reshape(2, 16).tolist()


def on_device(reflection, focus_index, shot_window, rcv_window):
    fwd_high, fwd_low, inv_high, inv_low, flip = [jnp.asarray(table) for table in tables()]
    waves = (fwd_high, fwd_low, inv_high, inv_low)
    shot_window = jnp.transpose(shot_window, (0, 2, 1))
    rcv_window = jnp.transpose(rcv_window, (0, 2, 1))
    traces = FOCI * RCV_HERE
    bounds = [((traces, LANES), jnp.int32)] * 2
    conv_scratch = [
        ((traces, 2 * LAGS), F32),
        ((FOCI * SHOTS_HERE, 2 * LAGS), F32),
        ((FOCI * HALVES * SHOTS_HERE, LANES), F32),
    ]
    corr_scratch = [conv_scratch[2], conv_scratch[1], conv_scratch[0]]
    conv_out = ((RCV_AXIS, SHARE, LANES), F32)
    picked = call(
        pick_kernel, "pick", [SM, VM, VM], [((SHOT_AXIS, traces, LAGS), BF16)], [], focus_index, reflection, flip
    )
    picked = lax.all_to_all(picked, "shot", 0, 0, tiled=True)
    refl = call(
        reflection_kernel, "reflection_spectra", [VM] * 3,
        [((4, RCV_HERE * SHOTS_HERE, LANES), F32)], [], reflection, fwd_high, fwd_low,
    )
    start, partial = call(
        first_kernel, "first_convolution", [VM] * 6, [((traces, LAGS), BF16), conv_out], conv_scratch,
        picked, refl, *waves,
    )
    for iteration in range(ITERS):
        parts = lax.all_to_all(partial, "rcv", 0, 0, tiled=True)
        focus_up, rounded = call(
            upgoing_kernel, "upgoing", [SM, VM],
            [((2, FOCI, LAGS), F32), ((16, SHARE, LANES), BF16)], [], shot_window, parts,
        )
        upgoing = lax.all_to_all(rounded, "rcv", 0, 0, tiled=True, axis_index_groups=over_plane())
        partial = call(
            correlate_kernel, "correlation", [VM] * 6, [((SHOT_AXIS, traces, LAGS), F32)], corr_scratch,
            upgoing, refl, *waves,
        )
        parts = lax.all_to_all(partial, "shot", 0, 0, tiled=True)
        if iteration + 1 < ITERS:
            partial = call(
                next_kernel, "next_convolution", [SM] + [VM] * 7, [conv_out], bounds + conv_scratch,
                rcv_window, parts, start, refl, *waves,
            )
    share = LAGS // SHOT_AXIS
    focus_down = call(
        last_kernel, "downgoing", [SM, VM, VM], [((RCV_HERE, FOCI, share), F32)], bounds, rcv_window, parts, start
    )
    return focus_down, focus_up


def solution(mesh):
    return jax.shard_map(
        on_device,
        mesh=mesh,
        in_specs=(P("shot", "rcv", None), P(), P(None, "shot", None), P(None, "rcv", None)),
        out_specs=(P("rcv", None, "shot"), P(("shot", "rcv"), None, None)),
        check_vma=False,
    )
```

time: 1440 us -> 118 us (0.08)
  waiting for transfers between devices: 502 us -> 0.48 us
  local copies, waits for them, and re-layouts: 449 us -> 5.65 us
  blocking collectives: 435 us -> 91 us
  matrix products: 21.1 us -> 0 us
  between operations: 19 us -> 0.74 us
    unnamed x6 -> x0, waiting for transfers between devices: 502 us -> none
    reshape x6 -> x0, local copies, waits for them, and re-layouts: 215 us -> none  [the longest x4 176 us: upper_toeplitz(): tiled.reshape(count, foci, lag_total, 2 * lag_total + 1)]
    all_gather x3 -> x0, blocking collectives: 212 us -> none  [the longest x2 194 us: on_device(): lax.all_gather(upgoing, 'rcv', axis=0, tiled=True)]
    unnamed x1 -> x0, blocking collectives: 196 us -> none
    another operation x12 -> x0, local copies, waits for them, and re-layouts: 119 us -> none  [the longest x8 93.1 us: upper_toeplitz(): jnp.tile(padded, (1, 1, lag_total + 1))]
    all_to_all x0 -> x6, blocking collectives: none -> 91 us  [the longest x2 38.2 us: on_device(): parts = lax.all_to_all(partial, 'rcv', 0, 0, tiled=True)]
    slice x7 -> x0, local copies, waits for them, and re-layouts: 69.8 us -> none  [the longest x4 55 us: upper_toeplitz(): jnp.tile(padded, (1, 1, lag_total + 1))]
    psum x1 -> x0, blocking collectives: 27.3 us -> none  [initial_field(): return lax.psum(stacked.astype(jnp.bfloat16), 'shot')]
  transfers between devices with their start and end apart: 3 -> 1, of which waited for: 3 -> 1; matrix products, arithmetic and copies ran while one was open for 0% -> 0% of each run, Pallas kernels for 0% -> 2%
where the time goes in v1:
time: 118 us
  blocking collectives  91 us (77%)
  Pallas kernels  12.7 us (11%)
  starting transfers between devices  7.4 us (6%)
  local copies, waits for them, and re-layouts  5.65 us (5%)
    all_to_all x2, blocking collectives, on_device(): parts = lax.all_to_all(partial, 'rcv', 0, 0, tiled=True)  38.2 us
    all_to_all x2, blocking collectives, on_device(): parts = lax.all_to_all(partial, 'shot', 0, 0, tiled=True)  34 us
    all_to_all x2, blocking collectives, on_device(): lax.all_to_all(rounded, 'rcv', 0, 0, tiled=True, axis_index_groups=over_p...  18.8 us
    pallas_call x9, Pallas kernels, call(): pl.pallas_call(kernel, name=name, in_specs=specs, out_specs=[VM] * len(ou...  12.7 us
    all_to_all x1, starting transfers between devices, on_device(): picked = lax.all_to_all(picked, 'shot', 0, 0, tiled=True)  7.4 us
    unnamed x24, local copies, waits for them, and re-layouts  5.65 us
  transfers between devices with their start and end apart: 1, of which 1 were waited for; matrix products, arithmetic and copies ran while one was open for 0% of the time, Pallas kernels for 2%

profile of v1, /device:TPU:1, one launch (start us, length us, event | category | flops | bytes accessed | tf_op | source)
XLA Modules:
  0.0 117.9 jit_solution(17793737374569343197)
XLA Ops:
  0.6 0.0 copy-start.1
  0.6 0.0 copy-start.3
  0.7 0.0 copy-start.4
  0.7 0.0 copy-start.5
  0.7 0.0 copy-start.6
  0.7 1.1 copy-done.6
  1.8 0.0 copy-start.8
  1.8 0.9 copy-done.8
  2.7 0.0 copy-start.11
  2.7 0.7 copy-done.11
  3.4 1.4 %pick.1 = bf16[8,32,256]{2,1,0:T(8,128)(2,1)} custom-call(s32[2]{0:T(128)S(1)} %copy-done.11, bf16[64,16,256]{2,1,0:T(8,128)(2,1)S(1)} %copy-done.6, bf16[256,256]{1,0:T(8,128)(2,1)S(1)} %copy-done.8), custom_call_target="tpu_custom_call" | custom-call | tf_op jit(solution)/shard_map/pick/pallas_call | solution.py:236
  4.7 7.4 %all-to-all-start = ((bf16[8,32,256]{2,1,0:T(8,128)(2,1)}), bf16[8,32,256]{2,1,0:T(8,128)(2,1)S(1)}, u32[]{:S(2)}, u32[]{:S(2)}) async-start(bf16[8,32,256]{2,1,0:T(8,128)(2,1)} %pick.1), calls=%async_computation | async-start | bytes 262144 | tf_op jit(solution)/shard_map/all_to_all | solution.py:269
  12.1 0.0 copy-start
  12.1 0.9 copy-done
  13.1 0.0 copy-start.2
  13.1 0.9 copy-done.2
  14.0 0.0 copy-start.7
  14.0 1.0 copy-done.7
  15.1 2.4 %reflection_spectra.1.refl = f32[4,1024,128]{2,1,0:T(8,128)S(1)} custom-call(bf16[64,16,256]{2,1,0:T(8,128)(2,1)S(1)} %copy-done.7, bf16[256,512]{1,0:T(8,128)(2,1)S(1)} %copy-done.2, bf16[256,512]{1,0:T(8,128)(2,1)S(1)} %copy-done), custom_call_target="tpu_custom_call" | custom-call | tf_op jit(solution)/shard_map/reflection_spectra/pallas_call | solution.py:236
  17.4 0.0 copy-start.9
  17.4 0.5 all-to-all-done.picked
  17.9 0.0 copy-done.1
  17.9 0.0 copy-done.3
  17.9 0.0 copy-done.4
  17.9 0.0 copy-done.5
  18.0 1.2 %first_convolution.1 = (bf16[32,256]{1,0:T(8,128)(2,1)S(1)}, f32[32,16,128]{2,1,0:T(8,128)S(1)}) custom-call(bf16[8,32,256]{2,1,0:T(8,128)(2,1)S(1)} %all-to-all-done.picked, f32[4,1024,128]{2,1,0:T(8,128)S(1)} %reflection_spectra.1.refl, bf16[256,512]{1,0:T(8,128)(2,1)S(1)} %copy-done.3, bf16[256,512]{1,0:T(8,128)(2,1)S(1)} %copy-done.1, ...), custom_call_target="tpu_custom_call" | custom-call | tf_op jit(solution)/shard_map/first_convolution/pallas_call | solution.py:236
  19.2 23.0 %all_to_all.35.parts = f32[32,16,128]{2,1,0:T(8,128)S(1)} all-to-all(f32[32,16,128]{2,1,0:T(8,128)S(1)} %get-tuple-element.7), channel_id=1, replica_groups=mesh['shot'=8,'rcv'=32] {'rcv'}, dimensions={0} | all-to-all | bytes 524288 | tf_op jit(solution)/shard_map/all_to_all | solution.py:279
  42.1 0.0 copy-done.9
  42.1 1.2 %upgoing.2 = (f32[2,2,256]{2,1,0:T(2,128)}, bf16[16,16,128]{2,1,0:T(8,128)(2,1)S(1)}) custom-call(s32[2,2,64]{2,1,0:T(2,128)S(1)} %bitcast.2, f32[32,16,128]{2,1,0:T(8,128)S(1)} %all_to_all.35.parts), custom_call_target="tpu_custom_call" | custom-call | tf_op jit(solution)/shard_map/upgoing/pallas_call | solution.py:236
  43.3 0.0 copy-start.10
  43.3 9.4 %all_to_all.36.upgoing = bf16[16,16,128]{2,1,0:T(8,128)(2,1)S(1)} all-to-all(bf16[16,16,128]{2,1,0:T(8,128)(2,1)S(1)} %get-tuple-element.8), channel_id=1, replica_groups={{0,1,2,3,8,9,10,11,16,17,18,19,24,25,26,27},{4,5,6,7,12,13,14,15,20,21,..., dimensions={0} | all-to-all | bytes 131072 | tf_op jit(solution)/shard_map/all_to_all | solution.py:284
  52.8 1.2 correlation.2
  53.9 17.8 %all_to_all.37.parts = f32[8,32,256]{2,1,0:T(8,128)S(1)} all-to-all(f32[8,32,256]{2,1,0:T(8,128)S(1)} %correlation.2), channel_id=1, replica_groups=mesh['shot'=8,'rcv'=32] {'shot'}, dimensions={0} | all-to-all | bytes 524288 | tf_op jit(solution)/shard_map/all_to_all | solution.py:289
  71.7 0.0 copy-done.10
  71.7 1.8 %next_convolution.1 = f32[32,16,128]{2,1,0:T(8,128)S(1)} custom-call(s32[2,2,16]{2,1,0:T(2,128)S(1)} %bitcast.4, f32[8,32,256]{2,1,0:T(8,128)S(1)} %all_to_all.37.parts, bf16[32,256]{1,0:T(8,128)(2,1)S(1)} %get-tuple-element.9.start, f32[4,1024,128]{2,1,0:T(8,128)S(1)} %reflection_spectra.1.refl, bf16[256,512]{1,0:T(8,128)(2,1)S(1)} %copy-done.3, ...), custom_call_target="tpu_custom_call" | custom-call | tf_op jit(solution)/shard_map/next_convolution/pallas_call | solution.py:236
  73.5 15.3 %all_to_all.38.parts = f32[32,16,128]{2,1,0:T(8,128)S(1)} all-to-all(f32[32,16,128]{2,1,0:T(8,128)S(1)} %next_convolution.1), channel_id=1, replica_groups=mesh['shot'=8,'rcv'=32] {'rcv'}, dimensions={0} | all-to-all | bytes 524288 | tf_op jit(solution)/shard_map/all_to_all | solution.py:279
  88.8 1.2 %upgoing.3 = (f32[2,2,256]{2,1,0:T(2,128)}, bf16[16,16,128]{2,1,0:T(8,128)(2,1)S(1)}) custom-call(s32[2,2,64]{2,1,0:T(2,128)S(1)} %bitcast.3, f32[32,16,128]{2,1,0:T(8,128)S(1)} %all_to_all.38.parts), custom_call_target="tpu_custom_call" | custom-call | tf_op jit(solution)/shard_map/upgoing/pallas_call | solution.py:236
  90.0 9.3 %all_to_all.39.upgoing = bf16[16,16,128]{2,1,0:T(8,128)(2,1)S(1)} all-to-all(bf16[16,16,128]{2,1,0:T(8,128)(2,1)S(1)} %get-tuple-element.10), channel_id=1, replica_groups={{0,1,2,3,8,9,10,11,16,17,18,19,24,25,26,27},{4,5,6,7,12,13,14,15,20,21,..., dimensions={0} | all-to-all | bytes 131072 | tf_op jit(solution)/shard_map/all_to_all | solution.py:284
  99.3 1.2 correlation.3
  100.5 16.2 %all_to_all.40.parts = f32[8,32,256]{2,1,0:T(8,128)S(1)} all-to-all(f32[8,32,256]{2,1,0:T(8,128)S(1)} %correlation.3), channel_id=1, replica_groups=mesh['shot'=8,'rcv'=32] {'shot'}, dimensions={0} | all-to-all | bytes 524288 | tf_op jit(solution)/shard_map/all_to_all | solution.py:289
  116.6 1.3 %downgoing.1 = f32[16,2,32]{2,1,0:T(2,128)} custom-call(s32[2,2,16]{2,1,0:T(2,128)S(1)} %bitcast.5, f32[8,32,256]{2,1,0:T(8,128)S(1)} %all_to_all.40.parts, bf16[32,256]{1,0:T(8,128)(2,1)S(1)} %get-tuple-element.9.start), custom_call_target="tpu_custom_call" | custom-call | tf_op jit(solution)/shard_map/downgoing/pallas_call | solution.py:236
Async XLA Ops:
  0.6 17.3 %copy-start.1 = (bf16[256,512]{1,0:T(8,128)(2,1)S(1)}, bf16[256,512]{1,0:T(8,128)(2,1)}, u32[]{:S(2)}) copy-start(bf16[256,512]{1,0:T(8,128)(2,1)} %constant.11.clone.low.fwd_low) | copy-start | bytes 786436
  0.6 17.3 %copy-start.3 = (bf16[256,512]{1,0:T(8,128)(2,1)S(1)}, bf16[256,512]{1,0:T(8,128)(2,1)}, u32[]{:S(2)}) copy-start(bf16[256,512]{1,0:T(8,128)(2,1)} %constant.10.clone.high.fwd_high) | copy-start | bytes 786436
  0.7 17.3 %copy-start.4 = (bf16[512,256]{1,0:T(8,128)(2,1)S(1)}, bf16[512,256]{1,0:T(8,128)(2,1)}, u32[]{:S(2)}) copy-start(bf16[512,256]{1,0:T(8,128)(2,1)} %constant.13.clone.inv_low) | copy-start | bytes 786436
  0.7 17.3 %copy-start.5 = (bf16[512,256]{1,0:T(8,128)(2,1)S(1)}, bf16[512,256]{1,0:T(8,128)(2,1)}, u32[]{:S(2)}) copy-start(bf16[512,256]{1,0:T(8,128)(2,1)} %constant.12.clone.inv_high) | copy-start | bytes 786436
  0.7 1.1 copy-start.6
  1.8 0.9 copy-start.8
  2.7 0.7 copy-start.11
  4.7 13.2 %all-to-all-start = ((bf16[8,32,256]{2,1,0:T(8,128)(2,1)}), bf16[8,32,256]{2,1,0:T(8,128)(2,1)S(1)}, u32[]{:S(2)}, u32[]{:S(2)}) async-start(bf16[8,32,256]{2,1,0:T(8,128)(2,1)} %pick.1), calls=%async_computation | async-start | bytes 262144 | tf_op jit(solution)/shard_map/all_to_all | solution.py:269
  12.1 0.9 copy-start
  13.1 0.9 copy-start.2
  14.0 1.0 copy-start.7
  17.4 24.7 %copy-start.9 = (s32[2,64,2]{1,2,0:T(2,128)S(1)}, s32[2,64,2]{1,2,0:T(2,128)}, u32[]{:S(2)}) copy-start(s32[2,64,2]{1,2,0:T(2,128)} %param.11) | copy-start | bytes 3076
  43.3 28.4 %copy-start.10 = (s32[2,16,2]{1,2,0:T(2,128)S(1)}, s32[2,16,2]{1,2,0:T(2,128)}, u32[]{:S(2)}) copy-start(s32[2,16,2]{1,2,0:T(2,128)} %param.12) | copy-start | bytes 772

commit v2 on v1

--- a/solution.py
+++ b/solution.py
@@ -55,29 +55,35 @@
     return (dot(top, high[...]) + (dot(top, low[...]) + dot(rest, high[...]))) * scale
 
 
-def pick_kernel(focus, reflection, flip, out):
-    first = lax.axis_index("shot") * SHOTS_HERE
-    picked = []
-    for which in range(FOCI):
-        row = focus[which] - first
-        inside = jnp.logical_and(row >= 0, row < SHOTS_HERE)
-        trace = reflection[jnp.clip(row, 0, SHOTS_HERE - 1)].astype(F32)
-        picked.append(jnp.where(inside, trace, 0.0).astype(BF16))
-    flipped = dot(jnp.concatenate(picked, axis=0), flip[...]).astype(BF16)
-    for place in range(SHOT_AXIS):
-        out[place] = flipped
-
-
 def shot_slot(shot):
     y, z, x, j = shot // 16, (shot // 8) % 2, (shot // 2) % 4, shot % 2
     return y * 16 + x * 4 + z * 2 + j
 
 
-def reflection_kernel(reflection, high, low, out):
+def prepare_kernel(
+    focus_hbm, shot_hbm, rcv_hbm, reflection_hbm, high_hbm, low_hbm, inv_high_hbm, inv_low_hbm, flip_hbm,
+    picks, out, shot_mask, rcv_mask, high, low, inv_high, inv_low, flip,
+    focus, shot_window, rcv_window, reflection, onset, ending, sems,
+):
+    def fetch(source, target, place):
+        copy = pltpu.make_async_copy(source, target, sems.at[place])
+        copy.start()
+        return copy
+
     step = 16
+    tables = [fetch(high_hbm, high, 0), fetch(low_hbm, low, 1)]
+    blocks = [
+        fetch(reflection_hbm.at[pl.ds(begin, step)], reflection.at[pl.ds(begin, step)], 2 + begin // step)
+        for begin in range(0, SHOTS_HERE, step)
+    ]
+    scalars = [fetch(focus_hbm, focus, 6), fetch(shot_hbm, shot_window, 7), fetch(rcv_hbm, rcv_window, 8)]
+    later = [fetch(inv_high_hbm, inv_high, 9), fetch(inv_low_hbm, inv_low, 10), fetch(flip_hbm, flip, 11)]
+    for copy in tables:
+        copy.wait()
     for begin in range(0, SHOTS_HERE, step):
-        rows = reflection[begin : begin + step].reshape(step * RCV_HERE, LAGS)
-        spectrum = to_spectrum(rows, high, low)
+        blocks[begin // step].wait()
+        lines = reflection[begin : begin + step].reshape(step * RCV_HERE, LAGS)
+        spectrum = to_spectrum(lines, high, low)
         for local in range(step):
             piece = spectrum[local * RCV_HERE : (local + 1) * RCV_HERE]
             slot = shot_slot(begin + local)
@@ -85,6 +91,49 @@
                 out[chunk, pl.ds(slot, RCV_HERE, SHOTS_HERE), :] = piece[
                     :, chunk * LANES : (chunk + 1) * LANES
                 ]
+    for copy in scalars:
+        copy.wait()
+    first = lax.axis_index("shot") * SHOTS_HERE
+    for which in range(FOCI):
+        row = focus[which] - first
+        inside = jnp.logical_and(row >= 0, row < SHOTS_HERE)
+        trace = reflection[jnp.clip(row, 0, SHOTS_HERE - 1)].astype(F32)
+        picked = jnp.where(inside, trace, 0.0).astype(BF16)
+        for place in range(SHOT_AXIS):
+            picks[place, which * RCV_HERE : (which + 1) * RCV_HERE, :] = picked
+    for copy in later:
+        copy.wait()
+    up_mask(shot_window, shot_mask)
+    down_mask(rcv_window, rcv_mask, onset, ending)
+
+
+def up_mask(window, out):
+    me = lax.axis_index("rcv")
+    corner = (me // 8) * 16 + (me % 4) * 2
+    row = lax.broadcasted_iota(jnp.int32, (SHARE, LANES), 0)
+    onset = jnp.zeros((SHARE, LANES), jnp.int32)
+    ending = jnp.zeros((SHARE, LANES), jnp.int32)
+    for z in range(2):
+        for j in range(2):
+            for q in range(FOCI):
+                shot = corner + z * 8 + j
+                mine = jnp.logical_and(row // 4 == z * 2 + j, row % 2 == q)
+                onset = jnp.where(mine, window[0, q, shot], onset)
+                ending = jnp.where(mine, window[1, q, shot], ending)
+    time = lax.broadcasted_iota(jnp.int32, (SHARE, LANES), 1) + ((row // 2) % 2) * LANES
+    out[...] = jnp.logical_and(time >= onset, time < ending).astype(jnp.int32)
+
+
+def down_mask(window, out, onset, ending):
+    for q in range(FOCI):
+        for r in range(RCV_HERE):
+            line = q * RCV_HERE + r
+            onset[line : line + 1, :] = jnp.full((1, LANES), window[0, q, r], jnp.int32)
+            ending[line : line + 1, :] = jnp.full((1, LANES), window[1, q, r], jnp.int32)
+    time = lax.broadcasted_iota(jnp.int32, (FOCI * RCV_HERE, LANES), 1)
+    for h in range(HALVES):
+        inside = jnp.logical_and(time + h * LANES >= onset[...], time + h * LANES < ending[...])
+        out[:, h * LANES : (h + 1) * LANES] = inside.astype(jnp.int32)
 
 
 def convolve_in(field, refl, fwd_high, fwd_low, inv_high, inv_low, out, spectrum, product, rows):
@@ -117,34 +166,23 @@
         out[place] = rows[group * SHARE : (group + 1) * SHARE, :]
 
 
-def first_kernel(picked, refl, fwd_high, fwd_low, inv_high, inv_low, start_out, out, spectrum, product, rows):
+def first_kernel(
+    picked, flip, refl, fwd_high, fwd_low, inv_high, inv_low, start_out, out, spectrum, product, rows
+):
     start = picked[0].astype(F32)
     for place in range(1, SHOT_AXIS):
         start = start + picked[place].astype(F32)
-    start = start.astype(BF16)
+    start = dot(start.astype(BF16), flip[...]).astype(BF16)
     start_out[...] = start
     convolve_in(start, refl, fwd_high, fwd_low, inv_high, inv_low, out, spectrum, product, rows)
 
 
-def upgoing_kernel(window, parts, up_out, out):
+def upgoing_kernel(mask, parts, up_out, out):
     total = parts[0]
     for place in range(1, RCV_AXIS):
         total = total + parts[place]
-    me = lax.axis_index("rcv")
-    corner = (me // 8) * 16 + (me % 4) * 2
-    row = lax.broadcasted_iota(jnp.int32, (SHARE, LANES), 0)
-    onset = jnp.zeros((SHARE, LANES), jnp.int32)
-    ending = jnp.zeros((SHARE, LANES), jnp.int32)
-    for z in range(2):
-        for j in range(2):
-            for q in range(FOCI):
-                shot = corner + z * 8 + j
-                mine = jnp.logical_and(row // 4 == z * 2 + j, row % 2 == q)
-                onset = jnp.where(mine, window[0, q, shot], onset)
-                ending = jnp.where(mine, window[1, q, shot], ending)
-    time = lax.broadcasted_iota(jnp.int32, (SHARE, LANES), 1) + ((row // 2) % 2) * LANES
-    up = jnp.where(jnp.logical_and(time >= onset, time < ending), total, 0.0)
-    own = jnp.where((me // 4) % 2 == 0, up[:8], up[8:])
+    up = jnp.where(mask[...] != 0, total, 0.0)
+    own = jnp.where((lax.axis_index("rcv") // 4) % 2 == 0, up[:8], up[8:])
     for j in range(2):
         for q in range(FOCI):
             for h in range(HALVES):
@@ -192,32 +230,20 @@
         out[place] = result
 
 
-def add_down(window, parts, start, onset, ending):
+def add_down(mask, parts, start):
     total = parts[0]
     for place in range(1, SHOT_AXIS):
         total = total + parts[place]
-    for q in range(FOCI):
-        for r in range(RCV_HERE):
-            line = q * RCV_HERE + r
-            onset[line : line + 1, :] = jnp.full((1, LANES), window[0, q, r], jnp.int32)
-            ending[line : line + 1, :] = jnp.full((1, LANES), window[1, q, r], jnp.int32)
-    time = lax.broadcasted_iota(jnp.int32, (FOCI * RCV_HERE, LANES), 1)
-    kept = []
-    for h in range(HALVES):
-        inside = jnp.logical_and(time + h * LANES >= onset[...], time + h * LANES < ending[...])
-        kept.append(jnp.where(inside, total[:, h * LANES : (h + 1) * LANES], 0.0))
-    return start[...].astype(F32) + jnp.concatenate(kept, axis=1)
-
-
-def next_kernel(
-    window, parts, start, refl, fwd_high, fwd_low, inv_high, inv_low, out, onset, ending, spectrum, product, rows
-):
-    field = add_down(window, parts, start, onset, ending).astype(BF16)
+    return start[...].astype(F32) + jnp.where(mask[...] != 0, total, 0.0)
+
+
+def next_kernel(mask, parts, start, refl, fwd_high, fwd_low, inv_high, inv_low, out, spectrum, product, rows):
+    field = add_down(mask, parts, start).astype(BF16)
     convolve_in(field, refl, fwd_high, fwd_low, inv_high, inv_low, out, spectrum, product, rows)
 
 
-def last_kernel(window, parts, start, out, onset, ending):
-    down = add_down(window, parts, start, onset, ending)
+def last_kernel(mask, parts, start, out):
+    down = add_down(mask, parts, start)
     share = LAGS // SHOT_AXIS
     begin = lax.axis_index("shot") * share
     mine = pltpu.roll(down, lax.rem(LAGS - begin, LAGS), 1)[:, :share]
@@ -226,7 +252,7 @@
 
 
 VM = pl.BlockSpec(memory_space=pltpu.VMEM)
-SM = pl.BlockSpec(memory_space=pltpu.SMEM)
+HB = pl.BlockSpec(memory_space=pltpu.HBM)
 LIMIT = 24 * 1024 * 1024
 
 
@@ -239,7 +265,7 @@
         in_specs=specs,
         out_specs=[VM] * len(outs) if many else VM,
         out_shape=shapes if many else shapes[0],
-        scratch_shapes=[pltpu.VMEM(shape, dtype) for shape, dtype in scratch],
+        scratch_shapes=scratch,
         compiler_params=pltpu.CompilerParams(vmem_limit_bytes=LIMIT),
     )(*args)
 
@@ -250,36 +276,48 @@
 
 
 def on_device(reflection, focus_index, shot_window, rcv_window):
-    fwd_high, fwd_low, inv_high, inv_low, flip = [jnp.asarray(table) for table in tables()]
-    waves = (fwd_high, fwd_low, inv_high, inv_low)
     shot_window = jnp.transpose(shot_window, (0, 2, 1))
     rcv_window = jnp.transpose(rcv_window, (0, 2, 1))
     traces = FOCI * RCV_HERE
-    bounds = [((traces, LANES), jnp.int32)] * 2
-    conv_scratch = [
-        ((traces, 2 * LAGS), F32),
-        ((FOCI * SHOTS_HERE, 2 * LAGS), F32),
-        ((FOCI * HALVES * SHOTS_HERE, LANES), F32),
-    ]
-    corr_scratch = [conv_scratch[2], conv_scratch[1], conv_scratch[0]]
+    fields = pltpu.VMEM((traces, 2 * LAGS), F32)
+    products = pltpu.VMEM((FOCI * SHOTS_HERE, 2 * LAGS), F32)
+    rows = pltpu.VMEM((FOCI * HALVES * SHOTS_HERE, LANES), F32)
+    conv_scratch = [fields, products, rows]
+    corr_scratch = [rows, products, fields]
     conv_out = ((RCV_AXIS, SHARE, LANES), F32)
-    picked = call(
-        pick_kernel, "pick", [SM, VM, VM], [((SHOT_AXIS, traces, LAGS), BF16)], [], focus_index, reflection, flip
+    sources = [focus_index, shot_window, rcv_window, reflection] + [jnp.asarray(table) for table in tables()]
+    picks, refl, shot_mask, rcv_mask, *waves, flip = call(
+        prepare_kernel, "preparation", [HB] * 9,
+        [
+            ((SHOT_AXIS, traces, LAGS), BF16),
+            ((4, RCV_HERE * SHOTS_HERE, LANES), F32),
+            ((SHARE, LANES), jnp.int32),
+            ((traces, LAGS), jnp.int32),
+            ((LAGS, 2 * LAGS), BF16),
+            ((LAGS, 2 * LAGS), BF16),
+            ((2 * LAGS, LAGS), BF16),
+            ((2 * LAGS, LAGS), BF16),
+            ((LAGS, LAGS), BF16),
+        ],
+        [
+            pltpu.SMEM((FOCI,), jnp.int32), pltpu.SMEM((2, FOCI, SHOTS_HERE), jnp.int32),
+            pltpu.SMEM((2, FOCI, RCV_HERE), jnp.int32),
+            pltpu.VMEM((SHOTS_HERE, RCV_HERE, LAGS), BF16),
+            pltpu.VMEM((traces, LANES), jnp.int32), pltpu.VMEM((traces, LANES), jnp.int32),
+            pltpu.SemaphoreType.DMA((12,)),
+        ],
+        *[pltpu.with_memory_space_constraint(source, pltpu.HBM) for source in sources],
     )
-    picked = lax.all_to_all(picked, "shot", 0, 0, tiled=True)
-    refl = call(
-        reflection_kernel, "reflection_spectra", [VM] * 3,
-        [((4, RCV_HERE * SHOTS_HERE, LANES), F32)], [], reflection, fwd_high, fwd_low,
-    )
+    picked = lax.all_to_all(picks, "shot", 0, 0, tiled=True)
     start, partial = call(
-        first_kernel, "first_convolution", [VM] * 6, [((traces, LAGS), BF16), conv_out], conv_scratch,
-        picked, refl, *waves,
+        first_kernel, "first_convolution", [VM] * 7, [((traces, LAGS), BF16), conv_out], conv_scratch,
+        picked, flip, refl, *waves,
     )
     for iteration in range(ITERS):
         parts = lax.all_to_all(partial, "rcv", 0, 0, tiled=True)
         focus_up, rounded = call(
-            upgoing_kernel, "upgoing", [SM, VM],
-            [((2, FOCI, LAGS), F32), ((16, SHARE, LANES), BF16)], [], shot_window, parts,
+            upgoing_kernel, "upgoing", [VM, VM],
+            [((2, FOCI, LAGS), F32), ((16, SHARE, LANES), BF16)], [], shot_mask, parts,
         )
         upgoing = lax.all_to_all(rounded, "rcv", 0, 0, tiled=True, axis_index_groups=over_plane())
         partial = call(
@@ -289,12 +327,12 @@
         parts = lax.all_to_all(partial, "shot", 0, 0, tiled=True)
         if iteration + 1 < ITERS:
             partial = call(
-                next_kernel, "next_convolution", [SM] + [VM] * 7, [conv_out], bounds + conv_scratch,
-                rcv_window, parts, start, refl, *waves,
+                next_kernel, "next_convolution", [VM] * 8, [conv_out], conv_scratch,
+                rcv_mask, parts, start, refl, *waves,
             )
     share = LAGS // SHOT_AXIS
     focus_down = call(
-        last_kernel, "downgoing", [SM, VM, VM], [((RCV_HERE, FOCI, share), F32)], bounds, rcv_window, parts, start
+        last_kernel, "downgoing", [VM, VM, VM], [((RCV_HERE, FOCI, share), F32)], [], rcv_mask, parts, start
     )
     return focus_down, focus_up
 

time: 118 us -> 115 us (0.975)
  blocking collectives: 91 us -> 103 us
  starting transfers between devices: 7.4 us -> 0 us
  local copies, waits for them, and re-layouts: 5.65 us -> 0 us
  Pallas kernels: 12.7 us -> 11.1 us
    all_to_all x0 -> x1, blocking collectives: none -> 13 us  [on_device(): picked = lax.all_to_all(picks, 'shot', 0, 0, tiled=True)]
    all_to_all x1 -> x0, starting transfers between devices: 7.4 us -> none  [on_device(): picked = lax.all_to_all(picked, 'shot', 0, 0, tiled=True)]
    unnamed x24 -> x0, local copies, waits for them, and re-layouts: 5.65 us -> none
    pallas_call x9 -> x8, Pallas kernels: 12.7 us -> 11.1 us  [call(): pl.pallas_call(kernel, name=name, in_specs=specs, out_specs=[VM] * len(ou...]
  transfers between devices with their start and end apart: 1 -> 0, of which waited for: 1 -> 0; matrix products, arithmetic and copies ran while one was open for 0% -> 0% of each run, Pallas kernels for 2% -> 0%
where the time goes in v2:
time: 115 us
  blocking collectives  103 us (90%)
  Pallas kernels  11.1 us (10%)
    all_to_all x2, blocking collectives, on_device(): parts = lax.all_to_all(partial, 'rcv', 0, 0, tiled=True)  38.2 us
    all_to_all x2, blocking collectives, on_device(): parts = lax.all_to_all(partial, 'shot', 0, 0, tiled=True)  32.9 us
    all_to_all x2, blocking collectives, on_device(): lax.all_to_all(rounded, 'rcv', 0, 0, tiled=True, axis_index_groups=over_p...  18.6 us
    all_to_all x1, blocking collectives, on_device(): picked = lax.all_to_all(picks, 'shot', 0, 0, tiled=True)  13 us
    pallas_call x8, Pallas kernels, call(): pl.pallas_call(kernel, name=name, in_specs=specs, out_specs=[VM] * len(ou...  11.1 us

profile of v2, /device:TPU:1, one launch (start us, length us, event | category | flops | bytes accessed | tf_op | source)
XLA Modules:
  0.0 114.5 jit_solution(3098182448153137647)
XLA Ops:
  0.6 4.3 %preparation.1 = (bf16[8,32,256]{2,1,0:T(8,128)(2,1)S(1)}, f32[4,1024,128]{2,1,0:T(8,128)S(1)}, s32[16,128]{1,0:T(8,128)S(1)}, s32[32,256]{1,0:T(8,128)S(1)}, bf...) custom-call(s32[2]{0:T(128)} %focus_hbm.1, ...), custom_call_target="tpu_custom_call" | custom-call | tf_op jit(solution)/shard_map/preparation/pallas_call | solution.py:262
  4.9 13.0 %all_to_all.35.picked = bf16[8,32,256]{2,1,0:T(8,128)(2,1)S(1)} all-to-all(bf16[8,32,256]{2,1,0:T(8,128)(2,1)S(1)} %get-tuple-element.18), channel_id=1, replica_groups=mesh['shot'=8,'rcv'=32] {'shot'}, dimensions={0} | all-to-all | bytes 262144 | tf_op jit(solution)/shard_map/all_to_all | solution.py:311
  17.9 1.3 %first_convolution.1 = (bf16[32,256]{1,0:T(8,128)(2,1)S(1)}, f32[32,16,128]{2,1,0:T(8,128)S(1)}) custom-call(bf16[8,32,256]{2,1,0:T(8,128)(2,1)S(1)} %all_to_all.35.picked, bf16[256,256]{1,0:T(8,128)(2,1)S(1)} %get-tuple-element.19.flip, f32[4,1024,128]{2,1,0:T(8,128)S(1)} %get-tuple-element.20.refl, bf16[256,512]{1,0:T(8,128)(2,1)S(1)} %get-tuple-element.21.fwd_high, ...), custom_call_target="tpu_custom_call" | custom-call | tf_op jit(solution)/shard_map/first_convolution/pallas_call | solution.py:262
  19.3 22.9 %all_to_all.36.parts = f32[32,16,128]{2,1,0:T(8,128)S(1)} all-to-all(f32[32,16,128]{2,1,0:T(8,128)S(1)} %get-tuple-element.25), channel_id=1, replica_groups=mesh['shot'=8,'rcv'=32] {'rcv'}, dimensions={0} | all-to-all | bytes 524288 | tf_op jit(solution)/shard_map/all_to_all | solution.py:317
  42.1 0.6 upgoing.2
  42.7 9.3 %all_to_all.37.upgoing = bf16[16,16,128]{2,1,0:T(8,128)(2,1)S(1)} all-to-all(bf16[16,16,128]{2,1,0:T(8,128)(2,1)S(1)} %get-tuple-element.26), channel_id=1, replica_groups={{0,1,2,3,8,9,10,11,16,17,18,19,24,25,26,27},{4,5,6,7,12,13,14,15,20,21,..., dimensions={0} | all-to-all | bytes 131072 | tf_op jit(solution)/shard_map/all_to_all | solution.py:322
  52.1 1.2 %correlation.2 = f32[8,32,256]{2,1,0:T(8,128)S(1)} custom-call(bf16[16,16,128]{2,1,0:T(8,128)(2,1)S(1)} %all_to_all.37.upgoing, f32[4,1024,128]{2,1,0:T(8,128)S(1)} %get-tuple-element.20.refl, bf16[256,512]{1,0:T(8,128)(2,1)S(1)} %get-tuple-element.21.fwd_high, bf16[256,512]{1,0:T(8,128)(2,1)S(1)} %get-tuple-element.22.fwd_low, ...), custom_call_target="tpu_custom_call" | custom-call | tf_op jit(solution)/shard_map/correlation/pallas_call | solution.py:262
  53.2 16.7 %all_to_all.38.parts = f32[8,32,256]{2,1,0:T(8,128)S(1)} all-to-all(f32[8,32,256]{2,1,0:T(8,128)S(1)} %correlation.2), channel_id=1, replica_groups=mesh['shot'=8,'rcv'=32] {'shot'}, dimensions={0} | all-to-all | bytes 524288 | tf_op jit(solution)/shard_map/all_to_all | solution.py:327
  70.0 1.2 %next_convolution.1 = f32[32,16,128]{2,1,0:T(8,128)S(1)} custom-call(s32[32,256]{1,0:T(8,128)S(1)} %get-tuple-element.16.mask, f32[8,32,256]{2,1,0:T(8,128)S(1)} %all_to_all.38.parts, bf16[32,256]{1,0:T(8,128)(2,1)S(1)} %get-tuple-element.27.start, f32[4,1024,128]{2,1,0:T(8,128)S(1)} %get-tuple-element.20.refl, ...), custom_call_target="tpu_custom_call" | custom-call | tf_op jit(solution)/shard_map/next_convolution/pallas_call | solution.py:262
  71.2 15.3 %all_to_all.39.parts = f32[32,16,128]{2,1,0:T(8,128)S(1)} all-to-all(f32[32,16,128]{2,1,0:T(8,128)S(1)} %next_convolution.1), channel_id=1, replica_groups=mesh['shot'=8,'rcv'=32] {'rcv'}, dimensions={0} | all-to-all | bytes 524288 | tf_op jit(solution)/shard_map/all_to_all | solution.py:317
  86.5 0.6 upgoing.3
  87.1 9.3 %all_to_all.40.upgoing = bf16[16,16,128]{2,1,0:T(8,128)(2,1)S(1)} all-to-all(bf16[16,16,128]{2,1,0:T(8,128)(2,1)S(1)} %get-tuple-element.28), channel_id=1, replica_groups={{0,1,2,3,8,9,10,11,16,17,18,19,24,25,26,27},{4,5,6,7,12,13,14,15,20,21,..., dimensions={0} | all-to-all | bytes 131072 | tf_op jit(solution)/shard_map/all_to_all | solution.py:322
  96.5 1.2 %correlation.3 = f32[8,32,256]{2,1,0:T(8,128)S(1)} custom-call(bf16[16,16,128]{2,1,0:T(8,128)(2,1)S(1)} %all_to_all.40.upgoing, f32[4,1024,128]{2,1,0:T(8,128)S(1)} %get-tuple-element.20.refl, bf16[256,512]{1,0:T(8,128)(2,1)S(1)} %get-tuple-element.21.fwd_high, bf16[256,512]{1,0:T(8,128)(2,1)S(1)} %get-tuple-element.22.fwd_low, ...), custom_call_target="tpu_custom_call" | custom-call | tf_op jit(solution)/shard_map/correlation/pallas_call | solution.py:262
  97.6 16.2 %all_to_all.41.parts = f32[8,32,256]{2,1,0:T(8,128)S(1)} all-to-all(f32[8,32,256]{2,1,0:T(8,128)S(1)} %correlation.3), channel_id=1, replica_groups=mesh['shot'=8,'rcv'=32] {'shot'}, dimensions={0} | all-to-all | bytes 524288 | tf_op jit(solution)/shard_map/all_to_all | solution.py:327
  113.8 0.7 downgoing.1

commit v3 on v2

--- a/solution.py
+++ b/solution.py
@@ -21,6 +21,7 @@
 SHOT_AXIS = 8
 SHARE = SHOTS_HERE * FOCI * 2 // 16
 HALVES = LAGS // LANES
+SHARE_LAGS = LAGS // SHOT_AXIS
 F32 = jnp.float32
 BF16 = jnp.bfloat16
 
@@ -60,10 +61,29 @@
     return y * 16 + x * 4 + z * 2 + j
 
 
+def pick_kernel(focus_hbm, reflection_hbm, out, focus, reflection, sems):
+    copies = [
+        pltpu.make_async_copy(focus_hbm, focus, sems.at[0]),
+        pltpu.make_async_copy(reflection_hbm, reflection, sems.at[1]),
+    ]
+    for copy in copies:
+        copy.start()
+    for copy in copies:
+        copy.wait()
+    first = lax.axis_index("shot") * SHOTS_HERE
+    for which in range(FOCI):
+        row = focus[which] - first
+        inside = jnp.logical_and(row >= 0, row < SHOTS_HERE)
+        trace = reflection[jnp.clip(row, 0, SHOTS_HERE - 1)].astype(F32)
+        picked = jnp.where(inside, trace, 0.0).astype(BF16)
+        for place in range(SHOT_AXIS):
+            out[place, which * RCV_HERE : (which + 1) * RCV_HERE, :] = picked
+
+
 def prepare_kernel(
-    focus_hbm, shot_hbm, rcv_hbm, reflection_hbm, high_hbm, low_hbm, inv_high_hbm, inv_low_hbm, flip_hbm,
-    picks, out, shot_mask, rcv_mask, high, low, inv_high, inv_low, flip,
-    focus, shot_window, rcv_window, reflection, onset, ending, sems,
+    shot_hbm, rcv_hbm, reflection_hbm, high_hbm, low_hbm, inv_high_hbm, inv_low_hbm, flip_hbm,
+    out, shot_mask, rcv_mask, high, low, inv_high, inv_low, flip,
+    shot_window, rcv_window, reflection, onset, ending, sems,
 ):
     def fetch(source, target, place):
         copy = pltpu.make_async_copy(source, target, sems.at[place])
@@ -76,8 +96,8 @@
         fetch(reflection_hbm.at[pl.ds(begin, step)], reflection.at[pl.ds(begin, step)], 2 + begin // step)
         for begin in range(0, SHOTS_HERE, step)
     ]
-    scalars = [fetch(focus_hbm, focus, 6), fetch(shot_hbm, shot_window, 7), fetch(rcv_hbm, rcv_window, 8)]
-    later = [fetch(inv_high_hbm, inv_high, 9), fetch(inv_low_hbm, inv_low, 10), fetch(flip_hbm, flip, 11)]
+    scalars = [fetch(shot_hbm, shot_window, 6), fetch(rcv_hbm, rcv_window, 7)]
+    later = [fetch(inv_high_hbm, inv_high, 8), fetch(inv_low_hbm, inv_low, 9), fetch(flip_hbm, flip, 10)]
     for copy in tables:
         copy.wait()
     for begin in range(0, SHOTS_HERE, step):
@@ -93,14 +113,6 @@
                 ]
     for copy in scalars:
         copy.wait()
-    first = lax.axis_index("shot") * SHOTS_HERE
-    for which in range(FOCI):
-        row = focus[which] - first
-        inside = jnp.logical_and(row >= 0, row < SHOTS_HERE)
-        trace = reflection[jnp.clip(row, 0, SHOTS_HERE - 1)].astype(F32)
-        picked = jnp.where(inside, trace, 0.0).astype(BF16)
-        for place in range(SHOT_AXIS):
-            picks[place, which * RCV_HERE : (which + 1) * RCV_HERE, :] = picked
     for copy in later:
         copy.wait()
     up_mask(shot_window, shot_mask)
@@ -193,7 +205,7 @@
         out[place] = rounded
 
 
-def correlate_kernel(upgoing, refl, fwd_high, fwd_low, inv_high, inv_low, out, rows, spectrum, product):
+def correlate_in(upgoing, refl, fwd_high, fwd_low, inv_high, inv_low, rows, spectrum, product):
     for place in range(16):
         rows[place * SHARE : (place + 1) * SHARE, :] = upgoing[place].astype(F32)
     traces = jnp.concatenate(
@@ -225,30 +237,48 @@
                 product[line : line + 1, re_lanes] = jnp.sum(totals[2 * q], axis=0, keepdims=True)
                 product[line : line + 1, im_lanes] = jnp.sum(totals[2 * q + 1], axis=0, keepdims=True)
     scale = 1.0 / (LAGS * math.sqrt(SHOTS_HERE * SHOT_AXIS * LAGS))
-    result = to_traces(product[...], inv_high, inv_low, scale)
+    return to_traces(product[...], inv_high, inv_low, scale)
+
+
+def correlate_kernel(upgoing, refl, fwd_high, fwd_low, inv_high, inv_low, out, rows, spectrum, product):
+    out[...] = correlate_in(upgoing, refl, fwd_high, fwd_low, inv_high, inv_low, rows, spectrum, product)
+
+
+def last_correlate_kernel(upgoing, refl, fwd_high, fwd_low, inv_high, inv_low, out, rows, spectrum, product):
+    result = correlate_in(upgoing, refl, fwd_high, fwd_low, inv_high, inv_low, rows, spectrum, product)
     for place in range(SHOT_AXIS):
-        out[place] = result
-
-
-def add_down(mask, parts, start):
+        piece = result[:, place * SHARE_LAGS : (place + 1) * SHARE_LAGS]
+        out[place] = jnp.concatenate([piece[begin : begin + 8] for begin in range(0, FOCI * RCV_HERE, 8)], axis=1)
+
+
+def pair_kernel(mine, other, out):
+    total = mine[...] + other[...]
+    for place in range(out.shape[0]):
+        out[place] = total
+
+
+def total_of(parts):
     total = parts[0]
-    for place in range(1, SHOT_AXIS):
+    for place in range(1, parts.shape[0]):
         total = total + parts[place]
-    return start[...].astype(F32) + jnp.where(mask[...] != 0, total, 0.0)
+    return total
 
 
 def next_kernel(mask, parts, start, refl, fwd_high, fwd_low, inv_high, inv_low, out, spectrum, product, rows):
-    field = add_down(mask, parts, start).astype(BF16)
-    convolve_in(field, refl, fwd_high, fwd_low, inv_high, inv_low, out, spectrum, product, rows)
+    down = start[...].astype(F32) + jnp.where(mask[...] != 0, total_of(parts), 0.0)
+    convolve_in(down.astype(BF16), refl, fwd_high, fwd_low, inv_high, inv_low, out, spectrum, product, rows)
 
 
 def last_kernel(mask, parts, start, out):
-    down = add_down(mask, parts, start)
-    share = LAGS // SHOT_AXIS
-    begin = lax.axis_index("shot") * share
-    mine = pltpu.roll(down, lax.rem(LAGS - begin, LAGS), 1)[:, :share]
+    begin = lax.axis_index("shot") * SHARE_LAGS
+    shift = lax.rem(LAGS - begin, LAGS)
+    start_here = pltpu.roll(start[...].astype(F32), shift, 1)[:, :SHARE_LAGS]
+    mask_here = pltpu.roll(mask[...], shift, 1)[:, :SHARE_LAGS]
+    total = total_of(parts)
+    total = jnp.concatenate([total[:, lane : lane + SHARE_LAGS] for lane in range(0, LANES, SHARE_LAGS)], axis=0)
+    down = start_here + jnp.where(mask_here != 0, total, 0.0)
     for q in range(FOCI):
-        out[:, q, :] = mine[q * RCV_HERE : (q + 1) * RCV_HERE]
+        out[:, q, :] = down[q * RCV_HERE : (q + 1) * RCV_HERE]
 
 
 VM = pl.BlockSpec(memory_space=pltpu.VMEM)
@@ -285,11 +315,21 @@
     conv_scratch = [fields, products, rows]
     corr_scratch = [rows, products, fields]
     conv_out = ((RCV_AXIS, SHARE, LANES), F32)
-    sources = [focus_index, shot_window, rcv_window, reflection] + [jnp.asarray(table) for table in tables()]
-    picks, refl, shot_mask, rcv_mask, *waves, flip = call(
-        prepare_kernel, "preparation", [HB] * 9,
+    def in_hbm(*arrays):
+        return [pltpu.with_memory_space_constraint(array, pltpu.HBM) for array in arrays]
+
+    picks = call(
+        pick_kernel, "pick", [HB] * 2, [((SHOT_AXIS, traces, LAGS), BF16)],
         [
-            ((SHOT_AXIS, traces, LAGS), BF16),
+            pltpu.SMEM((FOCI,), jnp.int32), pltpu.VMEM((SHOTS_HERE, RCV_HERE, LAGS), BF16),
+            pltpu.SemaphoreType.DMA((2,)),
+        ],
+        *in_hbm(focus_index, reflection),
+    )
+    picked = lax.all_to_all(picks, "shot", 0, 0, tiled=True)
+    refl, shot_mask, rcv_mask, *waves, flip = call(
+        prepare_kernel, "preparation", [HB] * 8,
+        [
             ((4, RCV_HERE * SHOTS_HERE, LANES), F32),
             ((SHARE, LANES), jnp.int32),
             ((traces, LAGS), jnp.int32),
@@ -300,15 +340,13 @@
             ((LAGS, LAGS), BF16),
         ],
         [
-            pltpu.SMEM((FOCI,), jnp.int32), pltpu.SMEM((2, FOCI, SHOTS_HERE), jnp.int32),
-            pltpu.SMEM((2, FOCI, RCV_HERE), jnp.int32),
+            pltpu.SMEM((2, FOCI, SHOTS_HERE), jnp.int32), pltpu.SMEM((2, FOCI, RCV_HERE), jnp.int32),
             pltpu.VMEM((SHOTS_HERE, RCV_HERE, LAGS), BF16),
             pltpu.VMEM((traces, LANES), jnp.int32), pltpu.VMEM((traces, LANES), jnp.int32),
-            pltpu.SemaphoreType.DMA((12,)),
+            pltpu.SemaphoreType.DMA((11,)),
         ],
-        *[pltpu.with_memory_space_constraint(source, pltpu.HBM) for source in sources],
-    )
-    picked = lax.all_to_all(picks, "shot", 0, 0, tiled=True)
+        *in_hbm(shot_window, rcv_window, reflection, *[jnp.asarray(table) for table in tables()]),
+    )
     start, partial = call(
         first_kernel, "first_convolution", [VM] * 7, [((traces, LAGS), BF16), conv_out], conv_scratch,
         picked, flip, refl, *waves,
@@ -320,19 +358,27 @@
             [((2, FOCI, LAGS), F32), ((16, SHARE, LANES), BF16)], [], shot_mask, parts,
         )
         upgoing = lax.all_to_all(rounded, "rcv", 0, 0, tiled=True, axis_index_groups=over_plane())
-        partial = call(
-            correlate_kernel, "correlation", [VM] * 6, [((SHOT_AXIS, traces, LAGS), F32)], corr_scratch,
-            upgoing, refl, *waves,
-        )
-        parts = lax.all_to_all(partial, "shot", 0, 0, tiled=True)
         if iteration + 1 < ITERS:
+            mine = call(
+                correlate_kernel, "correlation", [VM] * 6, [((traces, LAGS), F32)], corr_scratch,
+                upgoing, refl, *waves,
+            )
+            other = lax.ppermute(mine, "shot", [(place, place ^ 1) for place in range(SHOT_AXIS)])
+            pair = call(pair_kernel, "pair_sum", [VM] * 2, [((SHOT_AXIS // 2, traces, LAGS), F32)], [], mine, other)
+            chips = [list(range(core, SHOT_AXIS, 2)) for core in range(2)]
+            parts = lax.all_to_all(pair, "shot", 0, 0, tiled=True, axis_index_groups=chips)
             partial = call(
                 next_kernel, "next_convolution", [VM] * 8, [conv_out], conv_scratch,
                 rcv_mask, parts, start, refl, *waves,
             )
-    share = LAGS // SHOT_AXIS
+        else:
+            partial = call(
+                last_correlate_kernel, "last_correlation", [VM] * 6, [((SHOT_AXIS, 8, LANES), F32)],
+                corr_scratch, upgoing, refl, *waves,
+            )
+            parts = lax.all_to_all(partial, "shot", 0, 0, tiled=True)
     focus_down = call(
-        last_kernel, "downgoing", [VM, VM, VM], [((RCV_HERE, FOCI, share), F32)], [], rcv_mask, parts, start
+        last_kernel, "downgoing", [VM, VM, VM], [((RCV_HERE, FOCI, SHARE_LAGS), F32)], [], rcv_mask, parts, start
     )
     return focus_down, focus_up
 

time: 115 us -> 106 us (0.922)
  blocking collectives: 103 us -> 79.2 us
  starting transfers between devices: 0 us -> 11 us
  waiting for transfers between devices: 0 us -> 2.43 us
  Pallas kernels: 11.1 us -> 12.8 us
    all_to_all x2 -> x1, blocking collectives: 32.9 us -> 13.2 us  [on_device(): parts = lax.all_to_all(partial, 'shot', 0, 0, tiled=True)]
    all_to_all x0 -> x1, starting transfers between devices: none -> 7.41 us  [on_device(): picked = lax.all_to_all(picks, 'shot', 0, 0, tiled=True)]
    all_to_all x1, blocking collectives: 13 us -> 9.04 us  [on_device(): lax.all_to_all(pair, 'shot', 0, 0, tiled=True, axis_index_groups=chips)]
    ppermute x0 -> x1, starting transfers between devices: none -> 3.57 us  [on_device(): lax.ppermute(mine, 'shot', [(place, place ^ 1) for place in range(SHOT_AX...]
    pallas_call x8 -> x10, Pallas kernels: 11.1 us -> 12.8 us  [call(): pl.pallas_call(kernel, name=name, in_specs=specs, out_specs=[VM] * len(ou...]
    all_to_all x0 -> x1, waiting for transfers between devices: none -> 1.57 us  [on_device(): picked = lax.all_to_all(picks, 'shot', 0, 0, tiled=True)]
  transfers between devices with their start and end apart: 0 -> 2, of which waited for: 0 -> 2; matrix products, arithmetic and copies ran while one was open for 0% -> 0% of each run, Pallas kernels for 0% -> 4%
where the time goes in v3:
time: 106 us
  blocking collectives  79.2 us (75%)
  Pallas kernels  12.8 us (12%)
  starting transfers between devices  11 us (10%)
  waiting for transfers between devices  2.43 us (2%)
    all_to_all x2, blocking collectives, on_device(): parts = lax.all_to_all(partial, 'rcv', 0, 0, tiled=True)  38.3 us
    all_to_all x2, blocking collectives, on_device(): lax.all_to_all(rounded, 'rcv', 0, 0, tiled=True, axis_index_groups=over_p...  18.6 us
    all_to_all x1, blocking collectives, on_device(): parts = lax.all_to_all(partial, 'shot', 0, 0, tiled=True)  13.2 us
    pallas_call x10, Pallas kernels, call(): pl.pallas_call(kernel, name=name, in_specs=specs, out_specs=[VM] * len(ou...  12.8 us
    all_to_all x1, blocking collectives, on_device(): lax.all_to_all(pair, 'shot', 0, 0, tiled=True, axis_index_groups=chips)  9.04 us
    all_to_all x1, starting transfers between devices, on_device(): picked = lax.all_to_all(picks, 'shot', 0, 0, tiled=True)  7.41 us
    ppermute x1, starting transfers between devices, on_device(): lax.ppermute(mine, 'shot', [(place, place ^ 1) for place in range(SHOT_AX...  3.57 us
  transfers between devices with their start and end apart: 2, of which 2 were waited for; matrix products, arithmetic and copies ran while one was open for 0% of the time, Pallas kernels for 4%

profile of v3, /device:TPU:1, one launch (start us, length us, event | category | flops | bytes accessed | tf_op | source)
XLA Modules:
  0.0 106.0 jit_solution(8728053416877146727)
XLA Ops:
  0.6 1.7 %pick.1 = bf16[8,32,256]{2,1,0:T(8,128)(2,1)} custom-call(s32[2]{0:T(128)} %focus_hbm.1, bf16[64,16,256]{2,1,0:T(8,128)(2,1)} %reflection_hbm.3), custom_call_target="tpu_custom_call" | custom-call | tf_op jit(solution)/shard_map/pick/pallas_call | solution.py:292
  2.4 7.4 %all-to-all-start = ((bf16[8,32,256]{2,1,0:T(8,128)(2,1)}), bf16[8,32,256]{2,1,0:T(8,128)(2,1)S(1)}, u32[]{:S(2)}, u32[]{:S(2)}) async-start(bf16[8,32,256]{2,1,0:T(8,128)(2,1)} %pick.1), calls=%async_computation | async-start | bytes 262144 | tf_op jit(solution)/shard_map/all_to_all | solution.py:329
  9.8 4.2 %preparation.1 = (f32[4,1024,128]{2,1,0:T(8,128)S(1)}, s32[16,128]{1,0:T(8,128)S(1)}, s32[32,256]{1,0:T(8,128)S(1)}, bf16[256,512]{1,0:T(8,128)(2,1)S(1)}, bf16[...) custom-call(s32[2,2,64]{2,1,0:T(2,128)} %bitcast.2, ...), custom_call_target="tpu_custom_call" | custom-call | tf_op jit(solution)/shard_map/preparation/pallas_call | solution.py:292
  14.0 1.6 %all-to-all-done.picked = bf16[8,32,256]{2,1,0:T(8,128)(2,1)S(1)} async-done(((bf16[8,32,256]{2,1,0:T(8,128)(2,1)}), bf16[8,32,256]{2,1,0:T(8,128)(2,1)S(1)}, u32[]{:S(2)}, u32[]{:S(2)}) %all-to-all-start) | async-done | bytes 131104 | tf_op jit(solution)/shard_map/all_to_all | solution.py:329
  15.6 1.3 %first_convolution.1 = (bf16[32,256]{1,0:T(8,128)(2,1)S(1)}, f32[32,16,128]{2,1,0:T(8,128)S(1)}) custom-call(bf16[8,32,256]{2,1,0:T(8,128)(2,1)S(1)} %all-to-all-done.picked, bf16[256,256]{1,0:T(8,128)(2,1)S(1)} %get-tuple-element.17.flip, f32[4,1024,128]{2,1,0:T(8,128)S(1)} %get-tuple-element.18.refl, bf16[256,512]{1,0:T(8,128)(2,1)S(1)} %get-tuple-element.19.fwd_high, ...), custom_call_target="tpu_custom_call" | custom-call | tf_op jit(solution)/shard_map/first_convolution/pallas_call | solution.py:292
  16.9 23.0 %all_to_all.35.parts = f32[32,16,128]{2,1,0:T(8,128)S(1)} all-to-all(f32[32,16,128]{2,1,0:T(8,128)S(1)} %get-tuple-element.23), channel_id=1, replica_groups=mesh['shot'=8,'rcv'=32] {'rcv'}, dimensions={0} | all-to-all | bytes 524288 | tf_op jit(solution)/shard_map/all_to_all | solution.py:355
  39.8 0.6 upgoing.2
  40.5 9.3 %all_to_all.36.upgoing = bf16[16,16,128]{2,1,0:T(8,128)(2,1)S(1)} all-to-all(bf16[16,16,128]{2,1,0:T(8,128)(2,1)S(1)} %get-tuple-element.24), channel_id=1, replica_groups={{0,1,2,3,8,9,10,11,16,17,18,19,24,25,26,27},{4,5,6,7,12,13,14,15,20,21,..., dimensions={0} | all-to-all | bytes 131072 | tf_op jit(solution)/shard_map/all_to_all | solution.py:360
  49.8 1.1 %correlation.1.mine = f32[32,256]{1,0:T(8,128)S(1)} custom-call(bf16[16,16,128]{2,1,0:T(8,128)(2,1)S(1)} %all_to_all.36.upgoing, f32[4,1024,128]{2,1,0:T(8,128)S(1)} %get-tuple-element.18.refl, bf16[256,512]{1,0:T(8,128)(2,1)S(1)} %get-tuple-element.19.fwd_high, bf16[256,512]{1,0:T(8,128)(2,1)S(1)} %get-tuple-element.20.fwd_low, ...), custom_call_target="tpu_custom_call" | custom-call | tf_op jit(solution)/shard_map/correlation/pallas_call | solution.py:292
  50.9 3.6 %collective-permute-start = (f32[32,256]{1,0:T(8,128)S(1)}, f32[32,256]{1,0:T(8,128)S(1)}, u32[]{:S(2)}, u32[]{:S(2)}) collective-permute-start(f32[32,256]{1,0:T(8,128)S(1)} %correlation.1.mine), channel_id=1, source_target_pairs={{0,32},{32,0},{64,96},{96,64},{128,160},{160,128},{192,224},{224,1... | collective-permute-start | bytes 98312 | tf_op jit(solution)/shard_map/ppermute | solution.py:366
  54.5 0.9 collective-permute-done.other
  55.4 9.0 %all_to_all.37.parts = f32[4,32,256]{2,1,0:T(8,128)S(1)} all-to-all(f32[4,32,256]{2,1,0:T(8,128)S(1)} %pair_sum.1), channel_id=1, replica_groups={{0,64,128,192},{32,96,160,224},{1,65,129,193},{33,97,161,225},{2,66,130..., dimensions={0} | all-to-all | bytes 262144 | tf_op jit(solution)/shard_map/all_to_all | solution.py:369
  64.4 1.2 %next_convolution.1 = f32[32,16,128]{2,1,0:T(8,128)S(1)} custom-call(s32[32,256]{1,0:T(8,128)S(1)} %get-tuple-element.15.mask, f32[4,32,256]{2,1,0:T(8,128)S(1)} %all_to_all.37.parts, bf16[32,256]{1,0:T(8,128)(2,1)S(1)} %get-tuple-element.25.start, f32[4,1024,128]{2,1,0:T(8,128)S(1)} %get-tuple-element.18.refl, ...), custom_call_target="tpu_custom_call" | custom-call | tf_op jit(solution)/shard_map/next_convolution/pallas_call | solution.py:292
  65.6 15.4 %all_to_all.38.parts = f32[32,16,128]{2,1,0:T(8,128)S(1)} all-to-all(f32[32,16,128]{2,1,0:T(8,128)S(1)} %next_convolution.1), channel_id=1, replica_groups=mesh['shot'=8,'rcv'=32] {'rcv'}, dimensions={0} | all-to-all | bytes 524288 | tf_op jit(solution)/shard_map/all_to_all | solution.py:355
  81.0 0.6 upgoing.3
  81.6 9.2 %all_to_all.39.upgoing = bf16[16,16,128]{2,1,0:T(8,128)(2,1)S(1)} all-to-all(bf16[16,16,128]{2,1,0:T(8,128)(2,1)S(1)} %get-tuple-element.26), channel_id=1, replica_groups={{0,1,2,3,8,9,10,11,16,17,18,19,24,25,26,27},{4,5,6,7,12,13,14,15,20,21,..., dimensions={0} | all-to-all | bytes 131072 | tf_op jit(solution)/shard_map/all_to_all | solution.py:360
  90.9 1.2 %last_correlation.1 = f32[8,8,128]{2,1,0:T(8,128)S(1)} custom-call(bf16[16,16,128]{2,1,0:T(8,128)(2,1)S(1)} %all_to_all.39.upgoing, f32[4,1024,128]{2,1,0:T(8,128)S(1)} %get-tuple-element.18.refl, bf16[256,512]{1,0:T(8,128)(2,1)S(1)} %get-tuple-element.19.fwd_high, bf16[256,512]{1,0:T(8,128)(2,1)S(1)} %get-tuple-element.20.fwd_low, ...), custom_call_target="tpu_custom_call" | custom-call | tf_op jit(solution)/shard_map/last_correlation/pallas_call | solution.py:292
  92.1 13.2 %all_to_all.40.parts = f32[8,8,128]{2,1,0:T(8,128)S(1)} all-to-all(f32[8,8,128]{2,1,0:T(8,128)S(1)} %last_correlation.1), channel_id=1, replica_groups=mesh['shot'=8,'rcv'=32] {'shot'}, dimensions={0} | all-to-all | bytes 65536 | tf_op jit(solution)/shard_map/all_to_all | solution.py:379
  105.3 0.7 downgoing.1
  (1 shorter events, 0.0 us)
Async XLA Ops:
  2.4 13.2 %all-to-all-start = ((bf16[8,32,256]{2,1,0:T(8,128)(2,1)}), bf16[8,32,256]{2,1,0:T(8,128)(2,1)S(1)}, u32[]{:S(2)}, u32[]{:S(2)}) async-start(bf16[8,32,256]{2,1,0:T(8,128)(2,1)} %pick.1), calls=%async_computation | async-start | bytes 262144 | tf_op jit(solution)/shard_map/all_to_all | solution.py:329
  50.9 4.4 %collective-permute-start = (f32[32,256]{1,0:T(8,128)S(1)}, f32[32,256]{1,0:T(8,128)S(1)}, u32[]{:S(2)}, u32[]{:S(2)}) collective-permute-start(f32[32,256]{1,0:T(8,128)S(1)} %correlation.1.mine), channel_id=1, source_target_pairs={{0,32},{32,0},{64,96},{96,64},{128,160},{160,128},{192,224},{224,1... | collective-permute-start | bytes 98312 | tf_op jit(solution)/shard_map/ppermute | solution.py:366

commit v4 on v3

--- a/solution.py
+++ b/solution.py
@@ -21,6 +21,7 @@
 SHOT_AXIS = 8
 SHARE = SHOTS_HERE * FOCI * 2 // 16
 HALVES = LAGS // LANES
+PLANE = 16
 SHARE_LAGS = LAGS // SHOT_AXIS
 F32 = jnp.float32
 BF16 = jnp.bfloat16
@@ -173,9 +174,8 @@
             rows[pl.ds(h * FOCI + q, SHOTS_HERE, 2 * FOCI), :] = result[
                 q * SHOTS_HERE : (q + 1) * SHOTS_HERE, h * LANES : (h + 1) * LANES
             ]
-    for place in range(RCV_AXIS):
-        group = (place // 8) * 4 + place % 4
-        out[place] = rows[group * SHARE : (group + 1) * SHARE, :]
+    for place in range(PLANE):
+        out[place] = rows[place * SHARE : (place + 1) * SHARE, :]
 
 
 def first_kernel(
@@ -189,24 +189,21 @@
     convolve_in(start, refl, fwd_high, fwd_low, inv_high, inv_low, out, spectrum, product, rows)
 
 
-def upgoing_kernel(mask, parts, up_out, out):
-    total = parts[0]
-    for place in range(1, RCV_AXIS):
-        total = total + parts[place]
-    up = jnp.where(mask[...] != 0, total, 0.0)
-    own = jnp.where((lax.axis_index("rcv") // 4) % 2 == 0, up[:8], up[8:])
-    for j in range(2):
-        for q in range(FOCI):
-            for h in range(HALVES):
-                line = j * 4 + h * 2 + q
-                up_out[j, q : q + 1, h * LANES : (h + 1) * LANES] = own[line : line + 1]
+def sum_kernel(parts, out):
+    out[...] = total_of(parts)
+
+
+def upgoing_kernel(mask, mine, other, *outs):
+    up = jnp.where(mask[...] != 0, mine[...] + other[...], 0.0)
+    if len(outs) > 1:
+        outs[1][...] = jnp.where((lax.axis_index("rcv") // 4) % 2 == 0, up[:8], up[8:])
     rounded = up.astype(BF16)
-    for place in range(out.shape[0]):
-        out[place] = rounded
+    for place in range(PLANE):
+        outs[0][place] = rounded
 
 
 def correlate_in(upgoing, refl, fwd_high, fwd_low, inv_high, inv_low, rows, spectrum, product):
-    for place in range(16):
+    for place in range(PLANE):
         rows[place * SHARE : (place + 1) * SHARE, :] = upgoing[place].astype(F32)
     traces = jnp.concatenate(
         [
@@ -252,9 +249,7 @@
 
 
 def pair_kernel(mine, other, out):
-    total = mine[...] + other[...]
-    for place in range(out.shape[0]):
-        out[place] = total
+    out[...] = mine[...] + other[...]
 
 
 def total_of(parts):
@@ -264,12 +259,14 @@
     return total
 
 
-def next_kernel(mask, parts, start, refl, fwd_high, fwd_low, inv_high, inv_low, out, spectrum, product, rows):
-    down = start[...].astype(F32) + jnp.where(mask[...] != 0, total_of(parts), 0.0)
+def next_kernel(
+    mask, mine, other, start, refl, fwd_high, fwd_low, inv_high, inv_low, out, spectrum, product, rows
+):
+    down = start[...].astype(F32) + jnp.where(mask[...] != 0, mine[...] + other[...], 0.0)
     convolve_in(down.astype(BF16), refl, fwd_high, fwd_low, inv_high, inv_low, out, spectrum, product, rows)
 
 
-def last_kernel(mask, parts, start, out):
+def last_kernel(mask, parts, start, own, out, up_out):
     begin = lax.axis_index("shot") * SHARE_LAGS
     shift = lax.rem(LAGS - begin, LAGS)
     start_here = pltpu.roll(start[...].astype(F32), shift, 1)[:, :SHARE_LAGS]
@@ -279,6 +276,11 @@
     down = start_here + jnp.where(mask_here != 0, total, 0.0)
     for q in range(FOCI):
         out[:, q, :] = down[q * RCV_HERE : (q + 1) * RCV_HERE]
+    for j in range(2):
+        for q in range(FOCI):
+            for h in range(HALVES):
+                line = j * 4 + h * 2 + q
+                up_out[j, q : q + 1, h * LANES : (h + 1) * LANES] = own[line : line + 1]
 
 
 VM = pl.BlockSpec(memory_space=pltpu.VMEM)
@@ -288,7 +290,7 @@
 
 def call(kernel, name, specs, outs, scratch, *args):
     many = len(outs) > 1
-    shapes = [jax.ShapeDtypeStruct(shape, dtype) for shape, dtype in outs]
+    shapes = [jax.ShapeDtypeStruct(*out) if isinstance(out, tuple) else out for out in outs]
     return pl.pallas_call(
         kernel,
         name=name,
@@ -314,12 +316,12 @@
     rows = pltpu.VMEM((FOCI * HALVES * SHOTS_HERE, LANES), F32)
     conv_scratch = [fields, products, rows]
     corr_scratch = [rows, products, fields]
-    conv_out = ((RCV_AXIS, SHARE, LANES), F32)
+    conv_out = ((PLANE, SHARE, LANES), F32)
     def in_hbm(*arrays):
         return [pltpu.with_memory_space_constraint(array, pltpu.HBM) for array in arrays]
 
     picks = call(
-        pick_kernel, "pick", [HB] * 2, [((SHOT_AXIS, traces, LAGS), BF16)],
+        pick_kernel, "pick", [HB] * 2, [pltpu.VMEM((SHOT_AXIS, traces, LAGS), BF16)],
         [
             pltpu.SMEM((FOCI,), jnp.int32), pltpu.VMEM((SHOTS_HERE, RCV_HERE, LAGS), BF16),
             pltpu.SemaphoreType.DMA((2,)),
@@ -352,24 +354,29 @@
         picked, flip, refl, *waves,
     )
     for iteration in range(ITERS):
-        parts = lax.all_to_all(partial, "rcv", 0, 0, tiled=True)
-        focus_up, rounded = call(
-            upgoing_kernel, "upgoing", [VM, VM],
-            [((2, FOCI, LAGS), F32), ((16, SHARE, LANES), BF16)], [], shot_mask, parts,
-        )
+        parts = lax.all_to_all(partial, "rcv", 0, 0, tiled=True, axis_index_groups=over_plane())
+        mine = call(sum_kernel, "plane_sum", [VM], [((SHARE, LANES), F32)], [], parts)
+        other = lax.ppermute(mine, "rcv", [(place, place ^ 4) for place in range(RCV_AXIS)])
+        outs = [((PLANE, SHARE, LANES), BF16)]
+        if iteration + 1 < ITERS:
+            rounded = call(upgoing_kernel, "upgoing", [VM] * 3, outs, [], shot_mask, mine, other)
+        else:
+            rounded, own = call(
+                upgoing_kernel, "last_upgoing", [VM] * 3, outs + [((8, LANES), F32)], [], shot_mask, mine, other
+            )
         upgoing = lax.all_to_all(rounded, "rcv", 0, 0, tiled=True, axis_index_groups=over_plane())
         if iteration + 1 < ITERS:
             mine = call(
                 correlate_kernel, "correlation", [VM] * 6, [((traces, LAGS), F32)], corr_scratch,
                 upgoing, refl, *waves,
             )
-            other = lax.ppermute(mine, "shot", [(place, place ^ 1) for place in range(SHOT_AXIS)])
-            pair = call(pair_kernel, "pair_sum", [VM] * 2, [((SHOT_AXIS // 2, traces, LAGS), F32)], [], mine, other)
-            chips = [list(range(core, SHOT_AXIS, 2)) for core in range(2)]
-            parts = lax.all_to_all(pair, "shot", 0, 0, tiled=True, axis_index_groups=chips)
+            for step in (1, 2, 4):
+                other = lax.ppermute(mine, "shot", [(place, place ^ step) for place in range(SHOT_AXIS)])
+                if step < 4:
+                    mine = call(pair_kernel, "pair_sum", [VM] * 2, [((traces, LAGS), F32)], [], mine, other)
             partial = call(
-                next_kernel, "next_convolution", [VM] * 8, [conv_out], conv_scratch,
-                rcv_mask, parts, start, refl, *waves,
+                next_kernel, "next_convolution", [VM] * 9, [conv_out], conv_scratch,
+                rcv_mask, mine, other, start, refl, *waves,
             )
         else:
             partial = call(
@@ -377,8 +384,9 @@
                 corr_scratch, upgoing, refl, *waves,
             )
             parts = lax.all_to_all(partial, "shot", 0, 0, tiled=True)
-    focus_down = call(
-        last_kernel, "downgoing", [VM, VM, VM], [((RCV_HERE, FOCI, SHARE_LAGS), F32)], [], rcv_mask, parts, start
+    focus_down, focus_up = call(
+        last_kernel, "downgoing", [VM] * 4, [((RCV_HERE, FOCI, SHARE_LAGS), F32), ((2, FOCI, LAGS), F32)], [],
+        rcv_mask, parts, start, own,
     )
     return focus_down, focus_up
 

time: 106 us -> 103 us (0.972)
  blocking collectives: 79.2 us -> 56.3 us
  starting transfers between devices: 11 us -> 21.7 us
  waiting for transfers between devices: 2.43 us -> 12.3 us
  Pallas kernels: 12.8 us -> 11.6 us
    all_to_all x3 -> x2, blocking collectives: 47.4 us -> 23.1 us  [on_device(): lax.all_to_all(partial, 'rcv', 0, 0, tiled=True, axis_index_groups=over_p...]
    ppermute x1 -> x5, starting transfers between devices: 3.57 us -> 14.3 us  [the longest x2 8.8 us: on_device(): lax.ppermute(mine, 'rcv', [(place, place ^ 4) for place in range(RCV_AXIS)])]
    ppermute x1 -> x5, waiting for transfers between devices: 0.86 us -> 10.7 us  [the longest x3 6.55 us: on_device(): lax.ppermute(mine, 'shot', [(place, place ^ step) for place in range(SHOT...]
    pallas_call x10 -> x13, Pallas kernels: 12.8 us -> 11.6 us  [call(): pl.pallas_call(kernel, name=name, in_specs=specs, out_specs=[VM] * len(ou...]
    all_to_all x1, blocking collectives: 13.2 us -> 14.3 us  [on_device(): parts = lax.all_to_all(partial, 'shot', 0, 0, tiled=True)]
  transfers between devices with their start and end apart: 2 -> 6, of which waited for: 2 -> 6; matrix products, arithmetic and copies ran while one was open for 0% -> 0% of each run, Pallas kernels for 4% -> 4%
where the time goes in v4:
time: 103 us
  blocking collectives  56.3 us (55%)
  starting transfers between devices  21.7 us (21%)
  waiting for transfers between devices  12.3 us (12%)
  Pallas kernels  11.6 us (11%)
    all_to_all x2, blocking collectives, on_device(): lax.all_to_all(partial, 'rcv', 0, 0, tiled=True, axis_index_groups=over_p...  23.1 us
    all_to_all x2, blocking collectives, on_device(): lax.all_to_all(rounded, 'rcv', 0, 0, tiled=True, axis_index_groups=over_p...  18.9 us
    all_to_all x1, blocking collectives, on_device(): parts = lax.all_to_all(partial, 'shot', 0, 0, tiled=True)  14.3 us
    pallas_call x13, Pallas kernels, call(): pl.pallas_call(kernel, name=name, in_specs=specs, out_specs=[VM] * len(ou...  11.6 us
    ppermute x2, starting transfers between devices, on_device(): lax.ppermute(mine, 'rcv', [(place, place ^ 4) for place in range(RCV_AXIS)])  8.8 us
    all_to_all x1, starting transfers between devices, on_device(): picked = lax.all_to_all(picks, 'shot', 0, 0, tiled=True)  7.41 us
    ppermute x3, waiting for transfers between devices, on_device(): lax.ppermute(mine, 'shot', [(place, place ^ step) for place in range(SHOT...  6.55 us
    ppermute x3, starting transfers between devices, on_device(): lax.ppermute(mine, 'shot', [(place, place ^ step) for place in range(SHOT...  5.5 us
  transfers between devices with their start and end apart: 6, of which 6 were waited for; matrix products, arithmetic and copies ran while one was open for 0% of the time, Pallas kernels for 4%

profile of v4, /device:TPU:1, one launch (start us, length us, event | category | flops | bytes accessed | tf_op | source)
XLA Modules:
  0.0 102.6 jit_solution(12121553824485045472)
XLA Ops:
  0.6 1.7 %pick.1 = bf16[8,32,256]{2,1,0:T(8,128)(2,1)} custom-call(s32[2]{0:T(128)} %focus_hbm.1, bf16[64,16,256]{2,1,0:T(8,128)(2,1)} %reflection_hbm.3), custom_call_target="tpu_custom_call" | custom-call | tf_op jit(solution)/shard_map/pick/pallas_call | solution.py:294
  2.4 7.4 %all-to-all-start = ((bf16[8,32,256]{2,1,0:T(8,128)(2,1)}), bf16[8,32,256]{2,1,0:T(8,128)(2,1)S(1)}, u32[]{:S(2)}, u32[]{:S(2)}) async-start(bf16[8,32,256]{2,1,0:T(8,128)(2,1)} %pick.1), calls=%async_computation | async-start | bytes 262144 | tf_op jit(solution)/shard_map/all_to_all | solution.py:331
  9.8 4.2 %preparation.1 = (f32[4,1024,128]{2,1,0:T(8,128)S(1)}, s32[16,128]{1,0:T(8,128)S(1)}, s32[32,256]{1,0:T(8,128)S(1)}, bf16[256,512]{1,0:T(8,128)(2,1)S(1)}, bf16[...) custom-call(s32[2,2,64]{2,1,0:T(2,128)} %bitcast.2, ...), custom_call_target="tpu_custom_call" | custom-call | tf_op jit(solution)/shard_map/preparation/pallas_call | solution.py:294
  14.0 1.6 %all-to-all-done.picked = bf16[8,32,256]{2,1,0:T(8,128)(2,1)S(1)} async-done(((bf16[8,32,256]{2,1,0:T(8,128)(2,1)}), bf16[8,32,256]{2,1,0:T(8,128)(2,1)S(1)}, u32[]{:S(2)}, u32[]{:S(2)}) %all-to-all-start) | async-done | bytes 131104 | tf_op jit(solution)/shard_map/all_to_all | solution.py:331
  15.6 1.3 %first_convolution.1 = (bf16[32,256]{1,0:T(8,128)(2,1)S(1)}, f32[16,16,128]{2,1,0:T(8,128)S(1)}) custom-call(bf16[8,32,256]{2,1,0:T(8,128)(2,1)S(1)} %all-to-all-done.picked, bf16[256,256]{1,0:T(8,128)(2,1)S(1)} %get-tuple-element.16.flip, f32[4,1024,128]{2,1,0:T(8,128)S(1)} %get-tuple-element.17.refl, bf16[256,512]{1,0:T(8,128)(2,1)S(1)} %get-tuple-element.18.fwd_high, ...), custom_call_target="tpu_custom_call" | custom-call | tf_op jit(solution)/shard_map/first_convolution/pallas_call | solution.py:294
  16.9 13.4 %all_to_all.30.parts = f32[16,16,128]{2,1,0:T(8,128)S(1)} all-to-all(f32[16,16,128]{2,1,0:T(8,128)S(1)} %get-tuple-element.22), channel_id=1, replica_groups={{0,1,2,3,8,9,10,11,16,17,18,19,24,25,26,27},{4,5,6,7,12,13,14,15,20,21,..., dimensions={0} | all-to-all | bytes 262144 | tf_op jit(solution)/shard_map/all_to_all | solution.py:357
  30.3 4.4 %collective-permute-start = (f32[16,128]{1,0:T(8,128)S(1)}, f32[16,128]{1,0:T(8,128)S(1)}, u32[]{:S(2)}, u32[]{:S(2)}) collective-permute-start(f32[16,128]{1,0:T(8,128)S(1)} %plane_sum.2.mine), channel_id=1, source_target_pairs={{0,4},{1,5},{2,6},{3,7},{4,0},{5,1},{6,2},{7,3},{8,12},{9,13},{10,... | collective-permute-start | bytes 24584 | tf_op jit(solution)/shard_map/ppermute | solution.py:359
  34.7 2.1 %collective-permute-done.other = f32[16,128]{1,0:T(8,128)S(1)} collective-permute-done((f32[16,128]{1,0:T(8,128)S(1)}, f32[16,128]{1,0:T(8,128)S(1)}, u32[]{:S(2)}, u32[]{:S(2)}) %collective-permute-start) | collective-permute-done | bytes 8224 | tf_op jit(solution)/shard_map/ppermute | solution.py:359
  36.8 9.6 %all_to_all.31.upgoing = bf16[16,16,128]{2,1,0:T(8,128)(2,1)S(1)} all-to-all(bf16[16,16,128]{2,1,0:T(8,128)(2,1)S(1)} %upgoing.1), channel_id=1, replica_groups={{0,1,2,3,8,9,10,11,16,17,18,19,24,25,26,27},{4,5,6,7,12,13,14,15,20,21,..., dimensions={0} | all-to-all | bytes 131072 | tf_op jit(solution)/shard_map/all_to_all | solution.py:367
  46.4 1.1 %correlation.1.mine = f32[32,256]{1,0:T(8,128)S(1)} custom-call(bf16[16,16,128]{2,1,0:T(8,128)(2,1)S(1)} %all_to_all.31.upgoing, f32[4,1024,128]{2,1,0:T(8,128)S(1)} %get-tuple-element.17.refl, bf16[256,512]{1,0:T(8,128)(2,1)S(1)} %get-tuple-element.18.fwd_high, bf16[256,512]{1,0:T(8,128)(2,1)S(1)} %get-tuple-element.19.fwd_low, ...), custom_call_target="tpu_custom_call" | custom-call | tf_op jit(solution)/shard_map/correlation/pallas_call | solution.py:294
  47.5 4.8 %collective-permute-start.1 = (f32[32,256]{1,0:T(8,128)S(1)}, f32[32,256]{1,0:T(8,128)S(1)}, u32[]{:S(2)}, u32[]{:S(2)}) collective-permute-start(f32[32,256]{1,0:T(8,128)S(1)} %correlation.1.mine), channel_id=1, source_target_pairs={{0,32},{32,0},{64,96},{96,64},{128,160},{160,128},{192,224},{224,1... | collective-permute-start | bytes 98312 | tf_op jit(solution)/shard_map/ppermute | solution.py:374
  52.3 0.9 collective-permute-done.1.other
  53.2 0.6 collective-permute-start.2
  53.8 2.1 %collective-permute-done.2.other = f32[32,256]{1,0:T(8,128)S(1)} collective-permute-done((f32[32,256]{1,0:T(8,128)S(1)}, f32[32,256]{1,0:T(8,128)S(1)}, u32[]{:S(2)}, u32[]{:S(2)}) %collective-permute-start.2) | collective-permute-done | bytes 32800 | tf_op jit(solution)/shard_map/ppermute | solution.py:374
  55.9 0.1 collective-permute-start.3
  56.1 3.6 %collective-permute-done.3.other = f32[32,256]{1,0:T(8,128)S(1)} collective-permute-done((f32[32,256]{1,0:T(8,128)S(1)}, f32[32,256]{1,0:T(8,128)S(1)}, u32[]{:S(2)}, u32[]{:S(2)}) %collective-permute-start.3) | collective-permute-done | bytes 32800 | tf_op jit(solution)/shard_map/ppermute | solution.py:374
  59.6 1.2 %next_convolution.1 = f32[16,16,128]{2,1,0:T(8,128)S(1)} custom-call(s32[32,256]{1,0:T(8,128)S(1)} %get-tuple-element.14.mask, f32[32,256]{1,0:T(8,128)S(1)} %pair_sum.3.mine, f32[32,256]{1,0:T(8,128)S(1)} %collective-permute-done.3.other, bf16[32,256]{1,0:T(8,128)(2,1)S(1)} %get-tuple-element.23.start, f32[4,1024,128]{2,1,0:T(8,128)S(1)} %get-tuple-element.17.refl, ...), custom_call_target="tpu_custom_call" | custom-call | tf_op jit(solution)/shard_map/next_convolution/pallas_call | solution.py:294
  60.8 9.7 %all_to_all.32.parts = f32[16,16,128]{2,1,0:T(8,128)S(1)} all-to-all(f32[16,16,128]{2,1,0:T(8,128)S(1)} %next_convolution.1), channel_id=1, replica_groups={{0,1,2,3,8,9,10,11,16,17,18,19,24,25,26,27},{4,5,6,7,12,13,14,15,20,21,..., dimensions={0} | all-to-all | bytes 262144 | tf_op jit(solution)/shard_map/all_to_all | solution.py:357
  70.5 4.4 %collective-permute-start.4 = (f32[16,128]{1,0:T(8,128)S(1)}, f32[16,128]{1,0:T(8,128)S(1)}, u32[]{:S(2)}, u32[]{:S(2)}) collective-permute-start(f32[16,128]{1,0:T(8,128)S(1)} %plane_sum.3.mine), channel_id=1, source_target_pairs={{0,4},{1,5},{2,6},{3,7},{4,0},{5,1},{6,2},{7,3},{8,12},{9,13},{10,... | collective-permute-start | bytes 24584 | tf_op jit(solution)/shard_map/ppermute | solution.py:359
  74.9 2.1 %collective-permute-done.4.other = f32[16,128]{1,0:T(8,128)S(1)} collective-permute-done((f32[16,128]{1,0:T(8,128)S(1)}, f32[16,128]{1,0:T(8,128)S(1)}, u32[]{:S(2)}, u32[]{:S(2)}) %collective-permute-start.4) | collective-permute-done | bytes 8224 | tf_op jit(solution)/shard_map/ppermute | solution.py:359
  77.0 9.3 %all_to_all.33.upgoing = bf16[16,16,128]{2,1,0:T(8,128)(2,1)S(1)} all-to-all(bf16[16,16,128]{2,1,0:T(8,128)(2,1)S(1)} %get-tuple-element.24), channel_id=1, replica_groups={{0,1,2,3,8,9,10,11,16,17,18,19,24,25,26,27},{4,5,6,7,12,13,14,15,20,21,..., dimensions={0} | all-to-all | bytes 131072 | tf_op jit(solution)/shard_map/all_to_all | solution.py:367
  86.3 1.2 %last_correlation.1 = f32[8,8,128]{2,1,0:T(8,128)S(1)} custom-call(bf16[16,16,128]{2,1,0:T(8,128)(2,1)S(1)} %all_to_all.33.upgoing, f32[4,1024,128]{2,1,0:T(8,128)S(1)} %get-tuple-element.17.refl, bf16[256,512]{1,0:T(8,128)(2,1)S(1)} %get-tuple-element.18.fwd_high, bf16[256,512]{1,0:T(8,128)(2,1)S(1)} %get-tuple-element.19.fwd_low, ...), custom_call_target="tpu_custom_call" | custom-call | tf_op jit(solution)/shard_map/last_correlation/pallas_call | solution.py:294
  87.6 14.3 %all_to_all.34.parts = f32[8,8,128]{2,1,0:T(8,128)S(1)} all-to-all(f32[8,8,128]{2,1,0:T(8,128)S(1)} %last_correlation.1), channel_id=1, replica_groups=mesh['shot'=8,'rcv'=32] {'shot'}, dimensions={0} | all-to-all | bytes 65536 | tf_op jit(solution)/shard_map/all_to_all | solution.py:386
  101.9 0.7 downgoing.1
  (6 shorter events, 0.1 us)
Async XLA Ops:
  2.4 13.2 %all-to-all-start = ((bf16[8,32,256]{2,1,0:T(8,128)(2,1)}), bf16[8,32,256]{2,1,0:T(8,128)(2,1)S(1)}, u32[]{:S(2)}, u32[]{:S(2)}) async-start(bf16[8,32,256]{2,1,0:T(8,128)(2,1)} %pick.1), calls=%async_computation | async-start | bytes 262144 | tf_op jit(solution)/shard_map/all_to_all | solution.py:331
  30.3 6.5 %collective-permute-start = (f32[16,128]{1,0:T(8,128)S(1)}, f32[16,128]{1,0:T(8,128)S(1)}, u32[]{:S(2)}, u32[]{:S(2)}) collective-permute-start(f32[16,128]{1,0:T(8,128)S(1)} %plane_sum.2.mine), channel_id=1, source_target_pairs={{0,4},{1,5},{2,6},{3,7},{4,0},{5,1},{6,2},{7,3},{8,12},{9,13},{10,... | collective-permute-start | bytes 24584 | tf_op jit(solution)/shard_map/ppermute | solution.py:359
  47.5 5.6 %collective-permute-start.1 = (f32[32,256]{1,0:T(8,128)S(1)}, f32[32,256]{1,0:T(8,128)S(1)}, u32[]{:S(2)}, u32[]{:S(2)}) collective-permute-start(f32[32,256]{1,0:T(8,128)S(1)} %correlation.1.mine), channel_id=1, source_target_pairs={{0,32},{32,0},{64,96},{96,64},{128,160},{160,128},{192,224},{224,1... | collective-permute-start | bytes 98312 | tf_op jit(solution)/shard_map/ppermute | solution.py:374
  53.2 2.8 %collective-permute-start.2 = (f32[32,256]{1,0:T(8,128)S(1)}, f32[32,256]{1,0:T(8,128)S(1)}, u32[]{:S(2)}, u32[]{:S(2)}) collective-permute-start(f32[32,256]{1,0:T(8,128)S(1)} %pair_sum.2.mine), channel_id=1, source_target_pairs={{0,64},{32,96},{64,0},{96,32},{128,192},{160,224},{192,128},{224,1... | collective-permute-start | bytes 98312 | tf_op jit(solution)/shard_map/ppermute | solution.py:374
  55.9 3.7 %collective-permute-start.3 = (f32[32,256]{1,0:T(8,128)S(1)}, f32[32,256]{1,0:T(8,128)S(1)}, u32[]{:S(2)}, u32[]{:S(2)}) collective-permute-start(f32[32,256]{1,0:T(8,128)S(1)} %pair_sum.3.mine), channel_id=1, source_target_pairs={{0,128},{32,160},{64,192},{96,224},{128,0},{160,32},{192,64},{224,... | collective-permute-start | bytes 98312 | tf_op jit(solution)/shard_map/ppermute | solution.py:374
  70.5 6.5 %collective-permute-start.4 = (f32[16,128]{1,0:T(8,128)S(1)}, f32[16,128]{1,0:T(8,128)S(1)}, u32[]{:S(2)}, u32[]{:S(2)}) collective-permute-start(f32[16,128]{1,0:T(8,128)S(1)} %plane_sum.3.mine), channel_id=1, source_target_pairs={{0,4},{1,5},{2,6},{3,7},{4,0},{5,1},{6,2},{7,3},{8,12},{9,13},{10,... | collective-permute-start | bytes 24584 | tf_op jit(solution)/shard_map/ppermute | solution.py:359

commit v5 on v4

--- a/solution.py
+++ b/solution.py
@@ -54,7 +54,14 @@
 def to_traces(spectrum, high, low, scale):
     top = spectrum.astype(BF16)
     rest = (spectrum - top.astype(F32)).astype(BF16)
-    return (dot(top, high[...]) + (dot(top, low[...]) + dot(rest, high[...]))) * scale
+    both = dot(jnp.concatenate([top, rest], axis=0), high[...])
+    count = spectrum.shape[0]
+    return (both[:count] + (dot(top, low[...]) + both[count:])) * scale
+
+
+def factors(spectrum):
+    re, im = spectrum[:, :LAGS], spectrum[:, LAGS:]
+    return re, im - re, im + re
 
 
 def shot_slot(shot):
@@ -150,23 +157,28 @@
 
 
 def convolve_in(field, refl, fwd_high, fwd_low, inv_high, inv_low, out, spectrum, product, rows):
-    spectrum[...] = to_spectrum(field, fwd_high, fwd_low)
+    for kind, part in enumerate(factors(to_spectrum(field, fwd_high, fwd_low))):
+        spectrum[kind] = part
+    half = SHOTS_HERE // 2
     for chunk in range(2):
-        re_lanes = slice(chunk * LANES, (chunk + 1) * LANES)
+        lanes = slice(chunk * LANES, (chunk + 1) * LANES)
         im_lanes = slice(LAGS + chunk * LANES, LAGS + (chunk + 1) * LANES)
-        totals = [jnp.zeros((SHOTS_HERE, LANES), F32) for _ in range(2 * FOCI)]
-        for r in range(RCV_HERE):
-            re = refl[chunk, r * SHOTS_HERE : (r + 1) * SHOTS_HERE, :]
-            im = refl[2 + chunk, r * SHOTS_HERE : (r + 1) * SHOTS_HERE, :]
+        for begin in range(0, SHOTS_HERE, half):
+            totals = [jnp.zeros((half, LANES), F32) for _ in range(3 * FOCI)]
+            for r in range(RCV_HERE):
+                lines = slice(r * SHOTS_HERE + begin, r * SHOTS_HERE + begin + half)
+                re = refl[chunk, lines, :]
+                im = refl[2 + chunk, lines, :]
+                both = re + im
+                for q in range(FOCI):
+                    line = q * RCV_HERE + r
+                    for kind, value in enumerate((both, re, im)):
+                        totals[3 * q + kind] += value * spectrum[kind, line : line + 1, lanes]
             for q in range(FOCI):
-                line = q * RCV_HERE + r
-                f_re = spectrum[line : line + 1, re_lanes]
-                f_im = spectrum[line : line + 1, im_lanes]
-                totals[2 * q] += re * f_re - im * f_im
-                totals[2 * q + 1] += re * f_im + im * f_re
-        for q in range(FOCI):
-            product[q * SHOTS_HERE : (q + 1) * SHOTS_HERE, re_lanes] = totals[2 * q]
-            product[q * SHOTS_HERE : (q + 1) * SHOTS_HERE, im_lanes] = totals[2 * q + 1]
+                first, second, third = totals[3 * q : 3 * q + 3]
+                lines = slice(q * SHOTS_HERE + begin, q * SHOTS_HERE + begin + half)
+                product[lines, lanes] = first - third
+                product[lines, im_lanes] = first + second
     scale = 1.0 / (LAGS * math.sqrt(RCV_HERE * RCV_AXIS * LAGS))
     result = to_traces(product[...], inv_high, inv_low, scale)
     for q in range(FOCI):
@@ -214,25 +226,26 @@
         ],
         axis=0,
     ).astype(BF16)
-    spectrum[...] = to_spectrum(traces, fwd_high, fwd_low)
+    for kind, part in enumerate(factors(to_spectrum(traces, fwd_high, fwd_low))):
+        spectrum[kind] = part
     for chunk in range(2):
-        re_lanes = slice(chunk * LANES, (chunk + 1) * LANES)
+        lanes = slice(chunk * LANES, (chunk + 1) * LANES)
         im_lanes = slice(LAGS + chunk * LANES, LAGS + (chunk + 1) * LANES)
         for r in range(RCV_HERE):
-            totals = [jnp.zeros((8, LANES), F32) for _ in range(2 * FOCI)]
+            totals = [jnp.zeros((8, LANES), F32) for _ in range(3 * FOCI)]
             for begin in range(0, SHOTS_HERE, 8):
                 re = refl[chunk, r * SHOTS_HERE + begin : r * SHOTS_HERE + begin + 8, :]
                 im = refl[2 + chunk, r * SHOTS_HERE + begin : r * SHOTS_HERE + begin + 8, :]
+                both = re - im
                 for q in range(FOCI):
                     lines = slice(q * SHOTS_HERE + begin, q * SHOTS_HERE + begin + 8)
-                    u_re = spectrum[lines, re_lanes]
-                    u_im = spectrum[lines, im_lanes]
-                    totals[2 * q] += re * u_re + im * u_im
-                    totals[2 * q + 1] += re * u_im - im * u_re
+                    for kind, value in enumerate((both, re, im)):
+                        totals[3 * q + kind] += value * spectrum[kind, lines, lanes]
             for q in range(FOCI):
                 line = q * RCV_HERE + r
-                product[line : line + 1, re_lanes] = jnp.sum(totals[2 * q], axis=0, keepdims=True)
-                product[line : line + 1, im_lanes] = jnp.sum(totals[2 * q + 1], axis=0, keepdims=True)
+                first, second, third = totals[3 * q : 3 * q + 3]
+                product[line : line + 1, lanes] = jnp.sum(first + third, axis=0, keepdims=True)
+                product[line : line + 1, im_lanes] = jnp.sum(first + second, axis=0, keepdims=True)
     scale = 1.0 / (LAGS * math.sqrt(SHOTS_HERE * SHOT_AXIS * LAGS))
     return to_traces(product[...], inv_high, inv_low, scale)
 
@@ -311,11 +324,16 @@
     shot_window = jnp.transpose(shot_window, (0, 2, 1))
     rcv_window = jnp.transpose(rcv_window, (0, 2, 1))
     traces = FOCI * RCV_HERE
-    fields = pltpu.VMEM((traces, 2 * LAGS), F32)
-    products = pltpu.VMEM((FOCI * SHOTS_HERE, 2 * LAGS), F32)
     rows = pltpu.VMEM((FOCI * HALVES * SHOTS_HERE, LANES), F32)
-    conv_scratch = [fields, products, rows]
-    corr_scratch = [rows, products, fields]
+
+    def spectra(count):
+        return pltpu.VMEM((3, count, LAGS), F32)
+
+    def products(count):
+        return pltpu.VMEM((count, 2 * LAGS), F32)
+
+    conv_scratch = [spectra(traces), products(FOCI * SHOTS_HERE), rows]
+    corr_scratch = [rows, spectra(FOCI * SHOTS_HERE), products(traces)]
     conv_out = ((PLANE, SHARE, LANES), F32)
     def in_hbm(*arrays):
         return [pltpu.with_memory_space_constraint(array, pltpu.HBM) for array in arrays]

time: 103 us -> 102 us (level)
  no operation moved by 1% of the time
where the time goes in v5:
time: 102 us
  blocking collectives  56.3 us (55%)
  starting transfers between devices  21.7 us (21%)
  waiting for transfers between devices  12.3 us (12%)
  Pallas kernels  10.6 us (10%)
    all_to_all x2, blocking collectives, on_device(): lax.all_to_all(partial, 'rcv', 0, 0, tiled=True, axis_index_groups=over_p...  23.1 us
    all_to_all x2, blocking collectives, on_device(): lax.all_to_all(rounded, 'rcv', 0, 0, tiled=True, axis_index_groups=over_p...  18.9 us
    all_to_all x1, blocking collectives, on_device(): parts = lax.all_to_all(partial, 'shot', 0, 0, tiled=True)  14.3 us
    pallas_call x13, Pallas kernels, call(): pl.pallas_call(kernel, name=name, in_specs=specs, out_specs=[VM] * len(ou...  10.6 us
    ppermute x2, starting transfers between devices, on_device(): lax.ppermute(mine, 'rcv', [(place, place ^ 4) for place in range(RCV_AXIS)])  8.81 us
    all_to_all x1, starting transfers between devices, on_device(): picked = lax.all_to_all(picks, 'shot', 0, 0, tiled=True)  7.41 us
    ppermute x3, waiting for transfers between devices, on_device(): lax.ppermute(mine, 'shot', [(place, place ^ step) for place in range(SHOT...  6.55 us
    ppermute x3, starting transfers between devices, on_device(): lax.ppermute(mine, 'shot', [(place, place ^ step) for place in range(SHOT...  5.52 us
  transfers between devices with their start and end apart: 6, of which 6 were waited for; matrix products, arithmetic and copies ran while one was open for 0% of the time, Pallas kernels for 4%

profile of v5, /device:TPU:1, one launch (start us, length us, event | category | flops | bytes accessed | tf_op | source)
XLA Modules:
  0.0 101.7 jit_solution(9805691219586563998)
XLA Ops:
  0.6 1.7 %pick.1 = bf16[8,32,256]{2,1,0:T(8,128)(2,1)} custom-call(s32[2]{0:T(128)} %focus_hbm.1, bf16[64,16,256]{2,1,0:T(8,128)(2,1)} %reflection_hbm.3), custom_call_target="tpu_custom_call" | custom-call | tf_op jit(solution)/shard_map/pick/pallas_call | solution.py:307
  2.4 7.4 %all-to-all-start = ((bf16[8,32,256]{2,1,0:T(8,128)(2,1)}), bf16[8,32,256]{2,1,0:T(8,128)(2,1)S(1)}, u32[]{:S(2)}, u32[]{:S(2)}) async-start(bf16[8,32,256]{2,1,0:T(8,128)(2,1)} %pick.1), calls=%async_computation | async-start | bytes 262144 | tf_op jit(solution)/shard_map/all_to_all | solution.py:349
  9.8 4.2 %preparation.1 = (f32[4,1024,128]{2,1,0:T(8,128)S(1)}, s32[16,128]{1,0:T(8,128)S(1)}, s32[32,256]{1,0:T(8,128)S(1)}, bf16[256,512]{1,0:T(8,128)(2,1)S(1)}, bf16[...) custom-call(s32[2,2,64]{2,1,0:T(2,128)} %bitcast.2, ...), custom_call_target="tpu_custom_call" | custom-call | tf_op jit(solution)/shard_map/preparation/pallas_call | solution.py:307
  14.0 1.6 %all-to-all-done.picked = bf16[8,32,256]{2,1,0:T(8,128)(2,1)S(1)} async-done(((bf16[8,32,256]{2,1,0:T(8,128)(2,1)}), bf16[8,32,256]{2,1,0:T(8,128)(2,1)S(1)}, u32[]{:S(2)}, u32[]{:S(2)}) %all-to-all-start) | async-done | bytes 131104 | tf_op jit(solution)/shard_map/all_to_all | solution.py:349
  15.6 1.1 %first_convolution.1 = (bf16[32,256]{1,0:T(8,128)(2,1)S(1)}, f32[16,16,128]{2,1,0:T(8,128)S(1)}) custom-call(bf16[8,32,256]{2,1,0:T(8,128)(2,1)S(1)} %all-to-all-done.picked, bf16[256,256]{1,0:T(8,128)(2,1)S(1)} %get-tuple-element.16.flip, f32[4,1024,128]{2,1,0:T(8,128)S(1)} %get-tuple-element.17.refl, bf16[256,512]{1,0:T(8,128)(2,1)S(1)} %get-tuple-element.18.fwd_high, ...), custom_call_target="tpu_custom_call" | custom-call | tf_op jit(solution)/shard_map/first_convolution/pallas_call | solution.py:307
  16.6 13.4 %all_to_all.30.parts = f32[16,16,128]{2,1,0:T(8,128)S(1)} all-to-all(f32[16,16,128]{2,1,0:T(8,128)S(1)} %get-tuple-element.22), channel_id=1, replica_groups={{0,1,2,3,8,9,10,11,16,17,18,19,24,25,26,27},{4,5,6,7,12,13,14,15,20,21,..., dimensions={0} | all-to-all | bytes 262144 | tf_op jit(solution)/shard_map/all_to_all | solution.py:375
  30.1 4.4 %collective-permute-start = (f32[16,128]{1,0:T(8,128)S(1)}, f32[16,128]{1,0:T(8,128)S(1)}, u32[]{:S(2)}, u32[]{:S(2)}) collective-permute-start(f32[16,128]{1,0:T(8,128)S(1)} %plane_sum.2.mine), channel_id=1, source_target_pairs={{0,4},{1,5},{2,6},{3,7},{4,0},{5,1},{6,2},{7,3},{8,12},{9,13},{10,... | collective-permute-start | bytes 24584 | tf_op jit(solution)/shard_map/ppermute | solution.py:377
  34.5 2.1 %collective-permute-done.other = f32[16,128]{1,0:T(8,128)S(1)} collective-permute-done((f32[16,128]{1,0:T(8,128)S(1)}, f32[16,128]{1,0:T(8,128)S(1)}, u32[]{:S(2)}, u32[]{:S(2)}) %collective-permute-start) | collective-permute-done | bytes 8224 | tf_op jit(solution)/shard_map/ppermute | solution.py:377
  36.6 9.6 %all_to_all.31.upgoing = bf16[16,16,128]{2,1,0:T(8,128)(2,1)S(1)} all-to-all(bf16[16,16,128]{2,1,0:T(8,128)(2,1)S(1)} %upgoing.1), channel_id=1, replica_groups={{0,1,2,3,8,9,10,11,16,17,18,19,24,25,26,27},{4,5,6,7,12,13,14,15,20,21,..., dimensions={0} | all-to-all | bytes 131072 | tf_op jit(solution)/shard_map/all_to_all | solution.py:385
  46.2 0.9 correlation.1.mine
  47.1 4.8 %collective-permute-start.1 = (f32[32,256]{1,0:T(8,128)S(1)}, f32[32,256]{1,0:T(8,128)S(1)}, u32[]{:S(2)}, u32[]{:S(2)}) collective-permute-start(f32[32,256]{1,0:T(8,128)S(1)} %correlation.1.mine), channel_id=1, source_target_pairs={{0,32},{32,0},{64,96},{96,64},{128,160},{160,128},{192,224},{224,1... | collective-permute-start | bytes 98312 | tf_op jit(solution)/shard_map/ppermute | solution.py:392
  51.9 0.9 collective-permute-done.1.other
  52.7 0.6 collective-permute-start.2
  53.4 2.1 %collective-permute-done.2.other = f32[32,256]{1,0:T(8,128)S(1)} collective-permute-done((f32[32,256]{1,0:T(8,128)S(1)}, f32[32,256]{1,0:T(8,128)S(1)}, u32[]{:S(2)}, u32[]{:S(2)}) %collective-permute-start.2) | collective-permute-done | bytes 32800 | tf_op jit(solution)/shard_map/ppermute | solution.py:392
  55.5 0.1 collective-permute-start.3
  55.6 3.6 %collective-permute-done.3.other = f32[32,256]{1,0:T(8,128)S(1)} collective-permute-done((f32[32,256]{1,0:T(8,128)S(1)}, f32[32,256]{1,0:T(8,128)S(1)}, u32[]{:S(2)}, u32[]{:S(2)}) %collective-permute-start.3) | collective-permute-done | bytes 32800 | tf_op jit(solution)/shard_map/ppermute | solution.py:392
  59.2 1.0 next_convolution.1
  60.1 9.7 %all_to_all.32.parts = f32[16,16,128]{2,1,0:T(8,128)S(1)} all-to-all(f32[16,16,128]{2,1,0:T(8,128)S(1)} %next_convolution.1), channel_id=1, replica_groups={{0,1,2,3,8,9,10,11,16,17,18,19,24,25,26,27},{4,5,6,7,12,13,14,15,20,21,..., dimensions={0} | all-to-all | bytes 262144 | tf_op jit(solution)/shard_map/all_to_all | solution.py:375
  69.8 4.4 %collective-permute-start.4 = (f32[16,128]{1,0:T(8,128)S(1)}, f32[16,128]{1,0:T(8,128)S(1)}, u32[]{:S(2)}, u32[]{:S(2)}) collective-permute-start(f32[16,128]{1,0:T(8,128)S(1)} %plane_sum.3.mine), channel_id=1, source_target_pairs={{0,4},{1,5},{2,6},{3,7},{4,0},{5,1},{6,2},{7,3},{8,12},{9,13},{10,... | collective-permute-start | bytes 24584 | tf_op jit(solution)/shard_map/ppermute | solution.py:377
  74.2 2.1 %collective-permute-done.4.other = f32[16,128]{1,0:T(8,128)S(1)} collective-permute-done((f32[16,128]{1,0:T(8,128)S(1)}, f32[16,128]{1,0:T(8,128)S(1)}, u32[]{:S(2)}, u32[]{:S(2)}) %collective-permute-start.4) | collective-permute-done | bytes 8224 | tf_op jit(solution)/shard_map/ppermute | solution.py:377
  76.4 9.3 %all_to_all.33.upgoing = bf16[16,16,128]{2,1,0:T(8,128)(2,1)S(1)} all-to-all(bf16[16,16,128]{2,1,0:T(8,128)(2,1)S(1)} %get-tuple-element.24), channel_id=1, replica_groups={{0,1,2,3,8,9,10,11,16,17,18,19,24,25,26,27},{4,5,6,7,12,13,14,15,20,21,..., dimensions={0} | all-to-all | bytes 131072 | tf_op jit(solution)/shard_map/all_to_all | solution.py:385
  85.7 1.0 last_correlation.1
  86.7 14.3 %all_to_all.34.parts = f32[8,8,128]{2,1,0:T(8,128)S(1)} all-to-all(f32[8,8,128]{2,1,0:T(8,128)S(1)} %last_correlation.1), channel_id=1, replica_groups=mesh['shot'=8,'rcv'=32] {'shot'}, dimensions={0} | all-to-all | bytes 65536 | tf_op jit(solution)/shard_map/all_to_all | solution.py:404
  101.0 0.7 downgoing.1
  (6 shorter events, 0.1 us)
Async XLA Ops:
  2.4 13.2 %all-to-all-start = ((bf16[8,32,256]{2,1,0:T(8,128)(2,1)}), bf16[8,32,256]{2,1,0:T(8,128)(2,1)S(1)}, u32[]{:S(2)}, u32[]{:S(2)}) async-start(bf16[8,32,256]{2,1,0:T(8,128)(2,1)} %pick.1), calls=%async_computation | async-start | bytes 262144 | tf_op jit(solution)/shard_map/all_to_all | solution.py:349
  30.1 6.5 %collective-permute-start = (f32[16,128]{1,0:T(8,128)S(1)}, f32[16,128]{1,0:T(8,128)S(1)}, u32[]{:S(2)}, u32[]{:S(2)}) collective-permute-start(f32[16,128]{1,0:T(8,128)S(1)} %plane_sum.2.mine), channel_id=1, source_target_pairs={{0,4},{1,5},{2,6},{3,7},{4,0},{5,1},{6,2},{7,3},{8,12},{9,13},{10,... | collective-permute-start | bytes 24584 | tf_op jit(solution)/shard_map/ppermute | solution.py:377
  47.1 5.6 %collective-permute-start.1 = (f32[32,256]{1,0:T(8,128)S(1)}, f32[32,256]{1,0:T(8,128)S(1)}, u32[]{:S(2)}, u32[]{:S(2)}) collective-permute-start(f32[32,256]{1,0:T(8,128)S(1)} %correlation.1.mine), channel_id=1, source_target_pairs={{0,32},{32,0},{64,96},{96,64},{128,160},{160,128},{192,224},{224,1... | collective-permute-start | bytes 98312 | tf_op jit(solution)/shard_map/ppermute | solution.py:392
  52.7 2.8 %collective-permute-start.2 = (f32[32,256]{1,0:T(8,128)S(1)}, f32[32,256]{1,0:T(8,128)S(1)}, u32[]{:S(2)}, u32[]{:S(2)}) collective-permute-start(f32[32,256]{1,0:T(8,128)S(1)} %pair_sum.2.mine), channel_id=1, source_target_pairs={{0,64},{32,96},{64,0},{96,32},{128,192},{160,224},{192,128},{224,1... | collective-permute-start | bytes 98312 | tf_op jit(solution)/shard_map/ppermute | solution.py:392
  55.5 3.7 %collective-permute-start.3 = (f32[32,256]{1,0:T(8,128)S(1)}, f32[32,256]{1,0:T(8,128)S(1)}, u32[]{:S(2)}, u32[]{:S(2)}) collective-permute-start(f32[32,256]{1,0:T(8,128)S(1)} %pair_sum.3.mine), channel_id=1, source_target_pairs={{0,128},{32,160},{64,192},{96,224},{128,0},{160,32},{192,64},{224,... | collective-permute-start | bytes 98312 | tf_op jit(solution)/shard_map/ppermute | solution.py:392
  69.8 6.5 %collective-permute-start.4 = (f32[16,128]{1,0:T(8,128)S(1)}, f32[16,128]{1,0:T(8,128)S(1)}, u32[]{:S(2)}, u32[]{:S(2)}) collective-permute-start(f32[16,128]{1,0:T(8,128)S(1)} %plane_sum.3.mine), channel_id=1, source_target_pairs={{0,4},{1,5},{2,6},{3,7},{4,0},{5,1},{6,2},{7,3},{8,12},{9,13},{10,... | collective-permute-start | bytes 24584 | tf_op jit(solution)/shard_map/ppermute | solution.py:377

commit v6 on v5

--- a/solution.py
+++ b/solution.py
@@ -22,6 +22,7 @@
 SHARE = SHOTS_HERE * FOCI * 2 // 16
 HALVES = LAGS // LANES
 PLANE = 16
+CHIPS = SHOT_AXIS // 2
 SHARE_LAGS = LAGS // SHOT_AXIS
 F32 = jnp.float32
 BF16 = jnp.bfloat16
@@ -84,14 +85,12 @@
         inside = jnp.logical_and(row >= 0, row < SHOTS_HERE)
         trace = reflection[jnp.clip(row, 0, SHOTS_HERE - 1)].astype(F32)
         picked = jnp.where(inside, trace, 0.0).astype(BF16)
-        for place in range(SHOT_AXIS):
-            out[place, which * RCV_HERE : (which + 1) * RCV_HERE, :] = picked
+        out[which * RCV_HERE : (which + 1) * RCV_HERE, :] = picked
 
 
 def prepare_kernel(
-    shot_hbm, rcv_hbm, reflection_hbm, high_hbm, low_hbm, inv_high_hbm, inv_low_hbm, flip_hbm,
-    out, shot_mask, rcv_mask, high, low, inv_high, inv_low, flip,
-    shot_window, rcv_window, reflection, onset, ending, sems,
+    reflection_hbm, high_hbm, low_hbm, inv_high_hbm, inv_low_hbm, flip_hbm,
+    out, high, low, inv_high, inv_low, flip, reflection, sems,
 ):
     def fetch(source, target, place):
         copy = pltpu.make_async_copy(source, target, sems.at[place])
@@ -104,8 +103,7 @@
         fetch(reflection_hbm.at[pl.ds(begin, step)], reflection.at[pl.ds(begin, step)], 2 + begin // step)
         for begin in range(0, SHOTS_HERE, step)
     ]
-    scalars = [fetch(shot_hbm, shot_window, 6), fetch(rcv_hbm, rcv_window, 7)]
-    later = [fetch(inv_high_hbm, inv_high, 8), fetch(inv_low_hbm, inv_low, 9), fetch(flip_hbm, flip, 10)]
+    later = [fetch(inv_high_hbm, inv_high, 6), fetch(inv_low_hbm, inv_low, 7), fetch(flip_hbm, flip, 8)]
     for copy in tables:
         copy.wait()
     for begin in range(0, SHOTS_HERE, step):
@@ -119,9 +117,18 @@
                 out[chunk, pl.ds(slot, RCV_HERE, SHOTS_HERE), :] = piece[
                     :, chunk * LANES : (chunk + 1) * LANES
                 ]
-    for copy in scalars:
+    for copy in later:
         copy.wait()
-    for copy in later:
+
+
+def mask_kernel(shot_hbm, rcv_hbm, shot_mask, rcv_mask, shot_window, rcv_window, onset, ending, sems):
+    copies = [
+        pltpu.make_async_copy(shot_hbm, shot_window, sems.at[0]),
+        pltpu.make_async_copy(rcv_hbm, rcv_window, sems.at[1]),
+    ]
+    for copy in copies:
+        copy.start()
+    for copy in copies:
         copy.wait()
     up_mask(shot_window, shot_mask)
     down_mask(rcv_window, rcv_mask, onset, ending)
@@ -190,13 +197,15 @@
         out[place] = rows[place * SHARE : (place + 1) * SHARE, :]
 
 
+def gather_kernel(mine, near, middle, far, flip, out):
+    total = (mine[...].astype(F32) + near[...].astype(F32)) + (middle[...].astype(F32) + far[...].astype(F32))
+    out[...] = dot(total.astype(BF16), flip[...]).astype(BF16)
+
+
 def first_kernel(
-    picked, flip, refl, fwd_high, fwd_low, inv_high, inv_low, start_out, out, spectrum, product, rows
+    mine, other, refl, fwd_high, fwd_low, inv_high, inv_low, start_out, out, spectrum, product, rows
 ):
-    start = picked[0].astype(F32)
-    for place in range(1, SHOT_AXIS):
-        start = start + picked[place].astype(F32)
-    start = dot(start.astype(BF16), flip[...]).astype(BF16)
+    start = (mine[...].astype(F32) + other[...].astype(F32)).astype(BF16)
     start_out[...] = start
     convolve_in(start, refl, fwd_high, fwd_low, inv_high, inv_low, out, spectrum, product, rows)
 
@@ -254,11 +263,29 @@
     out[...] = correlate_in(upgoing, refl, fwd_high, fwd_low, inv_high, inv_low, rows, spectrum, product)
 
 
-def last_correlate_kernel(upgoing, refl, fwd_high, fwd_low, inv_high, inv_low, out, rows, spectrum, product):
+def last_correlate_kernel(
+    upgoing, refl, fwd_high, fwd_low, inv_high, inv_low, keep, send, rows, spectrum, product
+):
     result = correlate_in(upgoing, refl, fwd_high, fwd_low, inv_high, inv_low, rows, spectrum, product)
+    pieces = []
     for place in range(SHOT_AXIS):
         piece = result[:, place * SHARE_LAGS : (place + 1) * SHARE_LAGS]
-        out[place] = jnp.concatenate([piece[begin : begin + 8] for begin in range(0, FOCI * RCV_HERE, 8)], axis=1)
+        pieces.append(
+            jnp.concatenate([piece[begin : begin + 8] for begin in range(0, FOCI * RCV_HERE, 8)], axis=1)
+        )
+    even = lax.rem(lax.axis_index("shot"), 2) == 0
+    for chip in range(CHIPS):
+        first, second = pieces[2 * chip : 2 * chip + 2]
+        keep[chip] = jnp.where(even, first, second)
+        send[chip] = jnp.where(even, second, first)
+
+
+def last_pair_kernel(mine, other, own, near, middle, far, total):
+    total[...] = mine[...] + other[...]
+    chip = lax.axis_index("shot") // 2
+    for step, out in enumerate((own, near, middle, far)):
+        place = lax.bitwise_xor(chip, step)
+        out[...] = total[place]
 
 
 def pair_kernel(mine, other, out):
@@ -273,18 +300,19 @@
 
 
 def next_kernel(
-    mask, mine, other, start, refl, fwd_high, fwd_low, inv_high, inv_low, out, spectrum, product, rows
+    mask, mine, far, middle, near, start, refl, fwd_high, fwd_low, inv_high, inv_low, out, spectrum, product, rows
 ):
-    down = start[...].astype(F32) + jnp.where(mask[...] != 0, mine[...] + other[...], 0.0)
+    total = (mine[...] + near[...]) + (far[...] + middle[...])
+    down = start[...].astype(F32) + jnp.where(mask[...] != 0, total, 0.0)
     convolve_in(down.astype(BF16), refl, fwd_high, fwd_low, inv_high, inv_low, out, spectrum, product, rows)
 
 
-def last_kernel(mask, parts, start, own, out, up_out):
+def last_kernel(mask, mine, near, middle, far, start, own, out, up_out):
     begin = lax.axis_index("shot") * SHARE_LAGS
     shift = lax.rem(LAGS - begin, LAGS)
     start_here = pltpu.roll(start[...].astype(F32), shift, 1)[:, :SHARE_LAGS]
     mask_here = pltpu.roll(mask[...], shift, 1)[:, :SHARE_LAGS]
-    total = total_of(parts)
+    total = (mine[...] + near[...]) + (far[...] + middle[...])
     total = jnp.concatenate([total[:, lane : lane + SHARE_LAGS] for lane in range(0, LANES, SHARE_LAGS)], axis=0)
     down = start_here + jnp.where(mask_here != 0, total, 0.0)
     for q in range(FOCI):
@@ -315,6 +343,10 @@
     )(*args)
 
 
+def over_shot(array, step):
+    return lax.ppermute(array, "shot", [(place, place ^ step) for place in range(SHOT_AXIS)])
+
+
 def over_plane():
     places = np.arange(RCV_AXIS).reshape(4, 2, 4)
     return places.transpose(1, 0, 2).reshape(2, 16).tolist()
@@ -339,37 +371,40 @@
         return [pltpu.with_memory_space_constraint(array, pltpu.HBM) for array in arrays]
 
     picks = call(
-        pick_kernel, "pick", [HB] * 2, [pltpu.VMEM((SHOT_AXIS, traces, LAGS), BF16)],
+        pick_kernel, "pick", [HB] * 2, [((traces, LAGS), BF16)],
         [
             pltpu.SMEM((FOCI,), jnp.int32), pltpu.VMEM((SHOTS_HERE, RCV_HERE, LAGS), BF16),
             pltpu.SemaphoreType.DMA((2,)),
         ],
         *in_hbm(focus_index, reflection),
     )
-    picked = lax.all_to_all(picks, "shot", 0, 0, tiled=True)
-    refl, shot_mask, rcv_mask, *waves, flip = call(
-        prepare_kernel, "preparation", [HB] * 8,
+    far, middle, near = [over_shot(picks, step) for step in (6, 4, 2)]
+    refl, *waves, flip = call(
+        prepare_kernel, "preparation", [HB] * 6,
         [
             ((4, RCV_HERE * SHOTS_HERE, LANES), F32),
-            ((SHARE, LANES), jnp.int32),
-            ((traces, LAGS), jnp.int32),
             ((LAGS, 2 * LAGS), BF16),
             ((LAGS, 2 * LAGS), BF16),
             ((2 * LAGS, LAGS), BF16),
             ((2 * LAGS, LAGS), BF16),
             ((LAGS, LAGS), BF16),
         ],
+        [pltpu.VMEM((SHOTS_HERE, RCV_HERE, LAGS), BF16), pltpu.SemaphoreType.DMA((9,))],
+        *in_hbm(reflection, *[jnp.asarray(table) for table in tables()]),
+    )
+    shot_mask, rcv_mask = call(
+        mask_kernel, "masks", [HB] * 2, [((SHARE, LANES), jnp.int32), ((traces, LAGS), jnp.int32)],
         [
             pltpu.SMEM((2, FOCI, SHOTS_HERE), jnp.int32), pltpu.SMEM((2, FOCI, RCV_HERE), jnp.int32),
-            pltpu.VMEM((SHOTS_HERE, RCV_HERE, LAGS), BF16),
             pltpu.VMEM((traces, LANES), jnp.int32), pltpu.VMEM((traces, LANES), jnp.int32),
-            pltpu.SemaphoreType.DMA((11,)),
+            pltpu.SemaphoreType.DMA((2,)),
         ],
-        *in_hbm(shot_window, rcv_window, reflection, *[jnp.asarray(table) for table in tables()]),
-    )
+        *in_hbm(shot_window, rcv_window),
+    )
+    picks = call(gather_kernel, "chip_picks", [VM] * 5, [((traces, LAGS), BF16)], [], picks, near, middle, far, flip)
     start, partial = call(
         first_kernel, "first_convolution", [VM] * 7, [((traces, LAGS), BF16), conv_out], conv_scratch,
-        picked, flip, refl, *waves,
+        picks, over_shot(picks, 1), refl, *waves,
     )
     for iteration in range(ITERS):
         parts = lax.all_to_all(partial, "rcv", 0, 0, tiled=True, axis_index_groups=over_plane())
@@ -388,23 +423,26 @@
                 correlate_kernel, "correlation", [VM] * 6, [((traces, LAGS), F32)], corr_scratch,
                 upgoing, refl, *waves,
             )
-            for step in (1, 2, 4):
-                other = lax.ppermute(mine, "shot", [(place, place ^ step) for place in range(SHOT_AXIS)])
-                if step < 4:
-                    mine = call(pair_kernel, "pair_sum", [VM] * 2, [((traces, LAGS), F32)], [], mine, other)
+            other = over_shot(mine, 1)
+            mine = call(pair_kernel, "pair_sum", [VM] * 2, [((traces, LAGS), F32)], [], mine, other)
+            others = [over_shot(mine, step) for step in (6, 4, 2)]
             partial = call(
-                next_kernel, "next_convolution", [VM] * 9, [conv_out], conv_scratch,
-                rcv_mask, mine, other, start, refl, *waves,
+                next_kernel, "next_convolution", [VM] * 11, [conv_out], conv_scratch,
+                rcv_mask, mine, *others, start, refl, *waves,
             )
         else:
-            partial = call(
-                last_correlate_kernel, "last_correlation", [VM] * 6, [((SHOT_AXIS, 8, LANES), F32)],
+            keep, send = call(
+                last_correlate_kernel, "last_correlation", [VM] * 6, [((CHIPS, 8, LANES), F32)] * 2,
                 corr_scratch, upgoing, refl, *waves,
             )
-            parts = lax.all_to_all(partial, "shot", 0, 0, tiled=True)
+            mine, near, middle, far = call(
+                last_pair_kernel, "last_pair_sum", [VM] * 2, [((8, LANES), F32)] * CHIPS,
+                [pltpu.VMEM((CHIPS, 8, LANES), F32)], keep, over_shot(send, 1),
+            )
+            parts = [mine] + [over_shot(part, step) for part, step in ((near, 2), (middle, 4), (far, 6))]
     focus_down, focus_up = call(
-        last_kernel, "downgoing", [VM] * 4, [((RCV_HERE, FOCI, SHARE_LAGS), F32), ((2, FOCI, LAGS), F32)], [],
-        rcv_mask, parts, start, own,
+        last_kernel, "downgoing", [VM] * 7, [((RCV_HERE, FOCI, SHARE_LAGS), F32), ((2, FOCI, LAGS), F32)], [],
+        rcv_mask, *parts, start, own,
     )
     return focus_down, focus_up
 

time: 102 us -> 98.7 us (0.968)
  blocking collectives: 56.3 us -> 41.5 us
  starting transfers between devices: 21.7 us -> 34.9 us
  waiting for transfers between devices: 12.3 us -> 10.5 us
    ppermute x3 -> x12, starting transfers between devices: 5.52 us -> 24.5 us  [over_shot(): lax.ppermute(array, 'shot', [(place, place ^ step) for place in range(SHO...]
    all_to_all x1 -> x0, blocking collectives: 14.3 us -> none  [on_device(): parts = lax.all_to_all(partial, 'shot', 0, 0, tiled=True)]
    all_to_all x1 -> x0, starting transfers between devices: 7.41 us -> none  [on_device(): picked = lax.all_to_all(picks, 'shot', 0, 0, tiled=True)]
    ppermute x2, waiting for transfers between devices: 4.19 us -> 2.44 us  [on_device(): lax.ppermute(mine, 'rcv', [(place, place ^ 4) for place in range(RCV_AXIS)])]
    ppermute x2, starting transfers between devices: 8.81 us -> 10.4 us  [on_device(): lax.ppermute(mine, 'rcv', [(place, place ^ 4) for place in range(RCV_AXIS)])]
    all_to_all x1 -> x0, waiting for transfers between devices: 1.57 us -> none  [on_device(): picked = lax.all_to_all(picks, 'shot', 0, 0, tiled=True)]
    ppermute x3 -> x12, waiting for transfers between devices: 6.55 us -> 8.1 us  [over_shot(): lax.ppermute(array, 'shot', [(place, place ^ step) for place in range(SHO...]
    pallas_call x13 -> x15, Pallas kernels: 10.6 us -> 10.7 us  [call(): pl.pallas_call(kernel, name=name, in_specs=specs, out_specs=[VM] * len(ou...]
  transfers between devices with their start and end apart: 6 -> 14, of which waited for: 6 -> 8; matrix products, arithmetic and copies ran while one was open for 0% -> 0% of each run, Pallas kernels for 4% -> 5%
where the time goes in v6:
time: 98.7 us; the launch traced here: 98.4 us
  blocking collectives  41.5 us (42%)
  starting transfers between devices  34.9 us (35%)
  Pallas kernels  10.7 us (11%)
  waiting for transfers between devices  10.5 us (11%)
    ppermute x12, starting transfers between devices, over_shot(): lax.ppermute(array, 'shot', [(place, place ^ step) for place in range(SHO...  24.5 us
    all_to_all x2, blocking collectives, on_device(): lax.all_to_all(partial, 'rcv', 0, 0, tiled=True, axis_index_groups=over_p...  22.3 us
    all_to_all x2, blocking collectives, on_device(): lax.all_to_all(rounded, 'rcv', 0, 0, tiled=True, axis_index_groups=over_p...  19.2 us
    pallas_call x15, Pallas kernels, call(): pl.pallas_call(kernel, name=name, in_specs=specs, out_specs=[VM] * len(ou...  10.7 us
    ppermute x2, starting transfers between devices, on_device(): lax.ppermute(mine, 'rcv', [(place, place ^ 4) for place in range(RCV_AXIS)])  10.4 us
    ppermute x12, waiting for transfers between devices, over_shot(): lax.ppermute(array, 'shot', [(place, place ^ step) for place in range(SHO...  8.1 us
    ppermute x2, waiting for transfers between devices, on_device(): lax.ppermute(mine, 'rcv', [(place, place ^ 4) for place in range(RCV_AXIS)])  2.44 us
  transfers between devices with their start and end apart: 14, of which 8 were waited for; matrix products, arithmetic and copies ran while one was open for 0% of the time, Pallas kernels for 5%

profile of v6, /device:TPU:1, one launch (start us, length us, event | category | flops | bytes accessed | tf_op | source)
XLA Modules:
  0.0 98.4 jit_solution(6886010080365839152)
XLA Ops:
  0.6 1.1 %pick.1.mine = bf16[32,256]{1,0:T(8,128)(2,1)S(1)} custom-call(s32[2]{0:T(128)} %focus_hbm.1, bf16[64,16,256]{2,1,0:T(8,128)(2,1)} %reflection_hbm.3), custom_call_target="tpu_custom_call" | custom-call | tf_op jit(solution)/shard_map/pick/pallas_call | solution.py:335
  1.7 5.3 %collective-permute-start.2 = (bf16[32,256]{1,0:T(8,128)(2,1)S(1)}, bf16[32,256]{1,0:T(8,128)(2,1)S(1)}, u32[]{:S(2)}, u32[]{:S(2)}) collective-permute-start(bf16[32,256]{1,0:T(8,128)(2,1)S(1)} %pick.1.mine), channel_id=1, source_target_pairs={{0,192},{32,224},{64,128},{96,160},{128,64},{160,96},{192,0},{224,... | collective-permute-start | bytes 49160 | tf_op jit(solution)/shard_map/ppermute | solution.py:347
  7.0 0.0 collective-permute-start.1
  7.0 0.4 collective-permute-start
  7.4 4.1 %preparation.1 = (f32[4,1024,128]{2,1,0:T(8,128)S(1)}, bf16[256,512]{1,0:T(8,128)(2,1)S(1)}, bf16[256,512]{1,0:T(8,128)(2,1)S(1)}, bf16[512,256]{1,0:T(8,128)(2,...) custom-call(bf16[64,16,256]{2,1,0:T(8,128)(2,1)} %reflection_hbm.3, ...), custom_call_target="tpu_custom_call" | custom-call | tf_op jit(solution)/shard_map/preparation/pallas_call | solution.py:335
  11.5 0.0 collective-permute-done.2.far
  11.5 0.0 collective-permute-done.1.middle
  11.5 0.0 collective-permute-done.near
  11.5 0.1 chip_picks.1.mine
  11.7 2.1 %collective-permute-start.3 = (bf16[32,256]{1,0:T(8,128)(2,1)S(1)}, bf16[32,256]{1,0:T(8,128)(2,1)S(1)}, u32[]{:S(2)}, u32[]{:S(2)}) collective-permute-start(bf16[32,256]{1,0:T(8,128)(2,1)S(1)} %chip_picks.1.mine), channel_id=1, source_target_pairs={{0,32},{32,0},{64,96},{96,64},{128,160},{160,128},{192,224},{224,1... | collective-permute-start | bytes 49160 | tf_op jit(solution)/shard_map/ppermute | solution.py:347
  13.8 0.8 collective-permute-done.3.other
  14.6 0.9 first_convolution.1
  15.5 12.6 %all_to_all.20.parts = f32[16,16,128]{2,1,0:T(8,128)S(1)} all-to-all(f32[16,16,128]{2,1,0:T(8,128)S(1)} %get-tuple-element.28), channel_id=1, replica_groups={{0,1,2,3,8,9,10,11,16,17,18,19,24,25,26,27},{4,5,6,7,12,13,14,15,20,21,..., dimensions={0} | all-to-all | bytes 262144 | tf_op jit(solution)/shard_map/all_to_all | solution.py:410
  28.1 6.1 %collective-permute-start.4 = (f32[16,128]{1,0:T(8,128)S(1)}, f32[16,128]{1,0:T(8,128)S(1)}, u32[]{:S(2)}, u32[]{:S(2)}) collective-permute-start(f32[16,128]{1,0:T(8,128)S(1)} %plane_sum.2.mine), channel_id=1, source_target_pairs={{0,4},{1,5},{2,6},{3,7},{4,0},{5,1},{6,2},{7,3},{8,12},{9,13},{10,... | collective-permute-start | bytes 24584 | tf_op jit(solution)/shard_map/ppermute | solution.py:412
  34.2 0.8 masks.1
  35.0 0.2 collective-permute-done.4.other
  35.3 9.6 %all_to_all.21.upgoing = bf16[16,16,128]{2,1,0:T(8,128)(2,1)S(1)} all-to-all(bf16[16,16,128]{2,1,0:T(8,128)(2,1)S(1)} %upgoing.1), channel_id=1, replica_groups={{0,1,2,3,8,9,10,11,16,17,18,19,24,25,26,27},{4,5,6,7,12,13,14,15,20,21,..., dimensions={0} | all-to-all | bytes 131072 | tf_op jit(solution)/shard_map/all_to_all | solution.py:420
  44.9 0.9 correlation.1.mine
  45.8 3.9 %collective-permute-start.5 = (f32[32,256]{1,0:T(8,128)S(1)}, f32[32,256]{1,0:T(8,128)S(1)}, u32[]{:S(2)}, u32[]{:S(2)}) collective-permute-start(f32[32,256]{1,0:T(8,128)S(1)} %correlation.1.mine), channel_id=1, source_target_pairs={{0,32},{32,0},{64,96},{96,64},{128,160},{160,128},{192,224},{224,1... | collective-permute-start | bytes 98312 | tf_op jit(solution)/shard_map/ppermute | solution.py:347
  49.7 0.9 collective-permute-done.5.other
  50.5 0.7 collective-permute-start.8
  51.2 2.6 %collective-permute-start.7 = (f32[32,256]{1,0:T(8,128)S(1)}, f32[32,256]{1,0:T(8,128)S(1)}, u32[]{:S(2)}, u32[]{:S(2)}) collective-permute-start(f32[32,256]{1,0:T(8,128)S(1)} %pair_sum.1.mine), channel_id=1, source_target_pairs={{0,128},{32,160},{64,192},{96,224},{128,0},{160,32},{192,64},{224,... | collective-permute-start | bytes 98312 | tf_op jit(solution)/shard_map/ppermute | solution.py:347
  53.9 0.2 collective-permute-start.6
  54.1 0.0 collective-permute-done.8.near
  54.1 1.4 %collective-permute-done.7.middle = f32[32,256]{1,0:T(8,128)S(1)} collective-permute-done((f32[32,256]{1,0:T(8,128)S(1)}, f32[32,256]{1,0:T(8,128)S(1)}, u32[]{:S(2)}, u32[]{:S(2)}) %collective-permute-start.7) | collective-permute-done | bytes 32800 | tf_op jit(solution)/shard_map/ppermute | solution.py:347
  55.4 3.0 %collective-permute-done.6.far = f32[32,256]{1,0:T(8,128)S(1)} collective-permute-done((f32[32,256]{1,0:T(8,128)S(1)}, f32[32,256]{1,0:T(8,128)S(1)}, u32[]{:S(2)}, u32[]{:S(2)}) %collective-permute-start.6) | collective-permute-done | bytes 32800 | tf_op jit(solution)/shard_map/ppermute | solution.py:347
  58.5 0.9 next_convolution.1
  59.4 9.7 %all_to_all.22.parts = f32[16,16,128]{2,1,0:T(8,128)S(1)} all-to-all(f32[16,16,128]{2,1,0:T(8,128)S(1)} %next_convolution.1), channel_id=1, replica_groups={{0,1,2,3,8,9,10,11,16,17,18,19,24,25,26,27},{4,5,6,7,12,13,14,15,20,21,..., dimensions={0} | all-to-all | bytes 262144 | tf_op jit(solution)/shard_map/all_to_all | solution.py:410
  69.1 4.3 %collective-permute-start.9 = (f32[16,128]{1,0:T(8,128)S(1)}, f32[16,128]{1,0:T(8,128)S(1)}, u32[]{:S(2)}, u32[]{:S(2)}) collective-permute-start(f32[16,128]{1,0:T(8,128)S(1)} %plane_sum.3.mine), channel_id=1, source_target_pairs={{0,4},{1,5},{2,6},{3,7},{4,0},{5,1},{6,2},{7,3},{8,12},{9,13},{10,... | collective-permute-start | bytes 24584 | tf_op jit(solution)/shard_map/ppermute | solution.py:412
  73.4 2.2 %collective-permute-done.9.other = f32[16,128]{1,0:T(8,128)S(1)} collective-permute-done((f32[16,128]{1,0:T(8,128)S(1)}, f32[16,128]{1,0:T(8,128)S(1)}, u32[]{:S(2)}, u32[]{:S(2)}) %collective-permute-start.9) | collective-permute-done | bytes 8224 | tf_op jit(solution)/shard_map/ppermute | solution.py:412
  75.6 9.6 %all_to_all.23.upgoing = bf16[16,16,128]{2,1,0:T(8,128)(2,1)S(1)} all-to-all(bf16[16,16,128]{2,1,0:T(8,128)(2,1)S(1)} %get-tuple-element.30), channel_id=1, replica_groups={{0,1,2,3,8,9,10,11,16,17,18,19,24,25,26,27},{4,5,6,7,12,13,14,15,20,21,..., dimensions={0} | all-to-all | bytes 131072 | tf_op jit(solution)/shard_map/all_to_all | solution.py:420
  85.2 1.0 last_correlation.1
  86.2 5.9 %collective-permute-start.10 = (f32[4,8,128]{2,1,0:T(8,128)S(1)}, f32[4,8,128]{2,1,0:T(8,128)S(1)}, u32[]{:S(2)}, u32[]{:S(2)}) collective-permute-start(f32[4,8,128]{2,1,0:T(8,128)S(1)} %get-tuple-element.32), channel_id=1, source_target_pairs={{0,32},{32,0},{64,96},{96,64},{128,160},{160,128},{192,224},{224,1... | collective-permute-start | bytes 49160 | tf_op jit(solution)/shard_map/ppermute | solution.py:347
  92.1 0.8 collective-permute-done.10.other
  92.9 0.0 collective-permute-start.11
  93.0 0.5 collective-permute-start.12
  93.4 3.1 %collective-permute-start.13 = (f32[8,128]{1,0:T(8,128)S(1)}, f32[8,128]{1,0:T(8,128)S(1)}, u32[]{:S(2)}, u32[]{:S(2)}) collective-permute-start(f32[8,128]{1,0:T(8,128)S(1)} %get-tuple-element.36), channel_id=1, source_target_pairs={{0,192},{32,224},{64,128},{96,160},{128,64},{160,96},{192,0},{224,... | collective-permute-start | bytes 12296 | tf_op jit(solution)/shard_map/ppermute | solution.py:347
  96.5 0.0 collective-permute-done.11.near
  96.5 0.0 collective-permute-done.12.middle
  96.5 1.2 %collective-permute-done.13.far = f32[8,128]{1,0:T(8,128)S(1)} collective-permute-done((f32[8,128]{1,0:T(8,128)S(1)}, f32[8,128]{1,0:T(8,128)S(1)}, u32[]{:S(2)}, u32[]{:S(2)}) %collective-permute-start.13) | collective-permute-done | bytes 4128 | tf_op jit(solution)/shard_map/ppermute | solution.py:347
  97.7 0.7 downgoing.1
  (6 shorter events, 0.1 us)
Async XLA Ops:
  1.7 9.8 %collective-permute-start.2 = (bf16[32,256]{1,0:T(8,128)(2,1)S(1)}, bf16[32,256]{1,0:T(8,128)(2,1)S(1)}, u32[]{:S(2)}, u32[]{:S(2)}) collective-permute-start(bf16[32,256]{1,0:T(8,128)(2,1)S(1)} %pick.1.mine), channel_id=1, source_target_pairs={{0,192},{32,224},{64,128},{96,160},{128,64},{160,96},{192,0},{224,... | collective-permute-start | bytes 49160 | tf_op jit(solution)/shard_map/ppermute | solution.py:347
  7.0 4.5 %collective-permute-start.1 = (bf16[32,256]{1,0:T(8,128)(2,1)S(1)}, bf16[32,256]{1,0:T(8,128)(2,1)S(1)}, u32[]{:S(2)}, u32[]{:S(2)}) collective-permute-start(bf16[32,256]{1,0:T(8,128)(2,1)S(1)} %pick.1.mine), channel_id=1, source_target_pairs={{0,128},{32,160},{64,192},{96,224},{128,0},{160,32},{192,64},{224,... | collective-permute-start | bytes 49160 | tf_op jit(solution)/shard_map/ppermute | solution.py:347
  7.0 4.6 %collective-permute-start = (bf16[32,256]{1,0:T(8,128)(2,1)S(1)}, bf16[32,256]{1,0:T(8,128)(2,1)S(1)}, u32[]{:S(2)}, u32[]{:S(2)}) collective-permute-start(bf16[32,256]{1,0:T(8,128)(2,1)S(1)} %pick.1.mine), channel_id=1, source_target_pairs={{0,64},{32,96},{64,0},{96,32},{128,192},{160,224},{192,128},{224,1... | collective-permute-start | bytes 49160 | tf_op jit(solution)/shard_map/ppermute | solution.py:347
  11.7 2.9 %collective-permute-start.3 = (bf16[32,256]{1,0:T(8,128)(2,1)S(1)}, bf16[32,256]{1,0:T(8,128)(2,1)S(1)}, u32[]{:S(2)}, u32[]{:S(2)}) collective-permute-start(bf16[32,256]{1,0:T(8,128)(2,1)S(1)} %chip_picks.1.mine), channel_id=1, source_target_pairs={{0,32},{32,0},{64,96},{96,64},{128,160},{160,128},{192,224},{224,1... | collective-permute-start | bytes 49160 | tf_op jit(solution)/shard_map/ppermute | solution.py:347
  28.1 7.1 %collective-permute-start.4 = (f32[16,128]{1,0:T(8,128)S(1)}, f32[16,128]{1,0:T(8,128)S(1)}, u32[]{:S(2)}, u32[]{:S(2)}) collective-permute-start(f32[16,128]{1,0:T(8,128)S(1)} %plane_sum.2.mine), channel_id=1, source_target_pairs={{0,4},{1,5},{2,6},{3,7},{4,0},{5,1},{6,2},{7,3},{8,12},{9,13},{10,... | collective-permute-start | bytes 24584 | tf_op jit(solution)/shard_map/ppermute | solution.py:412
  45.8 4.7 %collective-permute-start.5 = (f32[32,256]{1,0:T(8,128)S(1)}, f32[32,256]{1,0:T(8,128)S(1)}, u32[]{:S(2)}, u32[]{:S(2)}) collective-permute-start(f32[32,256]{1,0:T(8,128)S(1)} %correlation.1.mine), channel_id=1, source_target_pairs={{0,32},{32,0},{64,96},{96,64},{128,160},{160,128},{192,224},{224,1... | collective-permute-start | bytes 98312 | tf_op jit(solution)/shard_map/ppermute | solution.py:347
  50.5 3.6 %collective-permute-start.8 = (f32[32,256]{1,0:T(8,128)S(1)}, f32[32,256]{1,0:T(8,128)S(1)}, u32[]{:S(2)}, u32[]{:S(2)}) collective-permute-start(f32[32,256]{1,0:T(8,128)S(1)} %pair_sum.1.mine), channel_id=1, source_target_pairs={{0,64},{32,96},{64,0},{96,32},{128,192},{160,224},{192,128},{224,1... | collective-permute-start | bytes 98312 | tf_op jit(solution)/shard_map/ppermute | solution.py:347
  51.2 4.2 %collective-permute-start.7 = (f32[32,256]{1,0:T(8,128)S(1)}, f32[32,256]{1,0:T(8,128)S(1)}, u32[]{:S(2)}, u32[]{:S(2)}) collective-permute-start(f32[32,256]{1,0:T(8,128)S(1)} %pair_sum.1.mine), channel_id=1, source_target_pairs={{0,128},{32,160},{64,192},{96,224},{128,0},{160,32},{192,64},{224,... | collective-permute-start | bytes 98312 | tf_op jit(solution)/shard_map/ppermute | solution.py:347
  53.9 4.6 %collective-permute-start.6 = (f32[32,256]{1,0:T(8,128)S(1)}, f32[32,256]{1,0:T(8,128)S(1)}, u32[]{:S(2)}, u32[]{:S(2)}) collective-permute-start(f32[32,256]{1,0:T(8,128)S(1)} %pair_sum.1.mine), channel_id=1, source_target_pairs={{0,192},{32,224},{64,128},{96,160},{128,64},{160,96},{192,0},{224,... | collective-permute-start | bytes 98312 | tf_op jit(solution)/shard_map/ppermute | solution.py:347
  69.1 6.5 %collective-permute-start.9 = (f32[16,128]{1,0:T(8,128)S(1)}, f32[16,128]{1,0:T(8,128)S(1)}, u32[]{:S(2)}, u32[]{:S(2)}) collective-permute-start(f32[16,128]{1,0:T(8,128)S(1)} %plane_sum.3.mine), channel_id=1, source_target_pairs={{0,4},{1,5},{2,6},{3,7},{4,0},{5,1},{6,2},{7,3},{8,12},{9,13},{10,... | collective-permute-start | bytes 24584 | tf_op jit(solution)/shard_map/ppermute | solution.py:412
  86.2 6.7 %collective-permute-start.10 = (f32[4,8,128]{2,1,0:T(8,128)S(1)}, f32[4,8,128]{2,1,0:T(8,128)S(1)}, u32[]{:S(2)}, u32[]{:S(2)}) collective-permute-start(f32[4,8,128]{2,1,0:T(8,128)S(1)} %get-tuple-element.32), channel_id=1, source_target_pairs={{0,32},{32,0},{64,96},{96,64},{128,160},{160,128},{192,224},{224,1... | collective-permute-start | bytes 49160 | tf_op jit(solution)/shard_map/ppermute | solution.py:347
  92.9 3.6 %collective-permute-start.11 = (f32[8,128]{1,0:T(8,128)S(1)}, f32[8,128]{1,0:T(8,128)S(1)}, u32[]{:S(2)}, u32[]{:S(2)}) collective-permute-start(f32[8,128]{1,0:T(8,128)S(1)} %get-tuple-element.34), channel_id=1, source_target_pairs={{0,64},{32,96},{64,0},{96,32},{128,192},{160,224},{192,128},{224,1... | collective-permute-start | bytes 12296 | tf_op jit(solution)/shard_map/ppermute | solution.py:347
  93.0 3.5 %collective-permute-start.12 = (f32[8,128]{1,0:T(8,128)S(1)}, f32[8,128]{1,0:T(8,128)S(1)}, u32[]{:S(2)}, u32[]{:S(2)}) collective-permute-start(f32[8,128]{1,0:T(8,128)S(1)} %get-tuple-element.35), channel_id=1, source_target_pairs={{0,128},{32,160},{64,192},{96,224},{128,0},{160,32},{192,64},{224,... | collective-permute-start | bytes 12296 | tf_op jit(solution)/shard_map/ppermute | solution.py:347
  93.4 4.3 %collective-permute-start.13 = (f32[8,128]{1,0:T(8,128)S(1)}, f32[8,128]{1,0:T(8,128)S(1)}, u32[]{:S(2)}, u32[]{:S(2)}) collective-permute-start(f32[8,128]{1,0:T(8,128)S(1)} %get-tuple-element.36), channel_id=1, source_target_pairs={{0,192},{32,224},{64,128},{96,160},{128,64},{160,96},{192,0},{224,... | collective-permute-start | bytes 12296 | tf_op jit(solution)/shard_map/ppermute | solution.py:347

commit v7 on v6

--- a/solution.py
+++ b/solution.py
@@ -22,6 +22,7 @@
 SHARE = SHOTS_HERE * FOCI * 2 // 16
 HALVES = LAGS // LANES
 PLANE = 16
+HALF = SHOTS_HERE // 2
 CHIPS = SHOT_AXIS // 2
 SHARE_LAGS = LAGS // SHOT_AXIS
 F32 = jnp.float32
@@ -88,37 +89,43 @@
         out[which * RCV_HERE : (which + 1) * RCV_HERE, :] = picked
 
 
+def spectra_of(reflection, high, low, out):
+    step = 16
+    for begin in range(0, HALF, step):
+        spectrum = to_spectrum(reflection[begin : begin + step].reshape(step * RCV_HERE, LAGS), high, low)
+        for local in range(step):
+            piece = spectrum[local * RCV_HERE : (local + 1) * RCV_HERE]
+            slot = shot_slot(begin + local)
+            for chunk in range(4):
+                out[chunk, pl.ds(slot, RCV_HERE, HALF), :] = piece[:, chunk * LANES : (chunk + 1) * LANES]
+
+
 def prepare_kernel(
     reflection_hbm, high_hbm, low_hbm, inv_high_hbm, inv_low_hbm, flip_hbm,
-    out, high, low, inv_high, inv_low, flip, reflection, sems,
+    out, rest, high, low, inv_high, inv_low, flip, reflection, sems,
 ):
     def fetch(source, target, place):
         copy = pltpu.make_async_copy(source, target, sems.at[place])
         copy.start()
         return copy
 
-    step = 16
     tables = [fetch(high_hbm, high, 0), fetch(low_hbm, low, 1)]
-    blocks = [
-        fetch(reflection_hbm.at[pl.ds(begin, step)], reflection.at[pl.ds(begin, step)], 2 + begin // step)
-        for begin in range(0, SHOTS_HERE, step)
+    block = fetch(reflection_hbm.at[pl.ds(0, HALF)], reflection, 2)
+    later = [
+        fetch(reflection_hbm.at[pl.ds(HALF, HALF)], rest, 3),
+        fetch(inv_high_hbm, inv_high, 4),
+        fetch(inv_low_hbm, inv_low, 5),
+        fetch(flip_hbm, flip, 6),
     ]
-    later = [fetch(inv_high_hbm, inv_high, 6), fetch(inv_low_hbm, inv_low, 7), fetch(flip_hbm, flip, 8)]
-    for copy in tables:
+    for copy in tables + [block]:
         copy.wait()
-    for begin in range(0, SHOTS_HERE, step):
-        blocks[begin // step].wait()
-        lines = reflection[begin : begin + step].reshape(step * RCV_HERE, LAGS)
-        spectrum = to_spectrum(lines, high, low)
-        for local in range(step):
-            piece = spectrum[local * RCV_HERE : (local + 1) * RCV_HERE]
-            slot = shot_slot(begin + local)
-            for chunk in range(4):
-                out[chunk, pl.ds(slot, RCV_HERE, SHOTS_HERE), :] = piece[
-                    :, chunk * LANES : (chunk + 1) * LANES
-                ]
+    spectra_of(reflection, high, low, out)
     for copy in later:
         copy.wait()
+
+
+def rest_kernel(reflection, high, low, out):
+    spectra_of(reflection, high, low, out)
 
 
 def mask_kernel(shot_hbm, rcv_hbm, shot_mask, rcv_mask, shot_window, rcv_window, onset, ending, sems):
@@ -166,16 +173,16 @@
 def convolve_in(field, refl, fwd_high, fwd_low, inv_high, inv_low, out, spectrum, product, rows):
     for kind, part in enumerate(factors(to_spectrum(field, fwd_high, fwd_low))):
         spectrum[kind] = part
-    half = SHOTS_HERE // 2
     for chunk in range(2):
         lanes = slice(chunk * LANES, (chunk + 1) * LANES)
         im_lanes = slice(LAGS + chunk * LANES, LAGS + (chunk + 1) * LANES)
-        for begin in range(0, SHOTS_HERE, half):
-            totals = [jnp.zeros((half, LANES), F32) for _ in range(3 * FOCI)]
+        for begin in range(0, SHOTS_HERE, HALF):
+            totals = [jnp.zeros((HALF, LANES), F32) for _ in range(3 * FOCI)]
+            here = refl[begin // HALF]
             for r in range(RCV_HERE):
-                lines = slice(r * SHOTS_HERE + begin, r * SHOTS_HERE + begin + half)
-                re = refl[chunk, lines, :]
-                im = refl[2 + chunk, lines, :]
+                lines = slice(r * HALF, (r + 1) * HALF)
+                re = here[chunk, lines, :]
+                im = here[2 + chunk, lines, :]
                 both = re + im
                 for q in range(FOCI):
                     line = q * RCV_HERE + r
@@ -183,7 +190,7 @@
                         totals[3 * q + kind] += value * spectrum[kind, line : line + 1, lanes]
             for q in range(FOCI):
                 first, second, third = totals[3 * q : 3 * q + 3]
-                lines = slice(q * SHOTS_HERE + begin, q * SHOTS_HERE + begin + half)
+                lines = slice(q * SHOTS_HERE + begin, q * SHOTS_HERE + begin + HALF)
                 product[lines, lanes] = first - third
                 product[lines, im_lanes] = first + second
     scale = 1.0 / (LAGS * math.sqrt(RCV_HERE * RCV_AXIS * LAGS))
@@ -203,11 +210,11 @@
 
 
 def first_kernel(
-    mine, other, refl, fwd_high, fwd_low, inv_high, inv_low, start_out, out, spectrum, product, rows
+    mine, other, refl, refl_rest, fwd_high, fwd_low, inv_high, inv_low, start_out, out, spectrum, product, rows
 ):
     start = (mine[...].astype(F32) + other[...].astype(F32)).astype(BF16)
     start_out[...] = start
-    convolve_in(start, refl, fwd_high, fwd_low, inv_high, inv_low, out, spectrum, product, rows)
+    convolve_in(start, (refl, refl_rest), fwd_high, fwd_low, inv_high, inv_low, out, spectrum, product, rows)
 
 
 def sum_kernel(parts, out):
@@ -243,8 +250,10 @@
         for r in range(RCV_HERE):
             totals = [jnp.zeros((8, LANES), F32) for _ in range(3 * FOCI)]
             for begin in range(0, SHOTS_HERE, 8):
-                re = refl[chunk, r * SHOTS_HERE + begin : r * SHOTS_HERE + begin + 8, :]
-                im = refl[2 + chunk, r * SHOTS_HERE + begin : r * SHOTS_HERE + begin + 8, :]
+                here = refl[begin // HALF]
+                shots = slice(r * HALF + begin % HALF, r * HALF + begin % HALF + 8)
+                re = here[chunk, shots, :]
+                im = here[2 + chunk, shots, :]
                 both = re - im
                 for q in range(FOCI):
                     lines = slice(q * SHOTS_HERE + begin, q * SHOTS_HERE + begin + 8)
@@ -259,14 +268,14 @@
     return to_traces(product[...], inv_high, inv_low, scale)
 
 
-def correlate_kernel(upgoing, refl, fwd_high, fwd_low, inv_high, inv_low, out, rows, spectrum, product):
-    out[...] = correlate_in(upgoing, refl, fwd_high, fwd_low, inv_high, inv_low, rows, spectrum, product)
+def correlate_kernel(upgoing, refl, refl_rest, fwd_high, fwd_low, inv_high, inv_low, out, rows, spectrum, product):
+    out[...] = correlate_in(upgoing, (refl, refl_rest), fwd_high, fwd_low, inv_high, inv_low, rows, spectrum, product)
 
 
 def last_correlate_kernel(
-    upgoing, refl, fwd_high, fwd_low, inv_high, inv_low, keep, send, rows, spectrum, product
+    upgoing, refl, refl_rest, fwd_high, fwd_low, inv_high, inv_low, keep, send, rows, spectrum, product
 ):
-    result = correlate_in(upgoing, refl, fwd_high, fwd_low, inv_high, inv_low, rows, spectrum, product)
+    result = correlate_in(upgoing, (refl, refl_rest), fwd_high, fwd_low, inv_high, inv_low, rows, spectrum, product)
     pieces = []
     for place in range(SHOT_AXIS):
         piece = result[:, place * SHARE_LAGS : (place + 1) * SHARE_LAGS]
@@ -300,11 +309,12 @@
 
 
 def next_kernel(
-    mask, mine, far, middle, near, start, refl, fwd_high, fwd_low, inv_high, inv_low, out, spectrum, product, rows
+    mask, mine, far, middle, near, start, refl, refl_rest, fwd_high, fwd_low, inv_high, inv_low,
+    out, spectrum, product, rows,
 ):
     total = (mine[...] + near[...]) + (far[...] + middle[...])
     down = start[...].astype(F32) + jnp.where(mask[...] != 0, total, 0.0)
-    convolve_in(down.astype(BF16), refl, fwd_high, fwd_low, inv_high, inv_low, out, spectrum, product, rows)
+    convolve_in(down.astype(BF16), (refl, refl_rest), fwd_high, fwd_low, inv_high, inv_low, out, spectrum, product, rows)
 
 
 def last_kernel(mask, mine, near, middle, far, start, own, out, up_out):
@@ -379,19 +389,22 @@
         *in_hbm(focus_index, reflection),
     )
     far, middle, near = [over_shot(picks, step) for step in (6, 4, 2)]
-    refl, *waves, flip = call(
+    spectra_half = ((4, RCV_HERE * HALF, LANES), F32)
+    refl, rest, *waves, flip = call(
         prepare_kernel, "preparation", [HB] * 6,
         [
-            ((4, RCV_HERE * SHOTS_HERE, LANES), F32),
+            spectra_half,
+            ((HALF, RCV_HERE, LAGS), BF16),
             ((LAGS, 2 * LAGS), BF16),
             ((LAGS, 2 * LAGS), BF16),
             ((2 * LAGS, LAGS), BF16),
             ((2 * LAGS, LAGS), BF16),
             ((LAGS, LAGS), BF16),
         ],
-        [pltpu.VMEM((SHOTS_HERE, RCV_HERE, LAGS), BF16), pltpu.SemaphoreType.DMA((9,))],
+        [pltpu.VMEM((HALF, RCV_HERE, LAGS), BF16), pltpu.SemaphoreType.DMA((7,))],
         *in_hbm(reflection, *[jnp.asarray(table) for table in tables()]),
     )
+    refl_rest = call(rest_kernel, "rest_preparation", [VM] * 3, [spectra_half], [], rest, waves[0], waves[1])
     shot_mask, rcv_mask = call(
         mask_kernel, "masks", [HB] * 2, [((SHARE, LANES), jnp.int32), ((traces, LAGS), jnp.int32)],
         [
@@ -403,8 +416,8 @@
     )
     picks = call(gather_kernel, "chip_picks", [VM] * 5, [((traces, LAGS), BF16)], [], picks, near, middle, far, flip)
     start, partial = call(
-        first_kernel, "first_convolution", [VM] * 7, [((traces, LAGS), BF16), conv_out], conv_scratch,
-        picks, over_shot(picks, 1), refl, *waves,
+        first_kernel, "first_convolution", [VM] * 8, [((traces, LAGS), BF16), conv_out], conv_scratch,
+        picks, over_shot(picks, 1), refl, refl_rest, *waves,
     )
     for iteration in range(ITERS):
         parts = lax.all_to_all(partial, "rcv", 0, 0, tiled=True, axis_index_groups=over_plane())
@@ -420,20 +433,20 @@
         upgoing = lax.all_to_all(rounded, "rcv", 0, 0, tiled=True, axis_index_groups=over_plane())
         if iteration + 1 < ITERS:
             mine = call(
-                correlate_kernel, "correlation", [VM] * 6, [((traces, LAGS), F32)], corr_scratch,
-                upgoing, refl, *waves,
+                correlate_kernel, "correlation", [VM] * 7, [((traces, LAGS), F32)], corr_scratch,
+                upgoing, refl, refl_rest, *waves,
             )
             other = over_shot(mine, 1)
             mine = call(pair_kernel, "pair_sum", [VM] * 2, [((traces, LAGS), F32)], [], mine, other)
             others = [over_shot(mine, step) for step in (6, 4, 2)]
             partial = call(
-                next_kernel, "next_convolution", [VM] * 11, [conv_out], conv_scratch,
-                rcv_mask, mine, *others, start, refl, *waves,
+                next_kernel, "next_convolution", [VM] * 12, [conv_out], conv_scratch,
+                rcv_mask, mine, *others, start, refl, refl_rest, *waves,
             )
         else:
             keep, send = call(
-                last_correlate_kernel, "last_correlation", [VM] * 6, [((CHIPS, 8, LANES), F32)] * 2,
-                corr_scratch, upgoing, refl, *waves,
+                last_correlate_kernel, "last_correlation", [VM] * 7, [((CHIPS, 8, LANES), F32)] * 2,
+                corr_scratch, upgoing, refl, refl_rest, *waves,
             )
             mine, near, middle, far = call(
                 last_pair_kernel, "last_pair_sum", [VM] * 2, [((8, LANES), F32)] * CHIPS,

time: 98.7 us -> 98.2 us (level)
  starting transfers between devices: 34.9 us -> 33.2 us
    ppermute x2, starting transfers between devices: 10.4 us -> 8.91 us  [on_device(): lax.ppermute(mine, 'rcv', [(place, place ^ 4) for place in range(RCV_AXIS)])]
    all_to_all x2, blocking collectives: 22.3 us -> 23.4 us  [on_device(): lax.all_to_all(partial, 'rcv', 0, 0, tiled=True, axis_index_groups=over_p...]
    pallas_call x15 -> x16, Pallas kernels: 10.7 us -> 10.3 us  [call(): pl.pallas_call(kernel, name=name, in_specs=specs, out_specs=[VM] * len(ou...]
where the time goes in v7:
time: 98.2 us; the launch traced here: 97.9 us
  blocking collectives  42.3 us (43%)
  starting transfers between devices  33.2 us (34%)
  waiting for transfers between devices  11.4 us (12%)
  Pallas kernels  10.3 us (10%)
    ppermute x12, starting transfers between devices, over_shot(): lax.ppermute(array, 'shot', [(place, place ^ step) for place in range(SHO...  24.3 us
    all_to_all x2, blocking collectives, on_device(): lax.all_to_all(partial, 'rcv', 0, 0, tiled=True, axis_index_groups=over_p...  23.4 us
    all_to_all x2, blocking collectives, on_device(): lax.all_to_all(rounded, 'rcv', 0, 0, tiled=True, axis_index_groups=over_p...  18.9 us
    pallas_call x16, Pallas kernels, call(): pl.pallas_call(kernel, name=name, in_specs=specs, out_specs=[VM] * len(ou...  10.3 us
    ppermute x2, starting transfers between devices, on_device(): lax.ppermute(mine, 'rcv', [(place, place ^ 4) for place in range(RCV_AXIS)])  8.91 us
    ppermute x12, waiting for transfers between devices, over_shot(): lax.ppermute(array, 'shot', [(place, place ^ step) for place in range(SHO...  8.08 us
    ppermute x2, waiting for transfers between devices, on_device(): lax.ppermute(mine, 'rcv', [(place, place ^ 4) for place in range(RCV_AXIS)])  3.28 us
  transfers between devices with their start and end apart: 14, of which 8 were waited for; matrix products, arithmetic and copies ran while one was open for 0% of the time, Pallas kernels for 5%

profile of v7, /device:TPU:1, one launch (start us, length us, event | category | flops | bytes accessed | tf_op | source)
XLA Modules:
  0.0 97.9 jit_solution(1162007886814921162)
XLA Ops:
  0.6 1.1 %pick.1.mine = bf16[32,256]{1,0:T(8,128)(2,1)S(1)} custom-call(s32[2]{0:T(128)} %focus_hbm.1, bf16[64,16,256]{2,1,0:T(8,128)(2,1)} %reflection_hbm.3), custom_call_target="tpu_custom_call" | custom-call | tf_op jit(solution)/shard_map/pick/pallas_call | solution.py:345
  1.7 5.3 %collective-permute-start.2 = (bf16[32,256]{1,0:T(8,128)(2,1)S(1)}, bf16[32,256]{1,0:T(8,128)(2,1)S(1)}, u32[]{:S(2)}, u32[]{:S(2)}) collective-permute-start(bf16[32,256]{1,0:T(8,128)(2,1)S(1)} %pick.1.mine), channel_id=1, source_target_pairs={{0,192},{32,224},{64,128},{96,160},{128,64},{160,96},{192,0},{224,... | collective-permute-start | bytes 49160 | tf_op jit(solution)/shard_map/ppermute | solution.py:357
  7.0 0.0 collective-permute-start.1
  7.0 0.4 collective-permute-start
  7.4 2.4 %preparation.1 = (f32[4,512,128]{2,1,0:T(8,128)S(1)}, bf16[32,16,256]{2,1,0:T(8,128)(2,1)S(1)}, bf16[256,512]{1,0:T(8,128)(2,1)S(1)}, bf16[256,512]{1,0:T(8,128)...) custom-call(bf16[64,16,256]{2,1,0:T(8,128)(2,1)} %reflection_hbm.3, ...), custom_call_target="tpu_custom_call" | custom-call | tf_op jit(solution)/shard_map/preparation/pallas_call | solution.py:345
  9.8 0.0 collective-permute-done.2.far
  9.8 0.8 collective-permute-done.1.middle
  10.6 0.0 collective-permute-done.near
  10.6 0.1 chip_picks.1.mine
  10.8 1.9 %collective-permute-start.3 = (bf16[32,256]{1,0:T(8,128)(2,1)S(1)}, bf16[32,256]{1,0:T(8,128)(2,1)S(1)}, u32[]{:S(2)}, u32[]{:S(2)}) collective-permute-start(bf16[32,256]{1,0:T(8,128)(2,1)S(1)} %chip_picks.1.mine), channel_id=1, source_target_pairs={{0,32},{32,0},{64,96},{96,64},{128,160},{160,128},{192,224},{224,1... | collective-permute-start | bytes 49160 | tf_op jit(solution)/shard_map/ppermute | solution.py:357
  12.7 1.3 %rest_preparation.1.refl_rest = f32[4,512,128]{2,1,0:T(8,128)S(1)} custom-call(bf16[32,16,256]{2,1,0:T(8,128)(2,1)S(1)} %get-tuple-element.25.reflection, bf16[256,512]{1,0:T(8,128)(2,1)S(1)} %get-tuple-element.26.high.fwd_high, bf16[256,512]{1,0:T(8,128)(2,1)S(1)} %get-tuple-element.27.low.fwd_low), custom_call_target="tpu_custom_call" | custom-call | tf_op jit(solution)/shard_map/rest_preparation/pallas_call | solution.py:345
  14.0 0.0 collective-permute-done.3.other
  14.0 1.0 first_convolution.1
  15.0 13.7 %all_to_all.20.parts = f32[16,16,128]{2,1,0:T(8,128)S(1)} all-to-all(f32[16,16,128]{2,1,0:T(8,128)S(1)} %get-tuple-element.30), channel_id=1, replica_groups={{0,1,2,3,8,9,10,11,16,17,18,19,24,25,26,27},{4,5,6,7,12,13,14,15,20,21,..., dimensions={0} | all-to-all | bytes 262144 | tf_op jit(solution)/shard_map/all_to_all | solution.py:423
  28.7 4.6 %collective-permute-start.4 = (f32[16,128]{1,0:T(8,128)S(1)}, f32[16,128]{1,0:T(8,128)S(1)}, u32[]{:S(2)}, u32[]{:S(2)}) collective-permute-start(f32[16,128]{1,0:T(8,128)S(1)} %plane_sum.2.mine), channel_id=1, source_target_pairs={{0,4},{1,5},{2,6},{3,7},{4,0},{5,1},{6,2},{7,3},{8,12},{9,13},{10,... | collective-permute-start | bytes 24584 | tf_op jit(solution)/shard_map/ppermute | solution.py:425
  33.3 0.8 masks.1
  34.1 1.1 %collective-permute-done.4.other = f32[16,128]{1,0:T(8,128)S(1)} collective-permute-done((f32[16,128]{1,0:T(8,128)S(1)}, f32[16,128]{1,0:T(8,128)S(1)}, u32[]{:S(2)}, u32[]{:S(2)}) %collective-permute-start.4) | collective-permute-done | bytes 8224 | tf_op jit(solution)/shard_map/ppermute | solution.py:425
  35.2 9.3 %all_to_all.21.upgoing = bf16[16,16,128]{2,1,0:T(8,128)(2,1)S(1)} all-to-all(bf16[16,16,128]{2,1,0:T(8,128)(2,1)S(1)} %upgoing.1), channel_id=1, replica_groups={{0,1,2,3,8,9,10,11,16,17,18,19,24,25,26,27},{4,5,6,7,12,13,14,15,20,21,..., dimensions={0} | all-to-all | bytes 131072 | tf_op jit(solution)/shard_map/all_to_all | solution.py:433
  44.5 0.9 correlation.1.mine
  45.4 3.8 %collective-permute-start.5 = (f32[32,256]{1,0:T(8,128)S(1)}, f32[32,256]{1,0:T(8,128)S(1)}, u32[]{:S(2)}, u32[]{:S(2)}) collective-permute-start(f32[32,256]{1,0:T(8,128)S(1)} %correlation.1.mine), channel_id=1, source_target_pairs={{0,32},{32,0},{64,96},{96,64},{128,160},{160,128},{192,224},{224,1... | collective-permute-start | bytes 98312 | tf_op jit(solution)/shard_map/ppermute | solution.py:357
  49.2 0.9 collective-permute-done.5.other
  50.1 0.0 collective-permute-start.8
  50.1 2.2 %collective-permute-start.7 = (f32[32,256]{1,0:T(8,128)S(1)}, f32[32,256]{1,0:T(8,128)S(1)}, u32[]{:S(2)}, u32[]{:S(2)}) collective-permute-start(f32[32,256]{1,0:T(8,128)S(1)} %pair_sum.1.mine), channel_id=1, source_target_pairs={{0,128},{32,160},{64,192},{96,224},{128,0},{160,32},{192,64},{224,... | collective-permute-start | bytes 98312 | tf_op jit(solution)/shard_map/ppermute | solution.py:357
  52.3 1.3 %collective-permute-start.6 = (f32[32,256]{1,0:T(8,128)S(1)}, f32[32,256]{1,0:T(8,128)S(1)}, u32[]{:S(2)}, u32[]{:S(2)}) collective-permute-start(f32[32,256]{1,0:T(8,128)S(1)} %pair_sum.1.mine), channel_id=1, source_target_pairs={{0,192},{32,224},{64,128},{96,160},{128,64},{160,96},{192,0},{224,... | collective-permute-start | bytes 98312 | tf_op jit(solution)/shard_map/ppermute | solution.py:357
  53.6 0.0 collective-permute-done.8.near
  53.6 0.3 collective-permute-done.7.middle
  53.9 2.9 %collective-permute-done.6.far = f32[32,256]{1,0:T(8,128)S(1)} collective-permute-done((f32[32,256]{1,0:T(8,128)S(1)}, f32[32,256]{1,0:T(8,128)S(1)}, u32[]{:S(2)}, u32[]{:S(2)}) %collective-permute-start.6) | collective-permute-done | bytes 32800 | tf_op jit(solution)/shard_map/ppermute | solution.py:357
  56.9 0.9 next_convolution.1
  57.8 9.7 %all_to_all.22.parts = f32[16,16,128]{2,1,0:T(8,128)S(1)} all-to-all(f32[16,16,128]{2,1,0:T(8,128)S(1)} %next_convolution.1), channel_id=1, replica_groups={{0,1,2,3,8,9,10,11,16,17,18,19,24,25,26,27},{4,5,6,7,12,13,14,15,20,21,..., dimensions={0} | all-to-all | bytes 262144 | tf_op jit(solution)/shard_map/all_to_all | solution.py:423
  67.5 4.3 %collective-permute-start.9 = (f32[16,128]{1,0:T(8,128)S(1)}, f32[16,128]{1,0:T(8,128)S(1)}, u32[]{:S(2)}, u32[]{:S(2)}) collective-permute-start(f32[16,128]{1,0:T(8,128)S(1)} %plane_sum.3.mine), channel_id=1, source_target_pairs={{0,4},{1,5},{2,6},{3,7},{4,0},{5,1},{6,2},{7,3},{8,12},{9,13},{10,... | collective-permute-start | bytes 24584 | tf_op jit(solution)/shard_map/ppermute | solution.py:425
  71.8 2.2 %collective-permute-done.9.other = f32[16,128]{1,0:T(8,128)S(1)} collective-permute-done((f32[16,128]{1,0:T(8,128)S(1)}, f32[16,128]{1,0:T(8,128)S(1)}, u32[]{:S(2)}, u32[]{:S(2)}) %collective-permute-start.9) | collective-permute-done | bytes 8224 | tf_op jit(solution)/shard_map/ppermute | solution.py:425
  74.0 9.6 %all_to_all.23.upgoing = bf16[16,16,128]{2,1,0:T(8,128)(2,1)S(1)} all-to-all(bf16[16,16,128]{2,1,0:T(8,128)(2,1)S(1)} %get-tuple-element.32), channel_id=1, replica_groups={{0,1,2,3,8,9,10,11,16,17,18,19,24,25,26,27},{4,5,6,7,12,13,14,15,20,21,..., dimensions={0} | all-to-all | bytes 131072 | tf_op jit(solution)/shard_map/all_to_all | solution.py:433
  83.7 1.0 %last_correlation.1 = (f32[4,8,128]{2,1,0:T(8,128)S(1)}, f32[4,8,128]{2,1,0:T(8,128)S(1)}) custom-call(bf16[16,16,128]{2,1,0:T(8,128)(2,1)S(1)} %all_to_all.23.upgoing, f32[4,512,128]{2,1,0:T(8,128)S(1)} %get-tuple-element.24.refl, f32[4,512,128]{2,1,0:T(8,128)S(1)} %rest_preparation.1.refl_rest, bf16[256,512]{1,0:T(8,128)(2,1)S(1)} %get-tuple-element.26.high.fwd_high, ...), custom_call_target="tpu_custom_call" | custom-call | tf_op jit(solution)/shard_map/last_correlation/pallas_call | solution.py:345
  84.6 5.9 %collective-permute-start.10 = (f32[4,8,128]{2,1,0:T(8,128)S(1)}, f32[4,8,128]{2,1,0:T(8,128)S(1)}, u32[]{:S(2)}, u32[]{:S(2)}) collective-permute-start(f32[4,8,128]{2,1,0:T(8,128)S(1)} %get-tuple-element.34), channel_id=1, source_target_pairs={{0,32},{32,0},{64,96},{96,64},{128,160},{160,128},{192,224},{224,1... | collective-permute-start | bytes 49160 | tf_op jit(solution)/shard_map/ppermute | solution.py:357
  90.5 0.8 collective-permute-done.10.other
  91.3 0.0 collective-permute-start.11
  91.4 1.6 %collective-permute-start.12 = (f32[8,128]{1,0:T(8,128)S(1)}, f32[8,128]{1,0:T(8,128)S(1)}, u32[]{:S(2)}, u32[]{:S(2)}) collective-permute-start(f32[8,128]{1,0:T(8,128)S(1)} %get-tuple-element.37), channel_id=1, source_target_pairs={{0,128},{32,160},{64,192},{96,224},{128,0},{160,32},{192,64},{224,... | collective-permute-start | bytes 12296 | tf_op jit(solution)/shard_map/ppermute | solution.py:357
  92.9 2.0 %collective-permute-start.13 = (f32[8,128]{1,0:T(8,128)S(1)}, f32[8,128]{1,0:T(8,128)S(1)}, u32[]{:S(2)}, u32[]{:S(2)}) collective-permute-start(f32[8,128]{1,0:T(8,128)S(1)} %get-tuple-element.38), channel_id=1, source_target_pairs={{0,192},{32,224},{64,128},{96,160},{128,64},{160,96},{192,0},{224,... | collective-permute-start | bytes 12296 | tf_op jit(solution)/shard_map/ppermute | solution.py:357
  94.9 0.0 collective-permute-done.11.near
  94.9 0.0 collective-permute-done.12.middle
  94.9 2.3 %collective-permute-done.13.far = f32[8,128]{1,0:T(8,128)S(1)} collective-permute-done((f32[8,128]{1,0:T(8,128)S(1)}, f32[8,128]{1,0:T(8,128)S(1)}, u32[]{:S(2)}, u32[]{:S(2)}) %collective-permute-start.13) | collective-permute-done | bytes 4128 | tf_op jit(solution)/shard_map/ppermute | solution.py:357
  97.2 0.7 downgoing.1
  (6 shorter events, 0.1 us)
Async XLA Ops:
  1.7 8.1 %collective-permute-start.2 = (bf16[32,256]{1,0:T(8,128)(2,1)S(1)}, bf16[32,256]{1,0:T(8,128)(2,1)S(1)}, u32[]{:S(2)}, u32[]{:S(2)}) collective-permute-start(bf16[32,256]{1,0:T(8,128)(2,1)S(1)} %pick.1.mine), channel_id=1, source_target_pairs={{0,192},{32,224},{64,128},{96,160},{128,64},{160,96},{192,0},{224,... | collective-permute-start | bytes 49160 | tf_op jit(solution)/shard_map/ppermute | solution.py:357
  7.0 3.7 %collective-permute-start.1 = (bf16[32,256]{1,0:T(8,128)(2,1)S(1)}, bf16[32,256]{1,0:T(8,128)(2,1)S(1)}, u32[]{:S(2)}, u32[]{:S(2)}) collective-permute-start(bf16[32,256]{1,0:T(8,128)(2,1)S(1)} %pick.1.mine), channel_id=1, source_target_pairs={{0,128},{32,160},{64,192},{96,224},{128,0},{160,32},{192,64},{224,... | collective-permute-start | bytes 49160 | tf_op jit(solution)/shard_map/ppermute | solution.py:357
  7.0 3.7 %collective-permute-start = (bf16[32,256]{1,0:T(8,128)(2,1)S(1)}, bf16[32,256]{1,0:T(8,128)(2,1)S(1)}, u32[]{:S(2)}, u32[]{:S(2)}) collective-permute-start(bf16[32,256]{1,0:T(8,128)(2,1)S(1)} %pick.1.mine), channel_id=1, source_target_pairs={{0,64},{32,96},{64,0},{96,32},{128,192},{160,224},{192,128},{224,1... | collective-permute-start | bytes 49160 | tf_op jit(solution)/shard_map/ppermute | solution.py:357
  10.8 3.2 %collective-permute-start.3 = (bf16[32,256]{1,0:T(8,128)(2,1)S(1)}, bf16[32,256]{1,0:T(8,128)(2,1)S(1)}, u32[]{:S(2)}, u32[]{:S(2)}) collective-permute-start(bf16[32,256]{1,0:T(8,128)(2,1)S(1)} %chip_picks.1.mine), channel_id=1, source_target_pairs={{0,32},{32,0},{64,96},{96,64},{128,160},{160,128},{192,224},{224,1... | collective-permute-start | bytes 49160 | tf_op jit(solution)/shard_map/ppermute | solution.py:357
  28.7 6.5 %collective-permute-start.4 = (f32[16,128]{1,0:T(8,128)S(1)}, f32[16,128]{1,0:T(8,128)S(1)}, u32[]{:S(2)}, u32[]{:S(2)}) collective-permute-start(f32[16,128]{1,0:T(8,128)S(1)} %plane_sum.2.mine), channel_id=1, source_target_pairs={{0,4},{1,5},{2,6},{3,7},{4,0},{5,1},{6,2},{7,3},{8,12},{9,13},{10,... | collective-permute-start | bytes 24584 | tf_op jit(solution)/shard_map/ppermute | solution.py:425
  45.4 4.7 %collective-permute-start.5 = (f32[32,256]{1,0:T(8,128)S(1)}, f32[32,256]{1,0:T(8,128)S(1)}, u32[]{:S(2)}, u32[]{:S(2)}) collective-permute-start(f32[32,256]{1,0:T(8,128)S(1)} %correlation.1.mine), channel_id=1, source_target_pairs={{0,32},{32,0},{64,96},{96,64},{128,160},{160,128},{192,224},{224,1... | collective-permute-start | bytes 98312 | tf_op jit(solution)/shard_map/ppermute | solution.py:357
  50.1 3.6 %collective-permute-start.8 = (f32[32,256]{1,0:T(8,128)S(1)}, f32[32,256]{1,0:T(8,128)S(1)}, u32[]{:S(2)}, u32[]{:S(2)}) collective-permute-start(f32[32,256]{1,0:T(8,128)S(1)} %pair_sum.1.mine), channel_id=1, source_target_pairs={{0,64},{32,96},{64,0},{96,32},{128,192},{160,224},{192,128},{224,1... | collective-permute-start | bytes 98312 | tf_op jit(solution)/shard_map/ppermute | solution.py:357
  50.1 3.9 %collective-permute-start.7 = (f32[32,256]{1,0:T(8,128)S(1)}, f32[32,256]{1,0:T(8,128)S(1)}, u32[]{:S(2)}, u32[]{:S(2)}) collective-permute-start(f32[32,256]{1,0:T(8,128)S(1)} %pair_sum.1.mine), channel_id=1, source_target_pairs={{0,128},{32,160},{64,192},{96,224},{128,0},{160,32},{192,64},{224,... | collective-permute-start | bytes 98312 | tf_op jit(solution)/shard_map/ppermute | solution.py:357
  52.3 4.6 %collective-permute-start.6 = (f32[32,256]{1,0:T(8,128)S(1)}, f32[32,256]{1,0:T(8,128)S(1)}, u32[]{:S(2)}, u32[]{:S(2)}) collective-permute-start(f32[32,256]{1,0:T(8,128)S(1)} %pair_sum.1.mine), channel_id=1, source_target_pairs={{0,192},{32,224},{64,128},{96,160},{128,64},{160,96},{192,0},{224,... | collective-permute-start | bytes 98312 | tf_op jit(solution)/shard_map/ppermute | solution.py:357
  67.5 6.5 %collective-permute-start.9 = (f32[16,128]{1,0:T(8,128)S(1)}, f32[16,128]{1,0:T(8,128)S(1)}, u32[]{:S(2)}, u32[]{:S(2)}) collective-permute-start(f32[16,128]{1,0:T(8,128)S(1)} %plane_sum.3.mine), channel_id=1, source_target_pairs={{0,4},{1,5},{2,6},{3,7},{4,0},{5,1},{6,2},{7,3},{8,12},{9,13},{10,... | collective-permute-start | bytes 24584 | tf_op jit(solution)/shard_map/ppermute | solution.py:425
  84.6 6.7 %collective-permute-start.10 = (f32[4,8,128]{2,1,0:T(8,128)S(1)}, f32[4,8,128]{2,1,0:T(8,128)S(1)}, u32[]{:S(2)}, u32[]{:S(2)}) collective-permute-start(f32[4,8,128]{2,1,0:T(8,128)S(1)} %get-tuple-element.34), channel_id=1, source_target_pairs={{0,32},{32,0},{64,96},{96,64},{128,160},{160,128},{192,224},{224,1... | collective-permute-start | bytes 49160 | tf_op jit(solution)/shard_map/ppermute | solution.py:357
  91.3 3.6 %collective-permute-start.11 = (f32[8,128]{1,0:T(8,128)S(1)}, f32[8,128]{1,0:T(8,128)S(1)}, u32[]{:S(2)}, u32[]{:S(2)}) collective-permute-start(f32[8,128]{1,0:T(8,128)S(1)} %get-tuple-element.36), channel_id=1, source_target_pairs={{0,64},{32,96},{64,0},{96,32},{128,192},{160,224},{192,128},{224,1... | collective-permute-start | bytes 12296 | tf_op jit(solution)/shard_map/ppermute | solution.py:357
  91.4 3.5 %collective-permute-start.12 = (f32[8,128]{1,0:T(8,128)S(1)}, f32[8,128]{1,0:T(8,128)S(1)}, u32[]{:S(2)}, u32[]{:S(2)}) collective-permute-start(f32[8,128]{1,0:T(8,128)S(1)} %get-tuple-element.37), channel_id=1, source_target_pairs={{0,128},{32,160},{64,192},{96,224},{128,0},{160,32},{192,64},{224,... | collective-permute-start | bytes 12296 | tf_op jit(solution)/shard_map/ppermute | solution.py:357
  92.9 4.3 %collective-permute-start.13 = (f32[8,128]{1,0:T(8,128)S(1)}, f32[8,128]{1,0:T(8,128)S(1)}, u32[]{:S(2)}, u32[]{:S(2)}) collective-permute-start(f32[8,128]{1,0:T(8,128)S(1)} %get-tuple-element.38), channel_id=1, source_target_pairs={{0,192},{32,224},{64,128},{96,160},{128,64},{160,96},{192,0},{224,... | collective-permute-start | bytes 12296 | tf_op jit(solution)/shard_map/ppermute | solution.py:357

commit v8 on v7

--- a/solution.py
+++ b/solution.py
@@ -309,7 +309,7 @@
 
 
 def next_kernel(
-    mask, mine, far, middle, near, start, refl, refl_rest, fwd_high, fwd_low, inv_high, inv_low,
+    mask, mine, near, middle, far, start, refl, refl_rest, fwd_high, fwd_low, inv_high, inv_low,
     out, spectrum, product, rows,
 ):
     total = (mine[...] + near[...]) + (far[...] + middle[...])
@@ -317,7 +317,7 @@
     convolve_in(down.astype(BF16), (refl, refl_rest), fwd_high, fwd_low, inv_high, inv_low, out, spectrum, product, rows)
 
 
-def last_kernel(mask, mine, near, middle, far, start, own, out, up_out):
+def last_kernel(mask, mine, far, middle, near, start, own, out, up_out):
     begin = lax.axis_index("shot") * SHARE_LAGS
     shift = lax.rem(LAGS - begin, LAGS)
     start_here = pltpu.roll(start[...].astype(F32), shift, 1)[:, :SHARE_LAGS]
@@ -438,7 +438,7 @@
             )
             other = over_shot(mine, 1)
             mine = call(pair_kernel, "pair_sum", [VM] * 2, [((traces, LAGS), F32)], [], mine, other)
-            others = [over_shot(mine, step) for step in (6, 4, 2)]
+            others = [over_shot(mine, step) for step in (6, 4, 2)][::-1]
             partial = call(
                 next_kernel, "next_convolution", [VM] * 12, [conv_out], conv_scratch,
                 rcv_mask, mine, *others, start, refl, refl_rest, *waves,
@@ -452,7 +452,7 @@
                 last_pair_kernel, "last_pair_sum", [VM] * 2, [((8, LANES), F32)] * CHIPS,
                 [pltpu.VMEM((CHIPS, 8, LANES), F32)], keep, over_shot(send, 1),
             )
-            parts = [mine] + [over_shot(part, step) for part, step in ((near, 2), (middle, 4), (far, 6))]
+            parts = [mine] + [over_shot(part, step) for part, step in ((far, 6), (middle, 4), (near, 2))]
     focus_down, focus_up = call(
         last_kernel, "downgoing", [VM] * 7, [((RCV_HERE, FOCI, SHARE_LAGS), F32), ((2, FOCI, LAGS), F32)], [],
         rcv_mask, *parts, start, own,

time: 98.2 us -> 96.5 us (0.983)
  waiting for transfers between devices: 11.4 us -> 10.3 us
    ppermute x12, waiting for transfers between devices: 8.08 us -> 6.98 us  [over_shot(): lax.ppermute(array, 'shot', [(place, place ^ step) for place in range(SHO...]
  transfers between devices with their start and end apart: 14 -> 14, of which waited for: 8 -> 9; matrix products, arithmetic and copies ran while one was open for 0% -> 0% of each run, Pallas kernels for 5% -> 5%
where the time goes in v8:
time: 96.5 us; the launch traced here: 96.2 us
  blocking collectives  42.3 us (44%)
  starting transfers between devices  32.6 us (34%)
  Pallas kernels  10.3 us (11%)
  waiting for transfers between devices  10.3 us (11%)
    ppermute x12, starting transfers between devices, over_shot(): lax.ppermute(array, 'shot', [(place, place ^ step) for place in range(SHO...  23.7 us
    all_to_all x2, blocking collectives, on_device(): lax.all_to_all(partial, 'rcv', 0, 0, tiled=True, axis_index_groups=over_p...  23.4 us
    all_to_all x2, blocking collectives, on_device(): lax.all_to_all(rounded, 'rcv', 0, 0, tiled=True, axis_index_groups=over_p...  18.9 us
    pallas_call x16, Pallas kernels, call(): pl.pallas_call(kernel, name=name, in_specs=specs, out_specs=[VM] * len(ou...  10.3 us
    ppermute x2, starting transfers between devices, on_device(): lax.ppermute(mine, 'rcv', [(place, place ^ 4) for place in range(RCV_AXIS)])  8.9 us
    ppermute x12, waiting for transfers between devices, over_shot(): lax.ppermute(array, 'shot', [(place, place ^ step) for place in range(SHO...  6.98 us
    ppermute x2, waiting for transfers between devices, on_device(): lax.ppermute(mine, 'rcv', [(place, place ^ 4) for place in range(RCV_AXIS)])  3.29 us
  transfers between devices with their start and end apart: 14, of which 9 were waited for; matrix products, arithmetic and copies ran while one was open for 0% of the time, Pallas kernels for 5%

profile of v8, /device:TPU:1, one launch (start us, length us, event | category | flops | bytes accessed | tf_op | source)
XLA Modules:
  0.0 96.2 jit_solution(6043037119097852838)
XLA Ops:
  0.6 1.1 %pick.1.mine = bf16[32,256]{1,0:T(8,128)(2,1)S(1)} custom-call(s32[2]{0:T(128)} %focus_hbm.1, bf16[64,16,256]{2,1,0:T(8,128)(2,1)} %reflection_hbm.3), custom_call_target="tpu_custom_call" | custom-call | tf_op jit(solution)/shard_map/pick/pallas_call | solution.py:345
  1.7 5.3 %collective-permute-start.2 = (bf16[32,256]{1,0:T(8,128)(2,1)S(1)}, bf16[32,256]{1,0:T(8,128)(2,1)S(1)}, u32[]{:S(2)}, u32[]{:S(2)}) collective-permute-start(bf16[32,256]{1,0:T(8,128)(2,1)S(1)} %pick.1.mine), channel_id=1, source_target_pairs={{0,192},{32,224},{64,128},{96,160},{128,64},{160,96},{192,0},{224,... | collective-permute-start | bytes 49160 | tf_op jit(solution)/shard_map/ppermute | solution.py:357
  7.0 0.0 collective-permute-start.1
  7.0 0.4 collective-permute-start
  7.4 2.4 %preparation.1 = (f32[4,512,128]{2,1,0:T(8,128)S(1)}, bf16[32,16,256]{2,1,0:T(8,128)(2,1)S(1)}, bf16[256,512]{1,0:T(8,128)(2,1)S(1)}, bf16[256,512]{1,0:T(8,128)...) custom-call(bf16[64,16,256]{2,1,0:T(8,128)(2,1)} %reflection_hbm.3, ...), custom_call_target="tpu_custom_call" | custom-call | tf_op jit(solution)/shard_map/preparation/pallas_call | solution.py:345
  9.8 0.0 collective-permute-done.2.far
  9.8 0.8 collective-permute-done.1.middle
  10.6 0.0 collective-permute-done.near
  10.6 0.1 chip_picks.1.mine
  10.8 1.9 %collective-permute-start.3 = (bf16[32,256]{1,0:T(8,128)(2,1)S(1)}, bf16[32,256]{1,0:T(8,128)(2,1)S(1)}, u32[]{:S(2)}, u32[]{:S(2)}) collective-permute-start(bf16[32,256]{1,0:T(8,128)(2,1)S(1)} %chip_picks.1.mine), channel_id=1, source_target_pairs={{0,32},{32,0},{64,96},{96,64},{128,160},{160,128},{192,224},{224,1... | collective-permute-start | bytes 49160 | tf_op jit(solution)/shard_map/ppermute | solution.py:357
  12.7 1.3 %rest_preparation.1.refl_rest = f32[4,512,128]{2,1,0:T(8,128)S(1)} custom-call(bf16[32,16,256]{2,1,0:T(8,128)(2,1)S(1)} %get-tuple-element.25.reflection, bf16[256,512]{1,0:T(8,128)(2,1)S(1)} %get-tuple-element.26.high.fwd_high, bf16[256,512]{1,0:T(8,128)(2,1)S(1)} %get-tuple-element.27.low.fwd_low), custom_call_target="tpu_custom_call" | custom-call | tf_op jit(solution)/shard_map/rest_preparation/pallas_call | solution.py:345
  14.0 0.0 collective-permute-done.3.other
  14.0 1.0 first_convolution.1
  15.0 13.7 %all_to_all.20.parts = f32[16,16,128]{2,1,0:T(8,128)S(1)} all-to-all(f32[16,16,128]{2,1,0:T(8,128)S(1)} %get-tuple-element.30), channel_id=1, replica_groups={{0,1,2,3,8,9,10,11,16,17,18,19,24,25,26,27},{4,5,6,7,12,13,14,15,20,21,..., dimensions={0} | all-to-all | bytes 262144 | tf_op jit(solution)/shard_map/all_to_all | solution.py:423
  28.7 4.6 %collective-permute-start.4 = (f32[16,128]{1,0:T(8,128)S(1)}, f32[16,128]{1,0:T(8,128)S(1)}, u32[]{:S(2)}, u32[]{:S(2)}) collective-permute-start(f32[16,128]{1,0:T(8,128)S(1)} %plane_sum.2.mine), channel_id=1, source_target_pairs={{0,4},{1,5},{2,6},{3,7},{4,0},{5,1},{6,2},{7,3},{8,12},{9,13},{10,... | collective-permute-start | bytes 24584 | tf_op jit(solution)/shard_map/ppermute | solution.py:425
  33.3 0.8 masks.1
  34.1 1.1 %collective-permute-done.4.other = f32[16,128]{1,0:T(8,128)S(1)} collective-permute-done((f32[16,128]{1,0:T(8,128)S(1)}, f32[16,128]{1,0:T(8,128)S(1)}, u32[]{:S(2)}, u32[]{:S(2)}) %collective-permute-start.4) | collective-permute-done | bytes 8224 | tf_op jit(solution)/shard_map/ppermute | solution.py:425
  35.2 9.3 %all_to_all.21.upgoing = bf16[16,16,128]{2,1,0:T(8,128)(2,1)S(1)} all-to-all(bf16[16,16,128]{2,1,0:T(8,128)(2,1)S(1)} %upgoing.1), channel_id=1, replica_groups={{0,1,2,3,8,9,10,11,16,17,18,19,24,25,26,27},{4,5,6,7,12,13,14,15,20,21,..., dimensions={0} | all-to-all | bytes 131072 | tf_op jit(solution)/shard_map/all_to_all | solution.py:433
  44.5 0.9 correlation.1.mine
  45.4 3.8 %collective-permute-start.5 = (f32[32,256]{1,0:T(8,128)S(1)}, f32[32,256]{1,0:T(8,128)S(1)}, u32[]{:S(2)}, u32[]{:S(2)}) collective-permute-start(f32[32,256]{1,0:T(8,128)S(1)} %correlation.1.mine), channel_id=1, source_target_pairs={{0,32},{32,0},{64,96},{96,64},{128,160},{160,128},{192,224},{224,1... | collective-permute-start | bytes 98312 | tf_op jit(solution)/shard_map/ppermute | solution.py:357
  49.2 0.9 collective-permute-done.5.other
  50.1 2.0 %collective-permute-start.8 = (f32[32,256]{1,0:T(8,128)S(1)}, f32[32,256]{1,0:T(8,128)S(1)}, u32[]{:S(2)}, u32[]{:S(2)}) collective-permute-start(f32[32,256]{1,0:T(8,128)S(1)} %pair_sum.1.mine), channel_id=1, source_target_pairs={{0,192},{32,224},{64,128},{96,160},{128,64},{160,96},{192,0},{224,... | collective-permute-start | bytes 98312 | tf_op jit(solution)/shard_map/ppermute | solution.py:357
  52.0 0.0 collective-permute-start.7
  52.0 1.6 %collective-permute-start.6 = (f32[32,256]{1,0:T(8,128)S(1)}, f32[32,256]{1,0:T(8,128)S(1)}, u32[]{:S(2)}, u32[]{:S(2)}) collective-permute-start(f32[32,256]{1,0:T(8,128)S(1)} %pair_sum.1.mine), channel_id=1, source_target_pairs={{0,64},{32,96},{64,0},{96,32},{128,192},{160,224},{192,128},{224,1... | collective-permute-start | bytes 98312 | tf_op jit(solution)/shard_map/ppermute | solution.py:357
  53.6 1.0 %collective-permute-done.8.far = f32[32,256]{1,0:T(8,128)S(1)} collective-permute-done((f32[32,256]{1,0:T(8,128)S(1)}, f32[32,256]{1,0:T(8,128)S(1)}, u32[]{:S(2)}, u32[]{:S(2)}) %collective-permute-start.8) | collective-permute-done | bytes 32800 | tf_op jit(solution)/shard_map/ppermute | solution.py:357
  54.6 1.5 %collective-permute-done.7.middle = f32[32,256]{1,0:T(8,128)S(1)} collective-permute-done((f32[32,256]{1,0:T(8,128)S(1)}, f32[32,256]{1,0:T(8,128)S(1)}, u32[]{:S(2)}, u32[]{:S(2)}) %collective-permute-start.7) | collective-permute-done | bytes 32800 | tf_op jit(solution)/shard_map/ppermute | solution.py:357
  56.2 0.0 collective-permute-done.6.near
  56.2 0.9 next_convolution.1
  57.1 9.7 %all_to_all.22.parts = f32[16,16,128]{2,1,0:T(8,128)S(1)} all-to-all(f32[16,16,128]{2,1,0:T(8,128)S(1)} %next_convolution.1), channel_id=1, replica_groups={{0,1,2,3,8,9,10,11,16,17,18,19,24,25,26,27},{4,5,6,7,12,13,14,15,20,21,..., dimensions={0} | all-to-all | bytes 262144 | tf_op jit(solution)/shard_map/all_to_all | solution.py:423
  66.8 4.3 %collective-permute-start.9 = (f32[16,128]{1,0:T(8,128)S(1)}, f32[16,128]{1,0:T(8,128)S(1)}, u32[]{:S(2)}, u32[]{:S(2)}) collective-permute-start(f32[16,128]{1,0:T(8,128)S(1)} %plane_sum.3.mine), channel_id=1, source_target_pairs={{0,4},{1,5},{2,6},{3,7},{4,0},{5,1},{6,2},{7,3},{8,12},{9,13},{10,... | collective-permute-start | bytes 24584 | tf_op jit(solution)/shard_map/ppermute | solution.py:425
  71.1 2.2 %collective-permute-done.9.other = f32[16,128]{1,0:T(8,128)S(1)} collective-permute-done((f32[16,128]{1,0:T(8,128)S(1)}, f32[16,128]{1,0:T(8,128)S(1)}, u32[]{:S(2)}, u32[]{:S(2)}) %collective-permute-start.9) | collective-permute-done | bytes 8224 | tf_op jit(solution)/shard_map/ppermute | solution.py:425
  73.4 9.6 %all_to_all.23.upgoing = bf16[16,16,128]{2,1,0:T(8,128)(2,1)S(1)} all-to-all(bf16[16,16,128]{2,1,0:T(8,128)(2,1)S(1)} %get-tuple-element.32), channel_id=1, replica_groups={{0,1,2,3,8,9,10,11,16,17,18,19,24,25,26,27},{4,5,6,7,12,13,14,15,20,21,..., dimensions={0} | all-to-all | bytes 131072 | tf_op jit(solution)/shard_map/all_to_all | solution.py:433
  83.0 1.0 %last_correlation.1 = (f32[4,8,128]{2,1,0:T(8,128)S(1)}, f32[4,8,128]{2,1,0:T(8,128)S(1)}) custom-call(bf16[16,16,128]{2,1,0:T(8,128)(2,1)S(1)} %all_to_all.23.upgoing, f32[4,512,128]{2,1,0:T(8,128)S(1)} %get-tuple-element.24.refl, f32[4,512,128]{2,1,0:T(8,128)S(1)} %rest_preparation.1.refl_rest, bf16[256,512]{1,0:T(8,128)(2,1)S(1)} %get-tuple-element.26.high.fwd_high, ...), custom_call_target="tpu_custom_call" | custom-call | tf_op jit(solution)/shard_map/last_correlation/pallas_call | solution.py:345
  84.0 5.2 %collective-permute-start.10 = (f32[4,8,128]{2,1,0:T(8,128)S(1)}, f32[4,8,128]{2,1,0:T(8,128)S(1)}, u32[]{:S(2)}, u32[]{:S(2)}) collective-permute-start(f32[4,8,128]{2,1,0:T(8,128)S(1)} %get-tuple-element.34), channel_id=1, source_target_pairs={{0,32},{32,0},{64,96},{96,64},{128,160},{160,128},{192,224},{224,1... | collective-permute-start | bytes 49160 | tf_op jit(solution)/shard_map/ppermute | solution.py:357
  89.2 0.8 collective-permute-done.10.other
  90.0 1.8 %collective-permute-start.11 = (f32[8,128]{1,0:T(8,128)S(1)}, f32[8,128]{1,0:T(8,128)S(1)}, u32[]{:S(2)}, u32[]{:S(2)}) collective-permute-start(f32[8,128]{1,0:T(8,128)S(1)} %get-tuple-element.36), channel_id=1, source_target_pairs={{0,192},{32,224},{64,128},{96,160},{128,64},{160,96},{192,0},{224,... | collective-permute-start | bytes 12296 | tf_op jit(solution)/shard_map/ppermute | solution.py:357
  91.9 0.2 collective-permute-start.12
  92.0 1.5 %collective-permute-start.13 = (f32[8,128]{1,0:T(8,128)S(1)}, f32[8,128]{1,0:T(8,128)S(1)}, u32[]{:S(2)}, u32[]{:S(2)}) collective-permute-start(f32[8,128]{1,0:T(8,128)S(1)} %get-tuple-element.38), channel_id=1, source_target_pairs={{0,64},{32,96},{64,0},{96,32},{128,192},{160,224},{192,128},{224,1... | collective-permute-start | bytes 12296 | tf_op jit(solution)/shard_map/ppermute | solution.py:357
  93.6 0.7 collective-permute-done.11.far
  94.3 1.2 %collective-permute-done.12.middle = f32[8,128]{1,0:T(8,128)S(1)} collective-permute-done((f32[8,128]{1,0:T(8,128)S(1)}, f32[8,128]{1,0:T(8,128)S(1)}, u32[]{:S(2)}, u32[]{:S(2)}) %collective-permute-start.12) | collective-permute-done | bytes 4128 | tf_op jit(solution)/shard_map/ppermute | solution.py:357
  95.5 0.0 collective-permute-done.13.near
  95.5 0.7 downgoing.1
  (6 shorter events, 0.1 us)
Async XLA Ops:
  1.7 8.1 %collective-permute-start.2 = (bf16[32,256]{1,0:T(8,128)(2,1)S(1)}, bf16[32,256]{1,0:T(8,128)(2,1)S(1)}, u32[]{:S(2)}, u32[]{:S(2)}) collective-permute-start(bf16[32,256]{1,0:T(8,128)(2,1)S(1)} %pick.1.mine), channel_id=1, source_target_pairs={{0,192},{32,224},{64,128},{96,160},{128,64},{160,96},{192,0},{224,... | collective-permute-start | bytes 49160 | tf_op jit(solution)/shard_map/ppermute | solution.py:357
  7.0 3.7 %collective-permute-start.1 = (bf16[32,256]{1,0:T(8,128)(2,1)S(1)}, bf16[32,256]{1,0:T(8,128)(2,1)S(1)}, u32[]{:S(2)}, u32[]{:S(2)}) collective-permute-start(bf16[32,256]{1,0:T(8,128)(2,1)S(1)} %pick.1.mine), channel_id=1, source_target_pairs={{0,128},{32,160},{64,192},{96,224},{128,0},{160,32},{192,64},{224,... | collective-permute-start | bytes 49160 | tf_op jit(solution)/shard_map/ppermute | solution.py:357
  7.0 3.7 %collective-permute-start = (bf16[32,256]{1,0:T(8,128)(2,1)S(1)}, bf16[32,256]{1,0:T(8,128)(2,1)S(1)}, u32[]{:S(2)}, u32[]{:S(2)}) collective-permute-start(bf16[32,256]{1,0:T(8,128)(2,1)S(1)} %pick.1.mine), channel_id=1, source_target_pairs={{0,64},{32,96},{64,0},{96,32},{128,192},{160,224},{192,128},{224,1... | collective-permute-start | bytes 49160 | tf_op jit(solution)/shard_map/ppermute | solution.py:357
  10.8 3.2 %collective-permute-start.3 = (bf16[32,256]{1,0:T(8,128)(2,1)S(1)}, bf16[32,256]{1,0:T(8,128)(2,1)S(1)}, u32[]{:S(2)}, u32[]{:S(2)}) collective-permute-start(bf16[32,256]{1,0:T(8,128)(2,1)S(1)} %chip_picks.1.mine), channel_id=1, source_target_pairs={{0,32},{32,0},{64,96},{96,64},{128,160},{160,128},{192,224},{224,1... | collective-permute-start | bytes 49160 | tf_op jit(solution)/shard_map/ppermute | solution.py:357
  28.7 6.5 %collective-permute-start.4 = (f32[16,128]{1,0:T(8,128)S(1)}, f32[16,128]{1,0:T(8,128)S(1)}, u32[]{:S(2)}, u32[]{:S(2)}) collective-permute-start(f32[16,128]{1,0:T(8,128)S(1)} %plane_sum.2.mine), channel_id=1, source_target_pairs={{0,4},{1,5},{2,6},{3,7},{4,0},{5,1},{6,2},{7,3},{8,12},{9,13},{10,... | collective-permute-start | bytes 24584 | tf_op jit(solution)/shard_map/ppermute | solution.py:425
  45.4 4.7 %collective-permute-start.5 = (f32[32,256]{1,0:T(8,128)S(1)}, f32[32,256]{1,0:T(8,128)S(1)}, u32[]{:S(2)}, u32[]{:S(2)}) collective-permute-start(f32[32,256]{1,0:T(8,128)S(1)} %correlation.1.mine), channel_id=1, source_target_pairs={{0,32},{32,0},{64,96},{96,64},{128,160},{160,128},{192,224},{224,1... | collective-permute-start | bytes 98312 | tf_op jit(solution)/shard_map/ppermute | solution.py:357
  50.1 4.6 %collective-permute-start.8 = (f32[32,256]{1,0:T(8,128)S(1)}, f32[32,256]{1,0:T(8,128)S(1)}, u32[]{:S(2)}, u32[]{:S(2)}) collective-permute-start(f32[32,256]{1,0:T(8,128)S(1)} %pair_sum.1.mine), channel_id=1, source_target_pairs={{0,192},{32,224},{64,128},{96,160},{128,64},{160,96},{192,0},{224,... | collective-permute-start | bytes 98312 | tf_op jit(solution)/shard_map/ppermute | solution.py:357
  52.0 4.2 %collective-permute-start.7 = (f32[32,256]{1,0:T(8,128)S(1)}, f32[32,256]{1,0:T(8,128)S(1)}, u32[]{:S(2)}, u32[]{:S(2)}) collective-permute-start(f32[32,256]{1,0:T(8,128)S(1)} %pair_sum.1.mine), channel_id=1, source_target_pairs={{0,128},{32,160},{64,192},{96,224},{128,0},{160,32},{192,64},{224,... | collective-permute-start | bytes 98312 | tf_op jit(solution)/shard_map/ppermute | solution.py:357
  52.0 4.2 %collective-permute-start.6 = (f32[32,256]{1,0:T(8,128)S(1)}, f32[32,256]{1,0:T(8,128)S(1)}, u32[]{:S(2)}, u32[]{:S(2)}) collective-permute-start(f32[32,256]{1,0:T(8,128)S(1)} %pair_sum.1.mine), channel_id=1, source_target_pairs={{0,64},{32,96},{64,0},{96,32},{128,192},{160,224},{192,128},{224,1... | collective-permute-start | bytes 98312 | tf_op jit(solution)/shard_map/ppermute | solution.py:357
  66.8 6.5 %collective-permute-start.9 = (f32[16,128]{1,0:T(8,128)S(1)}, f32[16,128]{1,0:T(8,128)S(1)}, u32[]{:S(2)}, u32[]{:S(2)}) collective-permute-start(f32[16,128]{1,0:T(8,128)S(1)} %plane_sum.3.mine), channel_id=1, source_target_pairs={{0,4},{1,5},{2,6},{3,7},{4,0},{5,1},{6,2},{7,3},{8,12},{9,13},{10,... | collective-permute-start | bytes 24584 | tf_op jit(solution)/shard_map/ppermute | solution.py:425
  84.0 6.1 %collective-permute-start.10 = (f32[4,8,128]{2,1,0:T(8,128)S(1)}, f32[4,8,128]{2,1,0:T(8,128)S(1)}, u32[]{:S(2)}, u32[]{:S(2)}) collective-permute-start(f32[4,8,128]{2,1,0:T(8,128)S(1)} %get-tuple-element.34), channel_id=1, source_target_pairs={{0,32},{32,0},{64,96},{96,64},{128,160},{160,128},{192,224},{224,1... | collective-permute-start | bytes 49160 | tf_op jit(solution)/shard_map/ppermute | solution.py:357
  90.0 4.3 %collective-permute-start.11 = (f32[8,128]{1,0:T(8,128)S(1)}, f32[8,128]{1,0:T(8,128)S(1)}, u32[]{:S(2)}, u32[]{:S(2)}) collective-permute-start(f32[8,128]{1,0:T(8,128)S(1)} %get-tuple-element.36), channel_id=1, source_target_pairs={{0,192},{32,224},{64,128},{96,160},{128,64},{160,96},{192,0},{224,... | collective-permute-start | bytes 12296 | tf_op jit(solution)/shard_map/ppermute | solution.py:357
  91.9 3.6 %collective-permute-start.12 = (f32[8,128]{1,0:T(8,128)S(1)}, f32[8,128]{1,0:T(8,128)S(1)}, u32[]{:S(2)}, u32[]{:S(2)}) collective-permute-start(f32[8,128]{1,0:T(8,128)S(1)} %get-tuple-element.37), channel_id=1, source_target_pairs={{0,128},{32,160},{64,192},{96,224},{128,0},{160,32},{192,64},{224,... | collective-permute-start | bytes 12296 | tf_op jit(solution)/shard_map/ppermute | solution.py:357
  92.0 3.4 %collective-permute-start.13 = (f32[8,128]{1,0:T(8,128)S(1)}, f32[8,128]{1,0:T(8,128)S(1)}, u32[]{:S(2)}, u32[]{:S(2)}) collective-permute-start(f32[8,128]{1,0:T(8,128)S(1)} %get-tuple-element.38), channel_id=1, source_target_pairs={{0,64},{32,96},{64,0},{96,32},{128,192},{160,224},{192,128},{224,1... | collective-permute-start | bytes 12296 | tf_op jit(solution)/shard_map/ppermute | solution.py:357

commit v9 on v8

--- a/solution.py
+++ b/solution.py
@@ -297,8 +297,8 @@
         out[...] = total[place]
 
 
-def pair_kernel(mine, other, out):
-    out[...] = mine[...] + other[...]
+def chips_kernel(mine, near, middle, far, out):
+    out[...] = (mine[...] + near[...]) + (far[...] + middle[...])
 
 
 def total_of(parts):
@@ -309,11 +309,10 @@
 
 
 def next_kernel(
-    mask, mine, near, middle, far, start, refl, refl_rest, fwd_high, fwd_low, inv_high, inv_low,
+    mask, mine, other, start, refl, refl_rest, fwd_high, fwd_low, inv_high, inv_low,
     out, spectrum, product, rows,
 ):
-    total = (mine[...] + near[...]) + (far[...] + middle[...])
-    down = start[...].astype(F32) + jnp.where(mask[...] != 0, total, 0.0)
+    down = start[...].astype(F32) + jnp.where(mask[...] != 0, mine[...] + other[...], 0.0)
     convolve_in(down.astype(BF16), (refl, refl_rest), fwd_high, fwd_low, inv_high, inv_low, out, spectrum, product, rows)
 
 
@@ -436,12 +435,11 @@
                 correlate_kernel, "correlation", [VM] * 7, [((traces, LAGS), F32)], corr_scratch,
                 upgoing, refl, refl_rest, *waves,
             )
-            other = over_shot(mine, 1)
-            mine = call(pair_kernel, "pair_sum", [VM] * 2, [((traces, LAGS), F32)], [], mine, other)
             others = [over_shot(mine, step) for step in (6, 4, 2)][::-1]
+            mine = call(chips_kernel, "chip_sum", [VM] * 4, [((traces, LAGS), F32)], [], mine, *others)
             partial = call(
-                next_kernel, "next_convolution", [VM] * 12, [conv_out], conv_scratch,
-                rcv_mask, mine, *others, start, refl, refl_rest, *waves,
+                next_kernel, "next_convolution", [VM] * 10, [conv_out], conv_scratch,
+                rcv_mask, mine, over_shot(mine, 1), start, refl, refl_rest, *waves,
             )
         else:
             keep, send = call(

time: 96.5 us -> 96.3 us (level)
  no operation moved by 1% of the time
where the time goes in v9:
time: 96.3 us; the launch traced here: 96 us
  blocking collectives  42.3 us (44%)
  starting transfers between devices  33.2 us (34%)
  Pallas kernels  10.3 us (11%)
  waiting for transfers between devices  9.54 us (10%)
    ppermute x12, starting transfers between devices, over_shot(): lax.ppermute(array, 'shot', [(place, place ^ step) for place in range(SHO...  24.1 us
    all_to_all x2, blocking collectives, on_device(): lax.all_to_all(partial, 'rcv', 0, 0, tiled=True, axis_index_groups=over_p...  23.4 us
    all_to_all x2, blocking collectives, on_device(): lax.all_to_all(rounded, 'rcv', 0, 0, tiled=True, axis_index_groups=over_p...  18.9 us
    pallas_call x16, Pallas kernels, call(): pl.pallas_call(kernel, name=name, in_specs=specs, out_specs=[VM] * len(ou...  10.3 us
    ppermute x2, starting transfers between devices, on_device(): lax.ppermute(mine, 'rcv', [(place, place ^ 4) for place in range(RCV_AXIS)])  9.01 us
    ppermute x12, waiting for transfers between devices, over_shot(): lax.ppermute(array, 'shot', [(place, place ^ step) for place in range(SHO...  6.36 us
    ppermute x2, waiting for transfers between devices, on_device(): lax.ppermute(mine, 'rcv', [(place, place ^ 4) for place in range(RCV_AXIS)])  3.18 us
  transfers between devices with their start and end apart: 14, of which 9 were waited for; matrix products, arithmetic and copies ran while one was open for 0% of the time, Pallas kernels for 5%

profile of v9, /device:TPU:1, one launch (start us, length us, event | category | flops | bytes accessed | tf_op | source)
XLA Modules:
  0.0 96.0 jit_solution(7177003715012031604)
XLA Ops:
  0.6 1.1 %pick.1.mine = bf16[32,256]{1,0:T(8,128)(2,1)S(1)} custom-call(s32[2]{0:T(128)} %focus_hbm.1, bf16[64,16,256]{2,1,0:T(8,128)(2,1)} %reflection_hbm.3), custom_call_target="tpu_custom_call" | custom-call | tf_op jit(solution)/shard_map/pick/pallas_call | solution.py:344
  1.7 5.3 %collective-permute-start.2 = (bf16[32,256]{1,0:T(8,128)(2,1)S(1)}, bf16[32,256]{1,0:T(8,128)(2,1)S(1)}, u32[]{:S(2)}, u32[]{:S(2)}) collective-permute-start(bf16[32,256]{1,0:T(8,128)(2,1)S(1)} %pick.1.mine), channel_id=1, source_target_pairs={{0,192},{32,224},{64,128},{96,160},{128,64},{160,96},{192,0},{224,... | collective-permute-start | bytes 49160 | tf_op jit(solution)/shard_map/ppermute | solution.py:356
  7.0 0.0 collective-permute-start.1
  7.0 0.4 collective-permute-start
  7.4 2.4 %preparation.1 = (f32[4,512,128]{2,1,0:T(8,128)S(1)}, bf16[32,16,256]{2,1,0:T(8,128)(2,1)S(1)}, bf16[256,512]{1,0:T(8,128)(2,1)S(1)}, bf16[256,512]{1,0:T(8,128)...) custom-call(bf16[64,16,256]{2,1,0:T(8,128)(2,1)} %reflection_hbm.3, ...), custom_call_target="tpu_custom_call" | custom-call | tf_op jit(solution)/shard_map/preparation/pallas_call | solution.py:344
  9.8 0.0 collective-permute-done.2.far
  9.8 0.8 collective-permute-done.1.middle
  10.6 0.0 collective-permute-done.near
  10.6 0.1 chip_picks.1.mine
  10.8 1.9 %collective-permute-start.3 = (bf16[32,256]{1,0:T(8,128)(2,1)S(1)}, bf16[32,256]{1,0:T(8,128)(2,1)S(1)}, u32[]{:S(2)}, u32[]{:S(2)}) collective-permute-start(bf16[32,256]{1,0:T(8,128)(2,1)S(1)} %chip_picks.1.mine), channel_id=1, source_target_pairs={{0,32},{32,0},{64,96},{96,64},{128,160},{160,128},{192,224},{224,1... | collective-permute-start | bytes 49160 | tf_op jit(solution)/shard_map/ppermute | solution.py:356
  12.7 1.3 %rest_preparation.1.refl_rest = f32[4,512,128]{2,1,0:T(8,128)S(1)} custom-call(bf16[32,16,256]{2,1,0:T(8,128)(2,1)S(1)} %get-tuple-element.25.reflection, bf16[256,512]{1,0:T(8,128)(2,1)S(1)} %get-tuple-element.26.high.fwd_high, bf16[256,512]{1,0:T(8,128)(2,1)S(1)} %get-tuple-element.27.low.fwd_low), custom_call_target="tpu_custom_call" | custom-call | tf_op jit(solution)/shard_map/rest_preparation/pallas_call | solution.py:344
  14.0 0.0 collective-permute-done.3.other
  14.0 1.0 first_convolution.1
  15.0 13.7 %all_to_all.20.parts = f32[16,16,128]{2,1,0:T(8,128)S(1)} all-to-all(f32[16,16,128]{2,1,0:T(8,128)S(1)} %get-tuple-element.30), channel_id=1, replica_groups={{0,1,2,3,8,9,10,11,16,17,18,19,24,25,26,27},{4,5,6,7,12,13,14,15,20,21,..., dimensions={0} | all-to-all | bytes 262144 | tf_op jit(solution)/shard_map/all_to_all | solution.py:422
  28.7 4.6 %collective-permute-start.4 = (f32[16,128]{1,0:T(8,128)S(1)}, f32[16,128]{1,0:T(8,128)S(1)}, u32[]{:S(2)}, u32[]{:S(2)}) collective-permute-start(f32[16,128]{1,0:T(8,128)S(1)} %plane_sum.2.mine), channel_id=1, source_target_pairs={{0,4},{1,5},{2,6},{3,7},{4,0},{5,1},{6,2},{7,3},{8,12},{9,13},{10,... | collective-permute-start | bytes 24584 | tf_op jit(solution)/shard_map/ppermute | solution.py:424
  33.3 0.8 masks.1
  34.1 1.1 %collective-permute-done.4.other = f32[16,128]{1,0:T(8,128)S(1)} collective-permute-done((f32[16,128]{1,0:T(8,128)S(1)}, f32[16,128]{1,0:T(8,128)S(1)}, u32[]{:S(2)}, u32[]{:S(2)}) %collective-permute-start.4) | collective-permute-done | bytes 8224 | tf_op jit(solution)/shard_map/ppermute | solution.py:424
  35.2 9.3 %all_to_all.21.upgoing = bf16[16,16,128]{2,1,0:T(8,128)(2,1)S(1)} all-to-all(bf16[16,16,128]{2,1,0:T(8,128)(2,1)S(1)} %upgoing.1), channel_id=1, replica_groups={{0,1,2,3,8,9,10,11,16,17,18,19,24,25,26,27},{4,5,6,7,12,13,14,15,20,21,..., dimensions={0} | all-to-all | bytes 131072 | tf_op jit(solution)/shard_map/all_to_all | solution.py:432
  44.5 0.9 correlation.1.mine
  45.4 2.0 %collective-permute-start.7 = (f32[32,256]{1,0:T(8,128)S(1)}, f32[32,256]{1,0:T(8,128)S(1)}, u32[]{:S(2)}, u32[]{:S(2)}) collective-permute-start(f32[32,256]{1,0:T(8,128)S(1)} %correlation.1.mine), channel_id=1, source_target_pairs={{0,192},{32,224},{64,128},{96,160},{128,64},{160,96},{192,0},{224,... | collective-permute-start | bytes 98312 | tf_op jit(solution)/shard_map/ppermute | solution.py:356
  47.4 0.0 collective-permute-start.6
  47.4 1.6 %collective-permute-start.5 = (f32[32,256]{1,0:T(8,128)S(1)}, f32[32,256]{1,0:T(8,128)S(1)}, u32[]{:S(2)}, u32[]{:S(2)}) collective-permute-start(f32[32,256]{1,0:T(8,128)S(1)} %correlation.1.mine), channel_id=1, source_target_pairs={{0,64},{32,96},{64,0},{96,32},{128,192},{160,224},{192,128},{224,1... | collective-permute-start | bytes 98312 | tf_op jit(solution)/shard_map/ppermute | solution.py:356
  49.0 1.0 %collective-permute-done.7.far = f32[32,256]{1,0:T(8,128)S(1)} collective-permute-done((f32[32,256]{1,0:T(8,128)S(1)}, f32[32,256]{1,0:T(8,128)S(1)}, u32[]{:S(2)}, u32[]{:S(2)}) %collective-permute-start.7) | collective-permute-done | bytes 32800 | tf_op jit(solution)/shard_map/ppermute | solution.py:356
  50.0 1.2 %collective-permute-done.6.middle = f32[32,256]{1,0:T(8,128)S(1)} collective-permute-done((f32[32,256]{1,0:T(8,128)S(1)}, f32[32,256]{1,0:T(8,128)S(1)}, u32[]{:S(2)}, u32[]{:S(2)}) %collective-permute-start.6) | collective-permute-done | bytes 32800 | tf_op jit(solution)/shard_map/ppermute | solution.py:356
  51.2 0.0 collective-permute-done.5.near
  51.2 5.2 %collective-permute-start.8 = (f32[32,256]{1,0:T(8,128)S(1)}, f32[32,256]{1,0:T(8,128)S(1)}, u32[]{:S(2)}, u32[]{:S(2)}) collective-permute-start(f32[32,256]{1,0:T(8,128)S(1)} %chip_sum.1.mine), channel_id=1, source_target_pairs={{0,32},{32,0},{64,96},{96,64},{128,160},{160,128},{192,224},{224,1... | collective-permute-start | bytes 98312 | tf_op jit(solution)/shard_map/ppermute | solution.py:356
  56.5 0.9 collective-permute-done.8.other
  57.3 0.9 next_convolution.1
  58.3 9.7 %all_to_all.22.parts = f32[16,16,128]{2,1,0:T(8,128)S(1)} all-to-all(f32[16,16,128]{2,1,0:T(8,128)S(1)} %next_convolution.1), channel_id=1, replica_groups={{0,1,2,3,8,9,10,11,16,17,18,19,24,25,26,27},{4,5,6,7,12,13,14,15,20,21,..., dimensions={0} | all-to-all | bytes 262144 | tf_op jit(solution)/shard_map/all_to_all | solution.py:422
  68.0 4.4 %collective-permute-start.9 = (f32[16,128]{1,0:T(8,128)S(1)}, f32[16,128]{1,0:T(8,128)S(1)}, u32[]{:S(2)}, u32[]{:S(2)}) collective-permute-start(f32[16,128]{1,0:T(8,128)S(1)} %plane_sum.3.mine), channel_id=1, source_target_pairs={{0,4},{1,5},{2,6},{3,7},{4,0},{5,1},{6,2},{7,3},{8,12},{9,13},{10,... | collective-permute-start | bytes 24584 | tf_op jit(solution)/shard_map/ppermute | solution.py:424
  72.4 2.1 %collective-permute-done.9.other = f32[16,128]{1,0:T(8,128)S(1)} collective-permute-done((f32[16,128]{1,0:T(8,128)S(1)}, f32[16,128]{1,0:T(8,128)S(1)}, u32[]{:S(2)}, u32[]{:S(2)}) %collective-permute-start.9) | collective-permute-done | bytes 8224 | tf_op jit(solution)/shard_map/ppermute | solution.py:424
  74.5 9.6 %all_to_all.23.upgoing = bf16[16,16,128]{2,1,0:T(8,128)(2,1)S(1)} all-to-all(bf16[16,16,128]{2,1,0:T(8,128)(2,1)S(1)} %get-tuple-element.32), channel_id=1, replica_groups={{0,1,2,3,8,9,10,11,16,17,18,19,24,25,26,27},{4,5,6,7,12,13,14,15,20,21,..., dimensions={0} | all-to-all | bytes 131072 | tf_op jit(solution)/shard_map/all_to_all | solution.py:432
  84.1 1.0 %last_correlation.1 = (f32[4,8,128]{2,1,0:T(8,128)S(1)}, f32[4,8,128]{2,1,0:T(8,128)S(1)}) custom-call(bf16[16,16,128]{2,1,0:T(8,128)(2,1)S(1)} %all_to_all.23.upgoing, f32[4,512,128]{2,1,0:T(8,128)S(1)} %get-tuple-element.24.refl, f32[4,512,128]{2,1,0:T(8,128)S(1)} %rest_preparation.1.refl_rest, bf16[256,512]{1,0:T(8,128)(2,1)S(1)} %get-tuple-element.26.high.fwd_high, ...), custom_call_target="tpu_custom_call" | custom-call | tf_op jit(solution)/shard_map/last_correlation/pallas_call | solution.py:344
  85.1 4.2 %collective-permute-start.10 = (f32[4,8,128]{2,1,0:T(8,128)S(1)}, f32[4,8,128]{2,1,0:T(8,128)S(1)}, u32[]{:S(2)}, u32[]{:S(2)}) collective-permute-start(f32[4,8,128]{2,1,0:T(8,128)S(1)} %get-tuple-element.34), channel_id=1, source_target_pairs={{0,32},{32,0},{64,96},{96,64},{128,160},{160,128},{192,224},{224,1... | collective-permute-start | bytes 49160 | tf_op jit(solution)/shard_map/ppermute | solution.py:356
  89.3 0.8 collective-permute-done.10.other
  90.1 1.5 %collective-permute-start.11 = (f32[8,128]{1,0:T(8,128)S(1)}, f32[8,128]{1,0:T(8,128)S(1)}, u32[]{:S(2)}, u32[]{:S(2)}) collective-permute-start(f32[8,128]{1,0:T(8,128)S(1)} %get-tuple-element.36), channel_id=1, source_target_pairs={{0,192},{32,224},{64,128},{96,160},{128,64},{160,96},{192,0},{224,... | collective-permute-start | bytes 12296 | tf_op jit(solution)/shard_map/ppermute | solution.py:356
  91.7 0.5 collective-permute-start.12
  92.1 1.5 %collective-permute-start.13 = (f32[8,128]{1,0:T(8,128)S(1)}, f32[8,128]{1,0:T(8,128)S(1)}, u32[]{:S(2)}, u32[]{:S(2)}) collective-permute-start(f32[8,128]{1,0:T(8,128)S(1)} %get-tuple-element.38), channel_id=1, source_target_pairs={{0,64},{32,96},{64,0},{96,32},{128,192},{160,224},{192,128},{224,1... | collective-permute-start | bytes 12296 | tf_op jit(solution)/shard_map/ppermute | solution.py:356
  93.7 0.7 collective-permute-done.11.far
  94.4 0.9 collective-permute-done.12.middle
  95.3 0.0 collective-permute-done.13.near
  95.3 0.7 downgoing.1
  (6 shorter events, 0.1 us)
Async XLA Ops:
  1.7 8.1 %collective-permute-start.2 = (bf16[32,256]{1,0:T(8,128)(2,1)S(1)}, bf16[32,256]{1,0:T(8,128)(2,1)S(1)}, u32[]{:S(2)}, u32[]{:S(2)}) collective-permute-start(bf16[32,256]{1,0:T(8,128)(2,1)S(1)} %pick.1.mine), channel_id=1, source_target_pairs={{0,192},{32,224},{64,128},{96,160},{128,64},{160,96},{192,0},{224,... | collective-permute-start | bytes 49160 | tf_op jit(solution)/shard_map/ppermute | solution.py:356
  7.0 3.7 %collective-permute-start.1 = (bf16[32,256]{1,0:T(8,128)(2,1)S(1)}, bf16[32,256]{1,0:T(8,128)(2,1)S(1)}, u32[]{:S(2)}, u32[]{:S(2)}) collective-permute-start(bf16[32,256]{1,0:T(8,128)(2,1)S(1)} %pick.1.mine), channel_id=1, source_target_pairs={{0,128},{32,160},{64,192},{96,224},{128,0},{160,32},{192,64},{224,... | collective-permute-start | bytes 49160 | tf_op jit(solution)/shard_map/ppermute | solution.py:356
  7.0 3.7 %collective-permute-start = (bf16[32,256]{1,0:T(8,128)(2,1)S(1)}, bf16[32,256]{1,0:T(8,128)(2,1)S(1)}, u32[]{:S(2)}, u32[]{:S(2)}) collective-permute-start(bf16[32,256]{1,0:T(8,128)(2,1)S(1)} %pick.1.mine), channel_id=1, source_target_pairs={{0,64},{32,96},{64,0},{96,32},{128,192},{160,224},{192,128},{224,1... | collective-permute-start | bytes 49160 | tf_op jit(solution)/shard_map/ppermute | solution.py:356
  10.8 3.2 %collective-permute-start.3 = (bf16[32,256]{1,0:T(8,128)(2,1)S(1)}, bf16[32,256]{1,0:T(8,128)(2,1)S(1)}, u32[]{:S(2)}, u32[]{:S(2)}) collective-permute-start(bf16[32,256]{1,0:T(8,128)(2,1)S(1)} %chip_picks.1.mine), channel_id=1, source_target_pairs={{0,32},{32,0},{64,96},{96,64},{128,160},{160,128},{192,224},{224,1... | collective-permute-start | bytes 49160 | tf_op jit(solution)/shard_map/ppermute | solution.py:356
  28.7 6.5 %collective-permute-start.4 = (f32[16,128]{1,0:T(8,128)S(1)}, f32[16,128]{1,0:T(8,128)S(1)}, u32[]{:S(2)}, u32[]{:S(2)}) collective-permute-start(f32[16,128]{1,0:T(8,128)S(1)} %plane_sum.2.mine), channel_id=1, source_target_pairs={{0,4},{1,5},{2,6},{3,7},{4,0},{5,1},{6,2},{7,3},{8,12},{9,13},{10,... | collective-permute-start | bytes 24584 | tf_op jit(solution)/shard_map/ppermute | solution.py:424
  45.4 4.7 %collective-permute-start.7 = (f32[32,256]{1,0:T(8,128)S(1)}, f32[32,256]{1,0:T(8,128)S(1)}, u32[]{:S(2)}, u32[]{:S(2)}) collective-permute-start(f32[32,256]{1,0:T(8,128)S(1)} %correlation.1.mine), channel_id=1, source_target_pairs={{0,192},{32,224},{64,128},{96,160},{128,64},{160,96},{192,0},{224,... | collective-permute-start | bytes 98312 | tf_op jit(solution)/shard_map/ppermute | solution.py:356
  47.4 3.8 %collective-permute-start.6 = (f32[32,256]{1,0:T(8,128)S(1)}, f32[32,256]{1,0:T(8,128)S(1)}, u32[]{:S(2)}, u32[]{:S(2)}) collective-permute-start(f32[32,256]{1,0:T(8,128)S(1)} %correlation.1.mine), channel_id=1, source_target_pairs={{0,128},{32,160},{64,192},{96,224},{128,0},{160,32},{192,64},{224,... | collective-permute-start | bytes 98312 | tf_op jit(solution)/shard_map/ppermute | solution.py:356
  47.4 3.8 %collective-permute-start.5 = (f32[32,256]{1,0:T(8,128)S(1)}, f32[32,256]{1,0:T(8,128)S(1)}, u32[]{:S(2)}, u32[]{:S(2)}) collective-permute-start(f32[32,256]{1,0:T(8,128)S(1)} %correlation.1.mine), channel_id=1, source_target_pairs={{0,64},{32,96},{64,0},{96,32},{128,192},{160,224},{192,128},{224,1... | collective-permute-start | bytes 98312 | tf_op jit(solution)/shard_map/ppermute | solution.py:356
  51.2 6.1 %collective-permute-start.8 = (f32[32,256]{1,0:T(8,128)S(1)}, f32[32,256]{1,0:T(8,128)S(1)}, u32[]{:S(2)}, u32[]{:S(2)}) collective-permute-start(f32[32,256]{1,0:T(8,128)S(1)} %chip_sum.1.mine), channel_id=1, source_target_pairs={{0,32},{32,0},{64,96},{96,64},{128,160},{160,128},{192,224},{224,1... | collective-permute-start | bytes 98312 | tf_op jit(solution)/shard_map/ppermute | solution.py:356
  68.0 6.5 %collective-permute-start.9 = (f32[16,128]{1,0:T(8,128)S(1)}, f32[16,128]{1,0:T(8,128)S(1)}, u32[]{:S(2)}, u32[]{:S(2)}) collective-permute-start(f32[16,128]{1,0:T(8,128)S(1)} %plane_sum.3.mine), channel_id=1, source_target_pairs={{0,4},{1,5},{2,6},{3,7},{4,0},{5,1},{6,2},{7,3},{8,12},{9,13},{10,... | collective-permute-start | bytes 24584 | tf_op jit(solution)/shard_map/ppermute | solution.py:424
  85.1 5.0 %collective-permute-start.10 = (f32[4,8,128]{2,1,0:T(8,128)S(1)}, f32[4,8,128]{2,1,0:T(8,128)S(1)}, u32[]{:S(2)}, u32[]{:S(2)}) collective-permute-start(f32[4,8,128]{2,1,0:T(8,128)S(1)} %get-tuple-element.34), channel_id=1, source_target_pairs={{0,32},{32,0},{64,96},{96,64},{128,160},{160,128},{192,224},{224,1... | collective-permute-start | bytes 49160 | tf_op jit(solution)/shard_map/ppermute | solution.py:356
  90.1 4.3 %collective-permute-start.11 = (f32[8,128]{1,0:T(8,128)S(1)}, f32[8,128]{1,0:T(8,128)S(1)}, u32[]{:S(2)}, u32[]{:S(2)}) collective-permute-start(f32[8,128]{1,0:T(8,128)S(1)} %get-tuple-element.36), channel_id=1, source_target_pairs={{0,192},{32,224},{64,128},{96,160},{128,64},{160,96},{192,0},{224,... | collective-permute-start | bytes 12296 | tf_op jit(solution)/shard_map/ppermute | solution.py:356
  91.7 3.7 %collective-permute-start.12 = (f32[8,128]{1,0:T(8,128)S(1)}, f32[8,128]{1,0:T(8,128)S(1)}, u32[]{:S(2)}, u32[]{:S(2)}) collective-permute-start(f32[8,128]{1,0:T(8,128)S(1)} %get-tuple-element.37), channel_id=1, source_target_pairs={{0,128},{32,160},{64,192},{96,224},{128,0},{160,32},{192,64},{224,... | collective-permute-start | bytes 12296 | tf_op jit(solution)/shard_map/ppermute | solution.py:356
  92.1 3.2 %collective-permute-start.13 = (f32[8,128]{1,0:T(8,128)S(1)}, f32[8,128]{1,0:T(8,128)S(1)}, u32[]{:S(2)}, u32[]{:S(2)}) collective-permute-start(f32[8,128]{1,0:T(8,128)S(1)} %get-tuple-element.38), channel_id=1, source_target_pairs={{0,64},{32,96},{64,0},{96,32},{128,192},{160,224},{192,128},{224,1... | collective-permute-start | bytes 12296 | tf_op jit(solution)/shard_map/ppermute | solution.py:356

commit v10 on v9

--- a/solution.py
+++ b/solution.py
@@ -74,7 +74,11 @@
 def pick_kernel(focus_hbm, reflection_hbm, out, focus, reflection, sems):
     copies = [
         pltpu.make_async_copy(focus_hbm, focus, sems.at[0]),
-        pltpu.make_async_copy(reflection_hbm, reflection, sems.at[1]),
+    ] + [
+        pltpu.make_async_copy(
+            reflection_hbm.at[pl.ds(part * PLANE, PLANE)], reflection.at[pl.ds(part * PLANE, PLANE)], sems.at[1 + part]
+        )
+        for part in range(SHOTS_HERE // PLANE)
     ]
     for copy in copies:
         copy.start()
@@ -383,7 +387,7 @@
         pick_kernel, "pick", [HB] * 2, [((traces, LAGS), BF16)],
         [
             pltpu.SMEM((FOCI,), jnp.int32), pltpu.VMEM((SHOTS_HERE, RCV_HERE, LAGS), BF16),
-            pltpu.SemaphoreType.DMA((2,)),
+            pltpu.SemaphoreType.DMA((5,)),
         ],
         *in_hbm(focus_index, reflection),
     )

time: 96.3 us -> 96.4 us (level)
  no operation moved by 1% of the time
where the time goes in v10:
time: 96.4 us; the launch traced here: 96.1 us
  blocking collectives  42.3 us (44%)
  starting transfers between devices  33.2 us (34%)
  Pallas kernels  10.4 us (11%)
  waiting for transfers between devices  9.54 us (10%)
    ppermute x12, starting transfers between devices, over_shot(): lax.ppermute(array, 'shot', [(place, place ^ step) for place in range(SHO...  24.2 us
    all_to_all x2, blocking collectives, on_device(): lax.all_to_all(partial, 'rcv', 0, 0, tiled=True, axis_index_groups=over_p...  23.4 us
    all_to_all x2, blocking collectives, on_device(): lax.all_to_all(rounded, 'rcv', 0, 0, tiled=True, axis_index_groups=over_p...  18.9 us
    pallas_call x16, Pallas kernels, call(): pl.pallas_call(kernel, name=name, in_specs=specs, out_specs=[VM] * len(ou...  10.4 us
    ppermute x2, starting transfers between devices, on_device(): lax.ppermute(mine, 'rcv', [(place, place ^ 4) for place in range(RCV_AXIS)])  9 us
    ppermute x12, waiting for transfers between devices, over_shot(): lax.ppermute(array, 'shot', [(place, place ^ step) for place in range(SHO...  6.36 us
    ppermute x2, waiting for transfers between devices, on_device(): lax.ppermute(mine, 'rcv', [(place, place ^ 4) for place in range(RCV_AXIS)])  3.18 us
  transfers between devices with their start and end apart: 14, of which 9 were waited for; matrix products, arithmetic and copies ran while one was open for 0% of the time, Pallas kernels for 5%

profile of v10, /device:TPU:1, one launch (start us, length us, event | category | flops | bytes accessed | tf_op | source)
XLA Modules:
  0.0 96.1 jit_solution(8264345060855401399)
XLA Ops:
  0.6 1.1 %pick.1.mine = bf16[32,256]{1,0:T(8,128)(2,1)S(1)} custom-call(s32[2]{0:T(128)} %focus_hbm.1, bf16[64,16,256]{2,1,0:T(8,128)(2,1)} %reflection_hbm.3), custom_call_target="tpu_custom_call" | custom-call | tf_op jit(solution)/shard_map/pick/pallas_call | solution.py:348
  1.8 5.3 %collective-permute-start.2 = (bf16[32,256]{1,0:T(8,128)(2,1)S(1)}, bf16[32,256]{1,0:T(8,128)(2,1)S(1)}, u32[]{:S(2)}, u32[]{:S(2)}) collective-permute-start(bf16[32,256]{1,0:T(8,128)(2,1)S(1)} %pick.1.mine), channel_id=1, source_target_pairs={{0,192},{32,224},{64,128},{96,160},{128,64},{160,96},{192,0},{224,... | collective-permute-start | bytes 49160 | tf_op jit(solution)/shard_map/ppermute | solution.py:360
  7.0 0.0 collective-permute-start.1
  7.0 0.4 collective-permute-start
  7.4 2.4 %preparation.1 = (f32[4,512,128]{2,1,0:T(8,128)S(1)}, bf16[32,16,256]{2,1,0:T(8,128)(2,1)S(1)}, bf16[256,512]{1,0:T(8,128)(2,1)S(1)}, bf16[256,512]{1,0:T(8,128)...) custom-call(bf16[64,16,256]{2,1,0:T(8,128)(2,1)} %reflection_hbm.3, ...), custom_call_target="tpu_custom_call" | custom-call | tf_op jit(solution)/shard_map/preparation/pallas_call | solution.py:348
  9.9 0.0 collective-permute-done.2.far
  9.9 0.8 collective-permute-done.1.middle
  10.7 0.0 collective-permute-done.near
  10.7 0.1 chip_picks.1.mine
  10.9 1.9 %collective-permute-start.3 = (bf16[32,256]{1,0:T(8,128)(2,1)S(1)}, bf16[32,256]{1,0:T(8,128)(2,1)S(1)}, u32[]{:S(2)}, u32[]{:S(2)}) collective-permute-start(bf16[32,256]{1,0:T(8,128)(2,1)S(1)} %chip_picks.1.mine), channel_id=1, source_target_pairs={{0,32},{32,0},{64,96},{96,64},{128,160},{160,128},{192,224},{224,1... | collective-permute-start | bytes 49160 | tf_op jit(solution)/shard_map/ppermute | solution.py:360
  12.8 1.3 %rest_preparation.1.refl_rest = f32[4,512,128]{2,1,0:T(8,128)S(1)} custom-call(bf16[32,16,256]{2,1,0:T(8,128)(2,1)S(1)} %get-tuple-element.25.reflection, bf16[256,512]{1,0:T(8,128)(2,1)S(1)} %get-tuple-element.26.high.fwd_high, bf16[256,512]{1,0:T(8,128)(2,1)S(1)} %get-tuple-element.27.low.fwd_low), custom_call_target="tpu_custom_call" | custom-call | tf_op jit(solution)/shard_map/rest_preparation/pallas_call | solution.py:348
  14.1 0.0 collective-permute-done.3.other
  14.1 1.0 first_convolution.1
  15.0 13.7 %all_to_all.20.parts = f32[16,16,128]{2,1,0:T(8,128)S(1)} all-to-all(f32[16,16,128]{2,1,0:T(8,128)S(1)} %get-tuple-element.30), channel_id=1, replica_groups={{0,1,2,3,8,9,10,11,16,17,18,19,24,25,26,27},{4,5,6,7,12,13,14,15,20,21,..., dimensions={0} | all-to-all | bytes 262144 | tf_op jit(solution)/shard_map/all_to_all | solution.py:426
  28.7 4.6 %collective-permute-start.4 = (f32[16,128]{1,0:T(8,128)S(1)}, f32[16,128]{1,0:T(8,128)S(1)}, u32[]{:S(2)}, u32[]{:S(2)}) collective-permute-start(f32[16,128]{1,0:T(8,128)S(1)} %plane_sum.2.mine), channel_id=1, source_target_pairs={{0,4},{1,5},{2,6},{3,7},{4,0},{5,1},{6,2},{7,3},{8,12},{9,13},{10,... | collective-permute-start | bytes 24584 | tf_op jit(solution)/shard_map/ppermute | solution.py:428
  33.4 0.8 masks.1
  34.2 1.1 %collective-permute-done.4.other = f32[16,128]{1,0:T(8,128)S(1)} collective-permute-done((f32[16,128]{1,0:T(8,128)S(1)}, f32[16,128]{1,0:T(8,128)S(1)}, u32[]{:S(2)}, u32[]{:S(2)}) %collective-permute-start.4) | collective-permute-done | bytes 8224 | tf_op jit(solution)/shard_map/ppermute | solution.py:428
  35.3 9.3 %all_to_all.21.upgoing = bf16[16,16,128]{2,1,0:T(8,128)(2,1)S(1)} all-to-all(bf16[16,16,128]{2,1,0:T(8,128)(2,1)S(1)} %upgoing.1), channel_id=1, replica_groups={{0,1,2,3,8,9,10,11,16,17,18,19,24,25,26,27},{4,5,6,7,12,13,14,15,20,21,..., dimensions={0} | all-to-all | bytes 131072 | tf_op jit(solution)/shard_map/all_to_all | solution.py:436
  44.6 0.9 correlation.1.mine
  45.5 2.0 %collective-permute-start.7 = (f32[32,256]{1,0:T(8,128)S(1)}, f32[32,256]{1,0:T(8,128)S(1)}, u32[]{:S(2)}, u32[]{:S(2)}) collective-permute-start(f32[32,256]{1,0:T(8,128)S(1)} %correlation.1.mine), channel_id=1, source_target_pairs={{0,192},{32,224},{64,128},{96,160},{128,64},{160,96},{192,0},{224,... | collective-permute-start | bytes 98312 | tf_op jit(solution)/shard_map/ppermute | solution.py:360
  47.5 0.0 collective-permute-start.6
  47.5 1.6 %collective-permute-start.5 = (f32[32,256]{1,0:T(8,128)S(1)}, f32[32,256]{1,0:T(8,128)S(1)}, u32[]{:S(2)}, u32[]{:S(2)}) collective-permute-start(f32[32,256]{1,0:T(8,128)S(1)} %correlation.1.mine), channel_id=1, source_target_pairs={{0,64},{32,96},{64,0},{96,32},{128,192},{160,224},{192,128},{224,1... | collective-permute-start | bytes 98312 | tf_op jit(solution)/shard_map/ppermute | solution.py:360
  49.1 1.0 %collective-permute-done.7.far = f32[32,256]{1,0:T(8,128)S(1)} collective-permute-done((f32[32,256]{1,0:T(8,128)S(1)}, f32[32,256]{1,0:T(8,128)S(1)}, u32[]{:S(2)}, u32[]{:S(2)}) %collective-permute-start.7) | collective-permute-done | bytes 32800 | tf_op jit(solution)/shard_map/ppermute | solution.py:360
  50.1 1.2 %collective-permute-done.6.middle = f32[32,256]{1,0:T(8,128)S(1)} collective-permute-done((f32[32,256]{1,0:T(8,128)S(1)}, f32[32,256]{1,0:T(8,128)S(1)}, u32[]{:S(2)}, u32[]{:S(2)}) %collective-permute-start.6) | collective-permute-done | bytes 32800 | tf_op jit(solution)/shard_map/ppermute | solution.py:360
  51.3 0.0 collective-permute-done.5.near
  51.3 5.2 %collective-permute-start.8 = (f32[32,256]{1,0:T(8,128)S(1)}, f32[32,256]{1,0:T(8,128)S(1)}, u32[]{:S(2)}, u32[]{:S(2)}) collective-permute-start(f32[32,256]{1,0:T(8,128)S(1)} %chip_sum.1.mine), channel_id=1, source_target_pairs={{0,32},{32,0},{64,96},{96,64},{128,160},{160,128},{192,224},{224,1... | collective-permute-start | bytes 98312 | tf_op jit(solution)/shard_map/ppermute | solution.py:360
  56.6 0.9 collective-permute-done.8.other
  57.4 0.9 next_convolution.1
  58.4 9.7 %all_to_all.22.parts = f32[16,16,128]{2,1,0:T(8,128)S(1)} all-to-all(f32[16,16,128]{2,1,0:T(8,128)S(1)} %next_convolution.1), channel_id=1, replica_groups={{0,1,2,3,8,9,10,11,16,17,18,19,24,25,26,27},{4,5,6,7,12,13,14,15,20,21,..., dimensions={0} | all-to-all | bytes 262144 | tf_op jit(solution)/shard_map/all_to_all | solution.py:426
  68.1 4.4 %collective-permute-start.9 = (f32[16,128]{1,0:T(8,128)S(1)}, f32[16,128]{1,0:T(8,128)S(1)}, u32[]{:S(2)}, u32[]{:S(2)}) collective-permute-start(f32[16,128]{1,0:T(8,128)S(1)} %plane_sum.3.mine), channel_id=1, source_target_pairs={{0,4},{1,5},{2,6},{3,7},{4,0},{5,1},{6,2},{7,3},{8,12},{9,13},{10,... | collective-permute-start | bytes 24584 | tf_op jit(solution)/shard_map/ppermute | solution.py:428
  72.5 2.1 %collective-permute-done.9.other = f32[16,128]{1,0:T(8,128)S(1)} collective-permute-done((f32[16,128]{1,0:T(8,128)S(1)}, f32[16,128]{1,0:T(8,128)S(1)}, u32[]{:S(2)}, u32[]{:S(2)}) %collective-permute-start.9) | collective-permute-done | bytes 8224 | tf_op jit(solution)/shard_map/ppermute | solution.py:428
  74.6 9.6 %all_to_all.23.upgoing = bf16[16,16,128]{2,1,0:T(8,128)(2,1)S(1)} all-to-all(bf16[16,16,128]{2,1,0:T(8,128)(2,1)S(1)} %get-tuple-element.32), channel_id=1, replica_groups={{0,1,2,3,8,9,10,11,16,17,18,19,24,25,26,27},{4,5,6,7,12,13,14,15,20,21,..., dimensions={0} | all-to-all | bytes 131072 | tf_op jit(solution)/shard_map/all_to_all | solution.py:436
  84.2 1.0 %last_correlation.1 = (f32[4,8,128]{2,1,0:T(8,128)S(1)}, f32[4,8,128]{2,1,0:T(8,128)S(1)}) custom-call(bf16[16,16,128]{2,1,0:T(8,128)(2,1)S(1)} %all_to_all.23.upgoing, f32[4,512,128]{2,1,0:T(8,128)S(1)} %get-tuple-element.24.refl, f32[4,512,128]{2,1,0:T(8,128)S(1)} %rest_preparation.1.refl_rest, bf16[256,512]{1,0:T(8,128)(2,1)S(1)} %get-tuple-element.26.high.fwd_high, ...), custom_call_target="tpu_custom_call" | custom-call | tf_op jit(solution)/shard_map/last_correlation/pallas_call | solution.py:348
  85.2 4.2 %collective-permute-start.10 = (f32[4,8,128]{2,1,0:T(8,128)S(1)}, f32[4,8,128]{2,1,0:T(8,128)S(1)}, u32[]{:S(2)}, u32[]{:S(2)}) collective-permute-start(f32[4,8,128]{2,1,0:T(8,128)S(1)} %get-tuple-element.34), channel_id=1, source_target_pairs={{0,32},{32,0},{64,96},{96,64},{128,160},{160,128},{192,224},{224,1... | collective-permute-start | bytes 49160 | tf_op jit(solution)/shard_map/ppermute | solution.py:360
  89.4 0.8 collective-permute-done.10.other
  90.2 1.5 %collective-permute-start.11 = (f32[8,128]{1,0:T(8,128)S(1)}, f32[8,128]{1,0:T(8,128)S(1)}, u32[]{:S(2)}, u32[]{:S(2)}) collective-permute-start(f32[8,128]{1,0:T(8,128)S(1)} %get-tuple-element.36), channel_id=1, source_target_pairs={{0,192},{32,224},{64,128},{96,160},{128,64},{160,96},{192,0},{224,... | collective-permute-start | bytes 12296 | tf_op jit(solution)/shard_map/ppermute | solution.py:360
  91.7 0.5 collective-permute-start.12
  92.2 1.5 %collective-permute-start.13 = (f32[8,128]{1,0:T(8,128)S(1)}, f32[8,128]{1,0:T(8,128)S(1)}, u32[]{:S(2)}, u32[]{:S(2)}) collective-permute-start(f32[8,128]{1,0:T(8,128)S(1)} %get-tuple-element.38), channel_id=1, source_target_pairs={{0,64},{32,96},{64,0},{96,32},{128,192},{160,224},{192,128},{224,1... | collective-permute-start | bytes 12296 | tf_op jit(solution)/shard_map/ppermute | solution.py:360
  93.8 0.7 collective-permute-done.11.far
  94.5 0.9 collective-permute-done.12.middle
  95.4 0.0 collective-permute-done.13.near
  95.4 0.7 downgoing.1
  (6 shorter events, 0.1 us)
Async XLA Ops:
  1.8 8.1 %collective-permute-start.2 = (bf16[32,256]{1,0:T(8,128)(2,1)S(1)}, bf16[32,256]{1,0:T(8,128)(2,1)S(1)}, u32[]{:S(2)}, u32[]{:S(2)}) collective-permute-start(bf16[32,256]{1,0:T(8,128)(2,1)S(1)} %pick.1.mine), channel_id=1, source_target_pairs={{0,192},{32,224},{64,128},{96,160},{128,64},{160,96},{192,0},{224,... | collective-permute-start | bytes 49160 | tf_op jit(solution)/shard_map/ppermute | solution.py:360
  7.0 3.7 %collective-permute-start.1 = (bf16[32,256]{1,0:T(8,128)(2,1)S(1)}, bf16[32,256]{1,0:T(8,128)(2,1)S(1)}, u32[]{:S(2)}, u32[]{:S(2)}) collective-permute-start(bf16[32,256]{1,0:T(8,128)(2,1)S(1)} %pick.1.mine), channel_id=1, source_target_pairs={{0,128},{32,160},{64,192},{96,224},{128,0},{160,32},{192,64},{224,... | collective-permute-start | bytes 49160 | tf_op jit(solution)/shard_map/ppermute | solution.py:360
  7.0 3.7 %collective-permute-start = (bf16[32,256]{1,0:T(8,128)(2,1)S(1)}, bf16[32,256]{1,0:T(8,128)(2,1)S(1)}, u32[]{:S(2)}, u32[]{:S(2)}) collective-permute-start(bf16[32,256]{1,0:T(8,128)(2,1)S(1)} %pick.1.mine), channel_id=1, source_target_pairs={{0,64},{32,96},{64,0},{96,32},{128,192},{160,224},{192,128},{224,1... | collective-permute-start | bytes 49160 | tf_op jit(solution)/shard_map/ppermute | solution.py:360
  10.9 3.2 %collective-permute-start.3 = (bf16[32,256]{1,0:T(8,128)(2,1)S(1)}, bf16[32,256]{1,0:T(8,128)(2,1)S(1)}, u32[]{:S(2)}, u32[]{:S(2)}) collective-permute-start(bf16[32,256]{1,0:T(8,128)(2,1)S(1)} %chip_picks.1.mine), channel_id=1, source_target_pairs={{0,32},{32,0},{64,96},{96,64},{128,160},{160,128},{192,224},{224,1... | collective-permute-start | bytes 49160 | tf_op jit(solution)/shard_map/ppermute | solution.py:360
  28.7 6.5 %collective-permute-start.4 = (f32[16,128]{1,0:T(8,128)S(1)}, f32[16,128]{1,0:T(8,128)S(1)}, u32[]{:S(2)}, u32[]{:S(2)}) collective-permute-start(f32[16,128]{1,0:T(8,128)S(1)} %plane_sum.2.mine), channel_id=1, source_target_pairs={{0,4},{1,5},{2,6},{3,7},{4,0},{5,1},{6,2},{7,3},{8,12},{9,13},{10,... | collective-permute-start | bytes 24584 | tf_op jit(solution)/shard_map/ppermute | solution.py:428
  45.5 4.7 %collective-permute-start.7 = (f32[32,256]{1,0:T(8,128)S(1)}, f32[32,256]{1,0:T(8,128)S(1)}, u32[]{:S(2)}, u32[]{:S(2)}) collective-permute-start(f32[32,256]{1,0:T(8,128)S(1)} %correlation.1.mine), channel_id=1, source_target_pairs={{0,192},{32,224},{64,128},{96,160},{128,64},{160,96},{192,0},{224,... | collective-permute-start | bytes 98312 | tf_op jit(solution)/shard_map/ppermute | solution.py:360
  47.5 3.8 %collective-permute-start.6 = (f32[32,256]{1,0:T(8,128)S(1)}, f32[32,256]{1,0:T(8,128)S(1)}, u32[]{:S(2)}, u32[]{:S(2)}) collective-permute-start(f32[32,256]{1,0:T(8,128)S(1)} %correlation.1.mine), channel_id=1, source_target_pairs={{0,128},{32,160},{64,192},{96,224},{128,0},{160,32},{192,64},{224,... | collective-permute-start | bytes 98312 | tf_op jit(solution)/shard_map/ppermute | solution.py:360
  47.5 3.8 %collective-permute-start.5 = (f32[32,256]{1,0:T(8,128)S(1)}, f32[32,256]{1,0:T(8,128)S(1)}, u32[]{:S(2)}, u32[]{:S(2)}) collective-permute-start(f32[32,256]{1,0:T(8,128)S(1)} %correlation.1.mine), channel_id=1, source_target_pairs={{0,64},{32,96},{64,0},{96,32},{128,192},{160,224},{192,128},{224,1... | collective-permute-start | bytes 98312 | tf_op jit(solution)/shard_map/ppermute | solution.py:360
  51.3 6.1 %collective-permute-start.8 = (f32[32,256]{1,0:T(8,128)S(1)}, f32[32,256]{1,0:T(8,128)S(1)}, u32[]{:S(2)}, u32[]{:S(2)}) collective-permute-start(f32[32,256]{1,0:T(8,128)S(1)} %chip_sum.1.mine), channel_id=1, source_target_pairs={{0,32},{32,0},{64,96},{96,64},{128,160},{160,128},{192,224},{224,1... | collective-permute-start | bytes 98312 | tf_op jit(solution)/shard_map/ppermute | solution.py:360
  68.1 6.5 %collective-permute-start.9 = (f32[16,128]{1,0:T(8,128)S(1)}, f32[16,128]{1,0:T(8,128)S(1)}, u32[]{:S(2)}, u32[]{:S(2)}) collective-permute-start(f32[16,128]{1,0:T(8,128)S(1)} %plane_sum.3.mine), channel_id=1, source_target_pairs={{0,4},{1,5},{2,6},{3,7},{4,0},{5,1},{6,2},{7,3},{8,12},{9,13},{10,... | collective-permute-start | bytes 24584 | tf_op jit(solution)/shard_map/ppermute | solution.py:428
  85.2 5.0 %collective-permute-start.10 = (f32[4,8,128]{2,1,0:T(8,128)S(1)}, f32[4,8,128]{2,1,0:T(8,128)S(1)}, u32[]{:S(2)}, u32[]{:S(2)}) collective-permute-start(f32[4,8,128]{2,1,0:T(8,128)S(1)} %get-tuple-element.34), channel_id=1, source_target_pairs={{0,32},{32,0},{64,96},{96,64},{128,160},{160,128},{192,224},{224,1... | collective-permute-start | bytes 49160 | tf_op jit(solution)/shard_map/ppermute | solution.py:360
  90.2 4.3 %collective-permute-start.11 = (f32[8,128]{1,0:T(8,128)S(1)}, f32[8,128]{1,0:T(8,128)S(1)}, u32[]{:S(2)}, u32[]{:S(2)}) collective-permute-start(f32[8,128]{1,0:T(8,128)S(1)} %get-tuple-element.36), channel_id=1, source_target_pairs={{0,192},{32,224},{64,128},{96,160},{128,64},{160,96},{192,0},{224,... | collective-permute-start | bytes 12296 | tf_op jit(solution)/shard_map/ppermute | solution.py:360
  91.7 3.7 %collective-permute-start.12 = (f32[8,128]{1,0:T(8,128)S(1)}, f32[8,128]{1,0:T(8,128)S(1)}, u32[]{:S(2)}, u32[]{:S(2)}) collective-permute-start(f32[8,128]{1,0:T(8,128)S(1)} %get-tuple-element.37), channel_id=1, source_target_pairs={{0,128},{32,160},{64,192},{96,224},{128,0},{160,32},{192,64},{224,... | collective-permute-start | bytes 12296 | tf_op jit(solution)/shard_map/ppermute | solution.py:360
  92.2 3.2 %collective-permute-start.13 = (f32[8,128]{1,0:T(8,128)S(1)}, f32[8,128]{1,0:T(8,128)S(1)}, u32[]{:S(2)}, u32[]{:S(2)}) collective-permute-start(f32[8,128]{1,0:T(8,128)S(1)} %get-tuple-element.38), channel_id=1, source_target_pairs={{0,64},{32,96},{64,0},{96,32},{128,192},{160,224},{192,128},{224,1... | collective-permute-start | bytes 12296 | tf_op jit(solution)/shard_map/ppermute | solution.py:360
